TPU v7x, 32 devices: a whole 2x2x4 slice. The times are simulated.
32 devices in a mesh: groups: 2 (over x), dev: 16 (over z, y, core).
Axes of the slice: x: 2, y: 2, z: 4, core: 2. Of those that a mesh axis runs over, the one named last changes fastest.
Arguments:
- x_in: bfloat16 [2, 64, 3072], P(None, ('groups', 'dev')), parts along dimension 1, may hold values from -6 to 6
- queries: bfloat16 [2, 64, 3072], P(None, ('groups', 'dev')), parts along dimension 1, may hold values from -75 to 75
- cache_keys: bfloat16 [2, 64, 128, 512], P(None, ('groups', 'dev')), parts along dimension 1, may hold values from -6 to 6
- cache_values: bfloat16 [2, 64, 128, 512], P(None, ('groups', 'dev')), parts along dimension 1, may hold values from -6 to 6
- new_keys: bfloat16 [2, 64, 512], P(None, ('groups', 'dev')), parts along dimension 1, may hold values from -6 to 6
- new_values: bfloat16 [2, 64, 512], P(None, ('groups', 'dev')), parts along dimension 1, may hold values from -6 to 6
- lengths: int32 [2, 64], P(None, ('groups', 'dev')), parts along dimension 1, may hold values from 1 to 128
- w_out: bfloat16 [3072, 3072], P('dev'), may hold values from -0.109375 to 0.109375
- norm_gain: bfloat16 [3072], replicated, may hold values from 0.25 to 1.75
- w_router: bfloat16 [3072, 4], replicated, may hold values from -0.3125 to 0.3125
- experts_idx: int32 [2, 64, 2], P(None, ('groups', 'dev')), parts along dimension 1, may hold values from 0 to 3, all different within a row; in each aligned block of 2 rows (0 to 1, 2 to 3, ..., all dimensions but the last counted through in order) at most 2 rows name the same one
- w_gate: bfloat16 [3072, 32768], P(None, 'dev'), may hold values from -0.109375 to 0.109375
- w_up: bfloat16 [3072, 32768], P(None, 'dev'), may hold values from -0.109375 to 0.109375
- w_down: bfloat16 [32768, 3072], P('dev'), may hold values from -0.0625 to 0.0625
Outputs:
- mixed: bfloat16 [2, 64, 3072], P(None, ('groups', 'dev')), parts along dimension 1
There are 2 independent parts, one for each index of `groups`. A program takes and returns all parts, laid end to end along the dimension named above; an argument that names none is the same for every part. Nothing has to cross between parts.
All inputs are finite; a program needn't handle non-finite values.
Results may differ from a plain program's by a relative error of at most 0.006.
Values may be sent and summed in bfloat16 or wider, within the bound.
No kernel may reach another device: no remote copies, remote signals or barrier semaphores. Data moves between devices by JAX's collectives and lax.ppermute only.
A program may use at most 128 MiB of HBM per device.

v0:
```python
import math

import jax
import jax.numpy as jnp
from jax import lax
from jax.sharding import PartitionSpec as P

QH = 24
KVH = 4
HD = 128


def attend_rows(query, keys_cache, values_cache, key_new, value_new, length):
    row_count = keys_cache.shape[0]
    cache_len = keys_cache.shape[1]
    q_heads = query.reshape(row_count, KVH, QH // KVH, HD)
    k_heads = keys_cache.reshape(row_count, cache_len, KVH, HD)
    v_heads = values_cache.reshape(row_count, cache_len, KVH, HD)
    score_scale = 1.0 / math.sqrt(HD)
    scores = (
        jnp.einsum("rkgd,rlkd->rkgl", q_heads, k_heads, preferred_element_type=jnp.float32)
        * score_scale
    )
    own_score = (
        jnp.einsum(
            "rkgd,rkd->rkg",
            q_heads,
            key_new.reshape(row_count, KVH, HD),
            preferred_element_type=jnp.float32,
        )
        * score_scale
    )
    live_mask = (jnp.arange(cache_len)[None, :] < length[:, None])[:, None, None, :]
    peak = jnp.maximum(jnp.max(jnp.where(live_mask, scores, -jnp.inf), axis=-1), own_score)
    weights_cache = jnp.where(live_mask, jnp.exp(scores - peak[..., None]), 0.0)
    weight_own = jnp.exp(own_score - peak)
    total_mass = jnp.sum(weights_cache, axis=-1) + weight_own
    probs = (weights_cache / total_mass[..., None]).astype(jnp.bfloat16)
    prob_own = (weight_own / total_mass).astype(jnp.bfloat16)
    mixed_cache = jnp.einsum("rkgl,rlkd->rkgd", probs, v_heads, preferred_element_type=jnp.float32)
    mixed_own = prob_own.astype(jnp.float32)[..., None] * value_new.reshape(
        row_count, KVH, 1, HD
    ).astype(jnp.float32)
    return (mixed_cache + mixed_own).reshape(row_count, QH * HD).astype(jnp.bfloat16)


def rms_normed(resid, norm_gain):
    mean_square = jnp.mean(resid * resid, axis=-1, keepdims=True)
    return (resid * lax.rsqrt(mean_square + 1e-05) * norm_gain.astype(jnp.float32)).astype(
        jnp.bfloat16
    )


def combine_weights(normed, route_ids, w_router):
    logits = jnp.dot(normed, w_router, preferred_element_type=jnp.float32)
    expert_count = w_router.shape[1]
    member_of = (route_ids[:, :, None] == jnp.arange(expert_count)[None, None, :]).astype(
        jnp.float32
    )
    chosen = jnp.sum(member_of * logits[:, None, :], axis=-1)
    return (jax.nn.softmax(chosen, axis=-1), member_of)


def expert_partial(rows_in, w_gate, w_up, w_down):
    gate = jnp.dot(rows_in, w_gate, preferred_element_type=jnp.float32)
    upper = jnp.dot(rows_in, w_up, preferred_element_type=jnp.float32)
    hidden = (jax.nn.silu(gate) * upper).astype(jnp.bfloat16)
    return jnp.dot(hidden, w_down, preferred_element_type=jnp.float32)


def local(
    x_in,
    queries,
    cache_keys,
    cache_values,
    new_keys,
    new_values,
    lengths,
    w_out,
    norm_gain,
    w_router,
    experts_idx,
    w_gate,
    w_up,
    w_down,
):
    devices = lax.axis_size("dev")
    expert_count = w_router.shape[1]
    per_expert = devices // expert_count
    rows_dev = x_in.shape[1]
    feature_dim = x_in.shape[2]
    results = []
    for micro_batch in range(x_in.shape[0]):
        attention = attend_rows(
            queries[micro_batch],
            cache_keys[micro_batch],
            cache_values[micro_batch],
            new_keys[micro_batch],
            new_values[micro_batch],
            lengths[micro_batch],
        )
        head_block = lax.all_to_all(attention, "dev", split_axis=1, concat_axis=0, tiled=True)
        attn_own = lax.psum_scatter(
            jnp.dot(head_block, w_out, preferred_element_type=jnp.float32),
            "dev",
            scatter_dimension=0,
            tiled=True,
        )
        resid = x_in[micro_batch].astype(jnp.float32) + attn_own
        normed = rms_normed(resid, norm_gain)
        route_ids = experts_idx[micro_batch]
        combine, member_of = combine_weights(normed, route_ids, w_router)
        in_expert = jnp.sum(member_of, axis=1)
        lower_rows = jnp.tril(jnp.ones((rows_dev, rows_dev), jnp.float32), -1)
        slot_rank = jnp.dot(lower_rows, in_expert, precision=lax.Precision.HIGHEST)
        slot_hit = (
            slot_rank[:, :, None] == jnp.arange(rows_dev, dtype=jnp.float32)[None, None, :]
        ).astype(jnp.float32) * in_expert[:, :, None]
        slot_pick = jnp.transpose(slot_hit, (1, 2, 0))
        send_expert = jnp.einsum(
            "ecs,sd->ecd",
            slot_pick.astype(jnp.bfloat16),
            normed,
            preferred_element_type=jnp.float32,
        ).astype(jnp.bfloat16)
        send_rows = jnp.repeat(send_expert, per_expert, axis=0)
        received = lax.all_to_all(send_rows, "dev", split_axis=0, concat_axis=0, tiled=True)
        flat_rows = received.reshape(-1, feature_dim)
        partial_value = expert_partial(flat_rows, w_gate, w_up, w_down).reshape(
            received.shape[0], received.shape[1], feature_dim
        )
        returned_rows = lax.all_to_all(
            partial_value, "dev", split_axis=0, concat_axis=0, tiled=True
        )
        expert_out = jnp.sum(
            returned_rows.reshape(expert_count, per_expert, rows_dev, feature_dim), axis=1
        )
        row_weight = jnp.sum(member_of * combine[:, :, None], axis=1)
        slot_weight = slot_pick * jnp.transpose(row_weight)[:, None, :]
        moe_own = jnp.einsum(
            "ecs,ecd->sd", slot_weight, expert_out, precision=lax.Precision.HIGHEST
        )
        results.append((resid + moe_own).astype(jnp.bfloat16))
    return jnp.stack(results)


def solution(mesh):
    return jax.shard_map(
        local,
        mesh=mesh,
        in_specs=(
            P(None, ("groups", "dev"), None),
            P(None, ("groups", "dev"), None),
            P(None, ("groups", "dev"), None, None),
            P(None, ("groups", "dev"), None, None),
            P(None, ("groups", "dev"), None),
            P(None, ("groups", "dev"), None),
            P(None, ("groups", "dev")),
            P("dev", None),
            P(),
            P(),
            P(None, ("groups", "dev"), None),
            P(None, "dev"),
            P(None, "dev"),
            P("dev", None),
        ),
        out_specs=P(None, ("groups", "dev"), None),
        check_vma=False,
    )
```

profile of v0, /device:TPU:0, one launch (start us, length us, event | category | flops | bytes accessed | tf_op | source)
XLA Modules:
  0.0 225.6 jit_solution(7641831598511669133)
XLA Ops:
  6.5 0.8 slice_bitcast_fusion.2
  7.3 0.7 fusion.88
  8.1 1.1 fusion.86
  9.3 0.7 fusion.89
  10.3 0.3 select_reduce_fusion
  10.7 1.1 fusion.87
  12.0 0.7 slice_convert_fusion
  12.7 0.3 fusion.9
  13.1 0.6 copy.54
  13.7 7.4 %all-to-all-start.3 = ((bf16[2,16,192]{2,0,1:T(2,128)(2,1)}), bf16[2,16,192]{2,0,1:T(2,128)(2,1)S(1)}, u32[]{:S(2)}, u32[]{:S(2)}) async-start(bf16[2,16,192]{2,0,1:T(2,128)(2,1)} %copy.54), calls=%async_computation.3 | async-start | bytes 32768 | tf_op jit(solution)/shard_map/all_to_all | solution.py:102
  21.4 0.3 select_reduce_fusion.1
  22.1 0.3 fusion.8
  22.5 0.6 copy.47
  23.1 4.5 %all-to-all-done.3 = bf16[2,16,192]{2,0,1:T(2,128)(2,1)S(1)} async-done(((bf16[2,16,192]{2,0,1:T(2,128)(2,1)}), bf16[2,16,192]{2,0,1:T(2,128)(2,1)S(1)}, u32[]{:S(2)}, u32[]{:S(2)}) %all-to-all-start.3) | async-done | bytes 12320 | tf_op jit(solution)/shard_map/all_to_all | solution.py:102
  27.6 3.5 %all-to-all-start = ((bf16[2,16,192]{2,0,1:T(2,128)(2,1)}), bf16[2,16,192]{2,0,1:T(2,128)(2,1)S(1)}, u32[]{:S(2)}, u32[]{:S(2)}) async-start(bf16[2,16,192]{2,0,1:T(2,128)(2,1)} %copy.47), calls=%async_computation | async-start | bytes 32768 | tf_op jit(solution)/shard_map/all_to_all | solution.py:102
  31.2 6.4 %all-to-all-done = bf16[2,16,192]{2,0,1:T(2,128)(2,1)S(1)} async-done(((bf16[2,16,192]{2,0,1:T(2,128)(2,1)}), bf16[2,16,192]{2,0,1:T(2,128)(2,1)S(1)}, u32[]{:S(2)}, u32[]{:S(2)}) %all-to-all-start) | async-done | bytes 12320 | tf_op jit(solution)/shard_map/all_to_all | solution.py:102
  37.6 1.1 fusion.95
  38.7 1.1 fusion.91
  39.8 0.7 convert_element_type.118
  40.5 1.2 dynamic-slice
  42.4 0.7 slice_bitcast_fusion.1
  43.1 86.3 %all-reduce.5.cloned.1.call-done = (f32[32,3072]{1,0:T(8,128)}, f32[32,3072]{1,0:T(8,128)}) async-done(((f32[32,3072]{1,0:T(8,128)}, f32[32,3072]{1,0:T(8,128)}), (f32[32,3072]{1,0:T(8,128)}, f32[32,3072]{1,0:T(8,128)})) %all-reduce.5.cloned.1.call-update) | async-done | bytes 786448
  129.5 1.2 multiply_reduce_fusion.1
  130.6 1.1 multiply_convert_fusion.1
  131.7 0.9 fusion.92
  132.9 0.2 fusion.65
  133.2 0.2 fusion.61
  133.4 0.2 convolution_convert_fusion.1
  133.7 0.8 broadcast_in_dim.35
  134.5 3.7 %all-to-all-start.1 = ((bf16[16,2,3072]{2,1,0:T(2,128)(2,1)}), bf16[16,2,3072]{2,1,0:T(2,128)(2,1)S(1)}, u32[]{:S(2)}, u32[]{:S(2)}) async-start(bf16[16,2,3072]{2,1,0:T(2,128)(2,1)} %bitcast.11), calls=%async_computation.1 | async-start | bytes 393216 | tf_op jit(solution)/shard_map/all_to_all | solution.py:127
  138.2 0.9 fusion.96
  139.3 0.2 fusion.67
  139.9 0.2 convolution_convert_fusion
  140.2 7.0 %all-to-all-done.1 = bf16[16,2,3072]{2,1,0:T(2,128)(2,1)S(1)} async-done(((bf16[16,2,3072]{2,1,0:T(2,128)(2,1)}), bf16[16,2,3072]{2,1,0:T(2,128)(2,1)S(1)}, u32[]{:S(2)}, u32[]{:S(2)}) %all-to-all-start.1) | async-done | bytes 196640 | tf_op jit(solution)/shard_map/all_to_all | solution.py:127
  147.2 0.8 broadcast_in_dim.37
  148.0 3.5 %all-to-all-start.4 = ((bf16[16,2,3072]{2,1,0:T(2,128)(2,1)}), bf16[16,2,3072]{2,1,0:T(2,128)(2,1)S(1)}, u32[]{:S(2)}, u32[]{:S(2)}) async-start(bf16[16,2,3072]{2,1,0:T(2,128)(2,1)} %bitcast.26), calls=%async_computation.4 | async-start | bytes 393216 | tf_op jit(solution)/shard_map/all_to_all | solution.py:127
  151.6 6.8 %fusion.93 = f32[32,2048]{1,0:T(8,128)S(1)} fusion(bf16[32,3072]{1,0:T(8,128)(2,1)S(1)} %reshape.202, bf16[3072,2048]{1,0:T(8,128)(2,1)} %param.25), kind=kOutput, calls=%fused_computation.146 | convolution fusion | flops 402653184 | bytes 13041664 | tf_op jit(solution)/shard_map/dot_general | solution.py:65
  158.4 12.6 %fusion.11 = f32[32,3072]{1,0:T(8,128)S(1)} fusion(bf16[2048,3072]{1,0:T(8,128)(2,1)} %param.27, bf16[32,3072]{1,0:T(8,128)(2,1)S(1)} %reshape.202, bf16[3072,2048]{1,0:T(8,128)(2,1)} %param.26, f32[32,2048]{1,0:T(8,128)S(1)} %fusion.93), kind=kOutput, calls=%fused_computation.21 | convolution fusion | flops 805699584 | bytes 26017792 | tf_op jit(solution)/shard_map/dot_general | solution.py:68
  171.0 1.0 reshape.203
  172.0 6.0 %all-to-all-start.2 = ((f32[16,2,3072]{2,1,0:T(2,128)}), f32[16,2,3072]{2,1,0:T(2,128)S(1)}, u32[]{:S(2)}, u32[]{:S(2)}) async-start(f32[16,2,3072]{2,1,0:T(2,128)} %reshape.203), calls=%async_computation.2 | async-start | bytes 786432 | tf_op jit(solution)/shard_map/all_to_all | solution.py:132
  178.1 6.8 %fusion.97 = f32[32,2048]{1,0:T(8,128)S(1)} fusion(bf16[32,3072]{1,0:T(8,128)(2,1)S(1)} %reshape.206, bf16[3072,2048]{1,0:T(8,128)(2,1)} %param.25), kind=kOutput, calls=%fused_computation.150 | convolution fusion | flops 402653184 | bytes 13041664 | tf_op jit(solution)/shard_map/dot_general | solution.py:65
  184.9 12.6 %fusion.10 = f32[32,3072]{1,0:T(8,128)S(1)} fusion(bf16[2048,3072]{1,0:T(8,128)(2,1)} %param.27, bf16[32,3072]{1,0:T(8,128)(2,1)S(1)} %reshape.206, bf16[3072,2048]{1,0:T(8,128)(2,1)} %param.26, f32[32,2048]{1,0:T(8,128)S(1)} %fusion.97), kind=kOutput, calls=%fused_computation.20 | convolution fusion | flops 805699584 | bytes 26017792 | tf_op jit(solution)/shard_map/dot_general | solution.py:68
  197.5 1.0 reshape.207
  198.5 6.0 %all-to-all-start.5 = ((f32[16,2,3072]{2,1,0:T(2,128)}), f32[16,2,3072]{2,1,0:T(2,128)S(1)}, u32[]{:S(2)}, u32[]{:S(2)}) async-start(f32[16,2,3072]{2,1,0:T(2,128)} %reshape.207), calls=%async_computation.5 | async-start | bytes 786432 | tf_op jit(solution)/shard_map/all_to_all | solution.py:132
  204.7 1.2 fusion.2
  205.9 10.8 %all-to-all-done.5 = f32[16,2,3072]{2,1,0:T(2,128)S(1)} async-done(((f32[16,2,3072]{2,1,0:T(2,128)}), f32[16,2,3072]{2,1,0:T(2,128)S(1)}, u32[]{:S(2)}, u32[]{:S(2)}) %all-to-all-start.5) | async-done | bytes 393248 | tf_op jit(solution)/shard_map/all_to_all | solution.py:132
  216.8 1.2 fusion.5
  218.1 0.6 pad_maximum_fusion
  (49 shorter events, 3.4 us)
Async XLA Ops:
  6.5 31.1 %copy-start = (bf16[192,3072]{1,0:T(8,128)(2,1)S(1)}, bf16[192,3072]{1,0:T(8,128)(2,1)}, u32[]{:S(2)}) copy-start(bf16[192,3072]{1,0:T(8,128)(2,1)} %param.21) | copy-start | bytes 3538948
  13.7 13.9 %all-to-all-start.3 = ((bf16[2,16,192]{2,0,1:T(2,128)(2,1)}), bf16[2,16,192]{2,0,1:T(2,128)(2,1)S(1)}, u32[]{:S(2)}, u32[]{:S(2)}) async-start(bf16[2,16,192]{2,0,1:T(2,128)(2,1)} %copy.54), calls=%async_computation.3 | async-start | bytes 32768 | tf_op jit(solution)/shard_map/all_to_all | solution.py:102
  27.6 10.0 %all-to-all-start = ((bf16[2,16,192]{2,0,1:T(2,128)(2,1)}), bf16[2,16,192]{2,0,1:T(2,128)(2,1)S(1)}, u32[]{:S(2)}, u32[]{:S(2)}) async-start(bf16[2,16,192]{2,0,1:T(2,128)(2,1)} %copy.47), calls=%async_computation | async-start | bytes 32768 | tf_op jit(solution)/shard_map/all_to_all | solution.py:102
  31.1 98.3 %all-reduce.5.cloned.1.call-start = ((), (), s32[]{:S(2)}) async-start(), calls=%async_computation.6 | async-start | bytes 1572864
  134.5 12.7 %all-to-all-start.1 = ((bf16[16,2,3072]{2,1,0:T(2,128)(2,1)}), bf16[16,2,3072]{2,1,0:T(2,128)(2,1)S(1)}, u32[]{:S(2)}, u32[]{:S(2)}) async-start(bf16[16,2,3072]{2,1,0:T(2,128)(2,1)} %bitcast.11), calls=%async_computation.1 | async-start | bytes 393216 | tf_op jit(solution)/shard_map/all_to_all | solution.py:127
  148.0 24.1 %all-to-all-start.4 = ((bf16[16,2,3072]{2,1,0:T(2,128)(2,1)}), bf16[16,2,3072]{2,1,0:T(2,128)(2,1)S(1)}, u32[]{:S(2)}, u32[]{:S(2)}) async-start(bf16[16,2,3072]{2,1,0:T(2,128)(2,1)} %bitcast.26), calls=%async_computation.4 | async-start | bytes 393216 | tf_op jit(solution)/shard_map/all_to_all | solution.py:127
  172.0 26.5 %all-to-all-start.2 = ((f32[16,2,3072]{2,1,0:T(2,128)}), f32[16,2,3072]{2,1,0:T(2,128)S(1)}, u32[]{:S(2)}, u32[]{:S(2)}) async-start(f32[16,2,3072]{2,1,0:T(2,128)} %reshape.203), calls=%async_computation.2 | async-start | bytes 786432 | tf_op jit(solution)/shard_map/all_to_all | solution.py:132
  184.9 19.7 %copy-start.1 = (bf16[2,2,3072]{2,1,0:T(2,128)(2,1)S(1)}, bf16[2,2,3072]{2,1,0:T(2,128)(2,1)}, u32[]{:S(2)}) copy-start(bf16[2,2,3072]{2,1,0:T(2,128)(2,1)} %param.14) | copy-start | bytes 73732
  198.5 18.2 %all-to-all-start.5 = ((f32[16,2,3072]{2,1,0:T(2,128)}), f32[16,2,3072]{2,1,0:T(2,128)S(1)}, u32[]{:S(2)}, u32[]{:S(2)}) async-start(f32[16,2,3072]{2,1,0:T(2,128)} %reshape.207), calls=%async_computation.5 | async-start | bytes 786432 | tf_op jit(solution)/shard_map/all_to_all | solution.py:132
Sparse Core Ops, SparseCore 0:
  39.9 89.4 all-reduce.4
where the time goes:
time: 227 us; the launch traced here: 226 us
  waiting for transfers between devices  115 us (51%)
  matrix products  47.4 us (21%)
  starting transfers between devices  30.1 us (13%)
  between operations  14.3 us (6%)
  local copies, waits for them, and re-layouts  12.4 us (5%)
  other arithmetic  6.28 us (3%)
    unnamed x2, waiting for transfers between devices  86.4 us
    dot_general x2, matrix products, expert_partial(): return jnp.dot(hidden, w_down, preferred_element_type=jnp.float32)  25.2 us
    dot_general x2, matrix products, expert_partial(): gate = jnp.dot(rows_in, w_gate, preferred_element_type=jnp.float32)  13.7 us
    all_to_all x2, starting transfers between devices, local(): lax.all_to_all(partial_value, 'dev', split_axis=0, concat_axis=0, tiled=T...  12 us
    all_to_all x2, starting transfers between devices, local(): lax.all_to_all(attention, 'dev', split_axis=1, concat_axis=0, tiled=True)  10.9 us
    all_to_all x2, waiting for transfers between devices, local(): lax.all_to_all(attention, 'dev', split_axis=1, concat_axis=0, tiled=True)  10.9 us
    all_to_all x2, waiting for transfers between devices, local(): lax.all_to_all(partial_value, 'dev', split_axis=0, concat_axis=0, tiled=T...  10.8 us
    all_to_all x2, starting transfers between devices, local(): lax.all_to_all(send_rows, 'dev', split_axis=0, concat_axis=0, tiled=True)  7.2 us
  transfers between devices with their start and end apart: 7, of which 5 were waited for; matrix products, arithmetic and copies ran while one was open for 22% of the time, Pallas kernels for 0%

commit v1 on v0

v1 whole, which is shorter than its diff:
```python
import math

import jax
import jax.numpy as jnp
from jax import lax
from jax.sharding import PartitionSpec as P

QH = 24
KVH = 4
HD = 128


def attend_rows(query, keys_cache, values_cache, key_new, value_new, length):
    row_count = keys_cache.shape[0]
    cache_len = keys_cache.shape[1]
    q_heads = query.reshape(row_count, KVH, QH // KVH, HD)
    k_heads = keys_cache.reshape(row_count, cache_len, KVH, HD)
    v_heads = values_cache.reshape(row_count, cache_len, KVH, HD)
    score_scale = 1.0 / math.sqrt(HD)
    scores = (
        jnp.einsum("rkgd,rlkd->rkgl", q_heads, k_heads, preferred_element_type=jnp.float32)
        * score_scale
    )
    own_score = (
        jnp.einsum(
            "rkgd,rkd->rkg",
            q_heads,
            key_new.reshape(row_count, KVH, HD),
            preferred_element_type=jnp.float32,
        )
        * score_scale
    )
    live_mask = (jnp.arange(cache_len)[None, :] < length[:, None])[:, None, None, :]
    peak = jnp.maximum(jnp.max(jnp.where(live_mask, scores, -jnp.inf), axis=-1), own_score)
    weights_cache = jnp.where(live_mask, jnp.exp(scores - peak[..., None]), 0.0)
    weight_own = jnp.exp(own_score - peak)
    total_mass = jnp.sum(weights_cache, axis=-1) + weight_own
    probs = (weights_cache / total_mass[..., None]).astype(jnp.bfloat16)
    prob_own = (weight_own / total_mass).astype(jnp.bfloat16)
    mixed_cache = jnp.einsum("rkgl,rlkd->rkgd", probs, v_heads, preferred_element_type=jnp.float32)
    mixed_own = prob_own.astype(jnp.float32)[..., None] * value_new.reshape(
        row_count, KVH, 1, HD
    ).astype(jnp.float32)
    return (mixed_cache + mixed_own).reshape(row_count, QH * HD).astype(jnp.bfloat16)


def row_weights(normed, route_ids, w_router):
    logits = jnp.dot(normed, w_router, preferred_element_type=jnp.float32)
    expert_count = w_router.shape[1]
    member_of = (route_ids[:, :, None] == jnp.arange(expert_count)[None, None, :]).astype(
        jnp.float32
    )
    chosen = jnp.sum(member_of * logits[:, None, :], axis=-1)
    combine = jax.nn.softmax(chosen, axis=-1)
    return jnp.sum(member_of * combine[:, :, None], axis=1)


def exchange(blocks):
    return lax.all_to_all(blocks, "dev", split_axis=0, concat_axis=0, tiled=True)


def local(
    x_in,
    queries,
    cache_keys,
    cache_values,
    new_keys,
    new_values,
    lengths,
    w_out,
    norm_gain,
    w_router,
    experts_idx,
    w_gate,
    w_up,
    w_down,
):
    devices = lax.axis_size("dev")
    expert_count = w_router.shape[1]
    per_expert = devices // expert_count
    out_shape = x_in.shape
    feature_dim = out_shape[2]
    rows = out_shape[0] * out_shape[1]

    def flat(a):
        return a.reshape((rows,) + a.shape[2:])

    attention = attend_rows(
        flat(queries),
        flat(cache_keys),
        flat(cache_values),
        flat(new_keys),
        flat(new_values),
        flat(lengths),
    )
    heads = jnp.transpose(attention.reshape(rows, devices, -1), (1, 0, 2))
    head_block = exchange(heads).reshape(devices * rows, -1)
    partial_attn = jnp.dot(head_block, w_out, preferred_element_type=jnp.float32)
    attn_parts = exchange(partial_attn.astype(jnp.bfloat16).reshape(devices, rows, feature_dim))
    resid = flat(x_in).astype(jnp.float32) + jnp.sum(attn_parts.astype(jnp.float32), axis=0)
    mean_square = jnp.mean(resid * resid, axis=-1, keepdims=True)
    normed = (resid * lax.rsqrt(mean_square + 1e-05) * norm_gain.astype(jnp.float32)).astype(
        jnp.bfloat16
    )
    weights = row_weights(normed, flat(experts_idx), w_router)
    high = weights.astype(jnp.bfloat16)
    low = (weights - high.astype(jnp.float32)).astype(jnp.bfloat16)
    padding = jnp.zeros((rows, 128 - 2 * expert_count), jnp.bfloat16)
    message = jnp.concatenate([normed, high, low, padding], axis=1)
    received = exchange(jnp.broadcast_to(message[None], (devices,) + message.shape))
    received = received.reshape(devices * rows, -1)
    all_rows = received[:, :feature_dim]
    packed = received[:, feature_dim : feature_dim + 2 * expert_count].astype(jnp.float32)
    expert = lax.axis_index("dev") // per_expert
    mine = (jnp.arange(2 * expert_count) % expert_count == expert).astype(jnp.float32)
    my_weight = jnp.sum(packed * mine[None, :], axis=1, keepdims=True)
    gate = jnp.dot(all_rows, w_gate, preferred_element_type=jnp.float32)
    upper = jnp.dot(all_rows, w_up, preferred_element_type=jnp.float32)
    hidden = (jax.nn.silu(gate) * upper).astype(jnp.bfloat16)
    partial = jnp.dot(hidden, w_down, preferred_element_type=jnp.float32) * my_weight
    parts = exchange(partial.astype(jnp.bfloat16).reshape(devices, rows, feature_dim))
    mixed = resid + jnp.sum(parts.astype(jnp.float32), axis=0)
    return mixed.astype(jnp.bfloat16).reshape(out_shape)


def solution(mesh):
    return jax.shard_map(
        local,
        mesh=mesh,
        in_specs=(
            P(None, ("groups", "dev"), None),
            P(None, ("groups", "dev"), None),
            P(None, ("groups", "dev"), None, None),
            P(None, ("groups", "dev"), None, None),
            P(None, ("groups", "dev"), None),
            P(None, ("groups", "dev"), None),
            P(None, ("groups", "dev")),
            P("dev", None),
            P(),
            P(),
            P(None, ("groups", "dev"), None),
            P(None, "dev"),
            P(None, "dev"),
            P("dev", None),
        ),
        out_specs=P(None, ("groups", "dev"), None),
        check_vma=False,
    )
```

time: 227 us -> 94.2 us (0.41)
  waiting for transfers between devices: 115 us -> 22.3 us
  blocking collectives: 0 us -> 29.4 us
  matrix products: 47.4 us -> 21.6 us
  starting transfers between devices: 30.1 us -> 7.11 us
  between operations: 14.3 us -> 0.19 us
  local copies, waits for them, and re-layouts: 12.4 us -> 9.35 us
  other arithmetic: 6.28 us -> 3.33 us
    unnamed x2 -> x0, waiting for transfers between devices: 86.4 us -> none
    all_to_all x0 -> x2, blocking collectives: none -> 29.4 us  [exchange(): lax.all_to_all(blocks, 'dev', split_axis=0, concat_axis=0, tiled=True)]
    dot_general x12 -> x3, matrix products: 43.9 us -> 20.4 us  [the longest x1 12.7 us: local(): jnp.dot(hidden, w_down, preferred_element_type=jnp.float32) * my_weight]
    all_to_all x6 -> x2, starting transfers between devices: 30.1 us -> 7.11 us  [exchange(): lax.all_to_all(blocks, 'dev', split_axis=0, concat_axis=0, tiled=True)]
    all_to_all x6 -> x2, waiting for transfers between devices: 28.7 us -> 22.3 us  [exchange(): lax.all_to_all(blocks, 'dev', split_axis=0, concat_axis=0, tiled=True)]
    slice x4 -> x1, local copies, waits for them, and re-layouts: 3.59 us -> 0.01 us  [local(): received[:, feature_dim:feature_dim + 2 * expert_count].astype(jnp.float32)]
    another operation x0 -> x2, local copies, waits for them, and re-layouts: none -> 2.33 us  [the longest x1 1.17 us: attend_rows(): v_heads = values_cache.reshape(row_count, cache_len, KVH, HD)]
  transfers between devices with their start and end apart: 7 -> 2, of which waited for: 5 -> 2; matrix products, arithmetic and copies ran while one was open for 22% -> 2% of each run, Pallas kernels for 0% -> 0%
where the time goes in v1:
time: 94.2 us; the launch traced here: 93.3 us
  blocking collectives  29.4 us (31%)
  waiting for transfers between devices  22.3 us (24%)
  matrix products  21.6 us (23%)
  local copies, waits for them, and re-layouts  9.35 us (10%)
  starting transfers between devices  7.11 us (8%)
  other arithmetic  3.33 us (4%)
    all_to_all x2, blocking collectives, exchange(): lax.all_to_all(blocks, 'dev', split_axis=0, concat_axis=0, tiled=True)  29.4 us
    all_to_all x2, waiting for transfers between devices, exchange(): lax.all_to_all(blocks, 'dev', split_axis=0, concat_axis=0, tiled=True)  22.3 us
    dot_general x1, matrix products, local(): jnp.dot(hidden, w_down, preferred_element_type=jnp.float32) * my_weight  12.7 us
    all_to_all x2, starting transfers between devices, exchange(): lax.all_to_all(blocks, 'dev', split_axis=0, concat_axis=0, tiled=True)  7.11 us
    dot_general x1, matrix products, local(): gate = jnp.dot(all_rows, w_gate, preferred_element_type=jnp.float32)  6.87 us
  transfers between devices with their start and end apart: 2, of which 2 were waited for; matrix products, arithmetic and copies ran while one was open for 2% of the time, Pallas kernels for 0%

profile of v1, /device:TPU:0, one launch (start us, length us, event | category | flops | bytes accessed | tf_op | source)
XLA Modules:
  0.0 93.3 jit_solution(9758993002873079434)
XLA Ops:
  0.0 0.0 copy-start
  0.0 0.9 lt.26
  0.9 0.1 iota_compare_fusion.1
  0.9 0.7 reshape.132
  1.6 0.7 reshape.127
  2.3 0.8 reshape_reshape.13
  3.1 1.2 %reshape_reshape.14 = bf16[4,128,4,128]{3,2,1,0:T(4,128)(2,1)S(1)} reshape(bf16[2,2,128,512]{3,2,1,0:T(8,128)(2,1)} %param.16) | data formatting | bytes 1048576 | tf_op jit(solution)/shard_map/reshape;reshape | solution.py:17
  4.3 0.1 fusion.26
  4.4 0.5 select_reduce_fusion
  4.9 0.2 fusion.15
  5.1 1.2 %reshape_reshape.16 = bf16[4,128,4,128]{3,2,1,0:T(4,128)(2,1)S(1)} reshape(bf16[2,2,128,512]{3,2,1,0:T(8,128)(2,1)} %param.17) | data formatting | bytes 1048576 | tf_op jit(solution)/shard_map/reshape;reshape | solution.py:18
  6.3 0.3 fusion.2
  6.6 0.1 convert_element_type.89
  6.7 13.8 %all_to_all.20 = bf16[16,4,192]{2,1,0:T(4,128)(2,1)S(1)} all-to-all(bf16[16,4,192]{2,1,0:T(4,128)(2,1)S(1)} %copy.42), channel_id=1, replica_groups=mesh['groups'=2,'dev'=16] {'dev'}, dimensions={0} | all-to-all | bytes 49152 | tf_op jit(solution)/shard_map/all_to_all | solution.py:59
  20.6 0.0 copy-done
  20.6 0.3 convolution_convert_fusion
  20.9 0.9 reshape.124
  21.8 3.6 %all-to-all-start.1 = ((bf16[16,4,3072]{2,1,0:T(4,128)(2,1)}), bf16[16,4,3072]{2,1,0:T(4,128)(2,1)S(1)}, u32[]{:S(2)}, u32[]{:S(2)}) async-start(bf16[16,4,3072]{2,1,0:T(4,128)(2,1)} %reshape.124), calls=%async_computation.1 | async-start | bytes 786432 | tf_op jit(solution)/shard_map/all_to_all | solution.py:59
  25.4 0.8 copy.47
  26.1 0.7 convert_element_type.94
  26.8 0.8 reshape.128
  27.6 9.9 %all-to-all-done.1 = bf16[16,4,3072]{2,1,0:T(4,128)(2,1)S(1)} async-done(((bf16[16,4,3072]{2,1,0:T(4,128)(2,1)}), bf16[16,4,3072]{2,1,0:T(4,128)(2,1)S(1)}, u32[]{:S(2)}, u32[]{:S(2)}) %all-to-all-start.1) | async-done | bytes 393248 | tf_op jit(solution)/shard_map/all_to_all | solution.py:59
  37.5 0.2 convert_reduce_fusion.1
  37.7 0.9 multiply_reduce_fusion
  38.6 0.1 rsqrt.12
  38.7 0.1 multiply_convert_fusion
  38.8 0.9 fusion.27
  39.7 0.2 select_reduce_fusion.2
  39.9 0.1 select_reduce_fusion.1
  40.0 0.1 concatenate.3
  40.1 0.8 broadcast_in_dim.26
  40.9 3.6 %all-to-all-start.2 = ((bf16[16,4,3200]{2,1,0:T(4,128)(2,1)}), bf16[16,4,3200]{2,1,0:T(4,128)(2,1)S(1)}, u32[]{:S(2)}, u32[]{:S(2)}) async-start(bf16[16,4,3200]{2,1,0:T(4,128)(2,1)} %broadcast_in_dim.26), calls=%async_computation.2 | async-start | bytes 819200 | tf_op jit(solution)/shard_map/all_to_all | solution.py:59
  44.5 12.4 %all-to-all-done.2 = bf16[16,4,3200]{2,1,0:T(4,128)(2,1)S(1)} async-done(((bf16[16,4,3200]{2,1,0:T(4,128)(2,1)}), bf16[16,4,3200]{2,1,0:T(4,128)(2,1)S(1)}, u32[]{:S(2)}, u32[]{:S(2)}) %all-to-all-start.2) | async-done | bytes 409632 | tf_op jit(solution)/shard_map/all_to_all | solution.py:59
  56.9 0.1 reshape.125
  57.0 0.1 copy.48
  57.1 6.9 %fusion.12 = f32[64,2048]{1,0:T(8,128)S(1)} fusion(bf16[3072,2048]{1,0:T(8,128)(2,1)} %param.25, bf16[64,3200]{1,0:T(8,128)(2,1)S(1)} %reshape.125), kind=kOutput, calls=%fused_computation.18 | convolution fusion | flops 805306368 | bytes 13500416 | tf_op jit(solution)/shard_map/dot_general | solution.py:117
  64.0 0.1 multiply_reduce_fusion.1
  64.1 0.0 copy-start.1
  64.1 12.7 %fusion = bf16[64,3072]{1,0:T(8,128)(2,1)S(1)} fusion(bf16[2048,3072]{1,0:T(8,128)(2,1)} %param.27, bf16[3072,2048]{1,0:T(8,128)(2,1)} %param.26, f32[64,2048]{1,0:T(8,128)S(1)} %fusion.12, f32[64]{0:T(128)S(1)} %multiply_reduce_fusion.1, bf16[64,3200]{1,0:T(8,128)(2,1)S(1)} %reshape.125), kind=kOutput, calls=%fused_computation.1 | convolution fusion | flops 1611792384 | bytes 26477056 | tf_op jit(solution)/shard_map/dot_general | solution.py:120
  76.7 0.1 reshape.126
  76.9 15.6 %all_to_all.21 = bf16[16,4,3072]{2,1,0:T(4,128)(2,1)S(1)} all-to-all(bf16[16,4,3072]{2,1,0:T(4,128)(2,1)S(1)} %reshape.126), channel_id=1, replica_groups=mesh['groups'=2,'dev'=16] {'dev'}, dimensions={0} | all-to-all | bytes 786432 | tf_op jit(solution)/shard_map/all_to_all | solution.py:59
  92.4 0.2 convert_reduce_fusion
  92.7 0.0 copy-done.1
  92.7 0.6 add_convert_fusion
  (14 shorter events, 0.2 us)
Async XLA Ops:
  0.0 20.6 %copy-start = (bf16[192,3072]{1,0:T(8,128)(2,1)S(1)}, bf16[192,3072]{1,0:T(8,128)(2,1)}, u32[]{:S(2)}) copy-start(bf16[192,3072]{1,0:T(8,128)(2,1)} %param.21) | copy-start | bytes 3538948
  21.8 15.7 %all-to-all-start.1 = ((bf16[16,4,3072]{2,1,0:T(4,128)(2,1)}), bf16[16,4,3072]{2,1,0:T(4,128)(2,1)S(1)}, u32[]{:S(2)}, u32[]{:S(2)}) async-start(bf16[16,4,3072]{2,1,0:T(4,128)(2,1)} %reshape.124), calls=%async_computation.1 | async-start | bytes 786432 | tf_op jit(solution)/shard_map/all_to_all | solution.py:59
  40.9 16.0 %all-to-all-start.2 = ((bf16[16,4,3200]{2,1,0:T(4,128)(2,1)}), bf16[16,4,3200]{2,1,0:T(4,128)(2,1)S(1)}, u32[]{:S(2)}, u32[]{:S(2)}) async-start(bf16[16,4,3200]{2,1,0:T(4,128)(2,1)} %broadcast_in_dim.26), calls=%async_computation.2 | async-start | bytes 819200 | tf_op jit(solution)/shard_map/all_to_all | solution.py:59
  64.1 28.6 %copy-start.1 = (bf16[2,2,3072]{2,1,0:T(2,128)(2,1)S(1)}, bf16[2,2,3072]{2,1,0:T(2,128)(2,1)}, u32[]{:S(2)}) copy-start(bf16[2,2,3072]{2,1,0:T(2,128)(2,1)} %param.14) | copy-start | bytes 73732

commit v2 on v1

v2 whole, which is shorter than its diff:
```python
import math

import jax
import jax.numpy as jnp
from jax import lax
from jax.experimental import pallas as pl
from jax.experimental.pallas import tpu as pltpu
from jax.sharding import PartitionSpec as P

QH = 24
KVH = 4
HD = 128
LANES = 128
MIB = 1 << 20

VMEM = pl.BlockSpec(memory_space=pltpu.VMEM)
SMEM = pl.BlockSpec(memory_space=pltpu.SMEM)


def params(mib):
    return pltpu.CompilerParams(vmem_limit_bytes=mib * MIB)


def attend_kernel(len_ref, q_ref, k_ref, v_ref, nk_ref, nv_ref, out_ref):
    batches, sessions = q_ref.shape[:2]
    cache_len = k_ref.shape[2]
    width = KVH * HD
    per_kv = QH // KVH
    scale = 1.0 / math.sqrt(HD)
    head = lax.broadcasted_iota(jnp.int32, (QH, width), 0) // per_kv
    lane = lax.broadcasted_iota(jnp.int32, (QH, width), 1) // HD
    own_kv = head == lane
    slot = lax.broadcasted_iota(jnp.int32, (QH, cache_len), 1)
    rows = []
    for m in range(batches):
        q_all = q_ref[m].astype(jnp.float32)
        nk_all = nk_ref[m].astype(jnp.float32)
        nv_all = nv_ref[m].astype(jnp.float32)
        for s in range(sessions):
            q_row = q_all[s : s + 1]
            q_heads = jnp.concatenate([q_row[:, h * HD : (h + 1) * HD] for h in range(QH)], axis=0)
            q_wide = jnp.where(own_kv, jnp.concatenate([q_heads] * KVH, axis=1), 0.0)
            scores = (
                lax.dot_general(
                    q_wide.astype(jnp.bfloat16),
                    k_ref[m, s],
                    (((1,), (1,)), ((), ())),
                    preferred_element_type=jnp.float32,
                )
                * scale
            )
            own_score = jnp.sum(q_wide * nk_all[s : s + 1], axis=1, keepdims=True) * scale
            live = slot < len_ref[m, s]
            peak = jnp.maximum(
                jnp.max(jnp.where(live, scores, -jnp.inf), axis=1, keepdims=True), own_score
            )
            mass = jnp.where(live, jnp.exp(scores - peak), 0.0)
            own_mass = jnp.exp(own_score - peak)
            total = jnp.sum(mass, axis=1, keepdims=True) + own_mass
            probs = (mass / total).astype(jnp.bfloat16)
            own_prob = (own_mass / total).astype(jnp.bfloat16).astype(jnp.float32)
            wide = jnp.dot(probs, v_ref[m, s], preferred_element_type=jnp.float32)
            wide = jnp.where(own_kv, wide + own_prob * nv_all[s : s + 1], 0.0)
            heads = wide[:, :HD]
            for k in range(1, KVH):
                heads = heads + wide[:, k * HD : (k + 1) * HD]
            rows.append(jnp.concatenate([heads[h : h + 1] for h in range(QH)], axis=1))
    attention = jnp.concatenate(rows, axis=0).astype(jnp.bfloat16)
    devices, _, part = out_ref.shape
    for d in range(devices):
        out_ref[d] = attention[:, d * part : (d + 1) * part]


def stacked(ref, width):
    blocks = [ref[d][:, :width].astype(jnp.float32) for d in range(ref.shape[0])]
    return jnp.concatenate(blocks, axis=0).astype(jnp.bfloat16)


def project_kernel(x_ref, w_ref, out_ref):
    devices, rows, features = out_ref.shape
    inputs = stacked(x_ref, x_ref.shape[2])
    chunk = 512 if features % 512 == 0 else LANES
    for start in range(0, features, chunk):
        part = jnp.dot(
            inputs, w_ref[:, start : start + chunk], preferred_element_type=jnp.float32
        )
        for d in range(devices):
            out_ref[d, :, start : start + chunk] = part[d * rows : (d + 1) * rows].astype(
                jnp.bfloat16
            )


def norm_kernel(idx_ref, parts_ref, x_ref, gain_ref, router_ref, resid_ref, out_ref):
    batches, sessions, features = x_ref.shape
    experts = router_ref.shape[1]
    rows = batches * sessions
    x_rows = jnp.concatenate([x_ref[m].astype(jnp.float32) for m in range(batches)], axis=0)
    total = parts_ref[0].astype(jnp.float32)
    for d in range(1, parts_ref.shape[0]):
        total = total + parts_ref[d].astype(jnp.float32)
    resid = x_rows + total
    resid_ref[...] = resid
    mean_square = jnp.mean(resid * resid, axis=1, keepdims=True)
    normed = (resid * lax.rsqrt(mean_square + 1e-05) * gain_ref[...].astype(jnp.float32)).astype(
        jnp.bfloat16
    )
    logits = jnp.dot(normed, router_ref[...], preferred_element_type=jnp.float32)
    row = lax.broadcasted_iota(jnp.int32, (rows, experts), 0)
    column = lax.broadcasted_iota(jnp.int32, (rows, experts), 1)
    member = row < 0
    for m in range(batches):
        for s in range(sessions):
            for k in range(idx_ref.shape[2]):
                member = member | ((row == m * sessions + s) & (column == idx_ref[m, s, k]))
    peak = jnp.max(jnp.where(member, logits, -jnp.inf), axis=1, keepdims=True)
    mass = jnp.where(member, jnp.exp(logits - peak), 0.0)
    weights = mass / jnp.sum(mass, axis=1, keepdims=True)
    high = weights.astype(jnp.bfloat16).astype(jnp.float32)
    low = weights - high
    extra = jnp.concatenate(
        [high, low, jnp.zeros((rows, LANES - 2 * experts), jnp.float32)], axis=1
    ).astype(jnp.bfloat16)
    for d in range(out_ref.shape[0]):
        out_ref[d, :, :features] = normed
        out_ref[d, :, features:] = extra


def expert_kernel(expert_count, expert_ref, x_ref, gate_ref, up_ref, down_ref, out_ref, hidden):
    devices, rows, features = out_ref.shape
    units = gate_ref.shape[1]
    inputs = stacked(x_ref, features)
    packed = jnp.concatenate(
        [x_ref[d][:, features:].astype(jnp.float32) for d in range(devices)], axis=0
    )
    lane = lax.broadcasted_iota(jnp.int32, packed.shape, 1)
    mine = (lane % expert_count == expert_ref[0]) & (lane < 2 * expert_count)
    weight = jnp.sum(jnp.where(mine, packed, 0.0), axis=1, keepdims=True)
    chunk = min(512, units)
    for start in range(0, units, chunk):
        cut = slice(start, start + chunk)
        gate = jnp.dot(inputs, gate_ref[:, cut], preferred_element_type=jnp.float32)
        upper = jnp.dot(inputs, up_ref[:, cut], preferred_element_type=jnp.float32)
        hidden[:, cut] = (jax.nn.silu(gate) * upper).astype(jnp.bfloat16)
    chunk = 512 if features % 512 == 0 else LANES
    for start in range(0, features, chunk):
        cut = slice(start, start + chunk)
        part = jnp.dot(hidden[...], down_ref[:, cut], preferred_element_type=jnp.float32) * weight
        for d in range(devices):
            out_ref[d, :, cut] = part[d * rows : (d + 1) * rows].astype(jnp.bfloat16)


def final_kernel(resid_ref, parts_ref, out_ref):
    batches, sessions, _ = out_ref.shape
    total = parts_ref[0].astype(jnp.float32)
    for d in range(1, parts_ref.shape[0]):
        total = total + parts_ref[d].astype(jnp.float32)
    mixed = resid_ref[...] + total
    for m in range(batches):
        out_ref[m] = mixed[m * sessions : (m + 1) * sessions].astype(jnp.bfloat16)


def exchange(blocks):
    return lax.all_to_all(blocks, "dev", split_axis=0, concat_axis=0, tiled=True)


def local(
    x_in,
    queries,
    cache_keys,
    cache_values,
    new_keys,
    new_values,
    lengths,
    w_out,
    norm_gain,
    w_router,
    experts_idx,
    w_gate,
    w_up,
    w_down,
):
    devices = lax.axis_size("dev")
    expert_count = w_router.shape[1]
    batches, sessions, features = x_in.shape
    rows = batches * sessions
    units = w_gate.shape[1]

    def blocks(width):
        return jax.ShapeDtypeStruct((devices, rows, width), jnp.bfloat16)

    heads = pl.pallas_call(
        attend_kernel,
        in_specs=[SMEM] + [VMEM] * 5,
        out_specs=VMEM,
        out_shape=blocks(w_out.shape[0]),
        compiler_params=params(8),
        name="attend",
    )(lengths, queries, cache_keys, cache_values, new_keys, new_values)
    head_blocks = exchange(heads)
    partial_attn = pl.pallas_call(
        project_kernel,
        in_specs=[VMEM] * 2,
        out_specs=VMEM,
        out_shape=blocks(features),
        compiler_params=params(8),
        name="project",
    )(head_blocks, w_out)
    attn_parts = exchange(partial_attn)
    resid, message = pl.pallas_call(
        norm_kernel,
        in_specs=[SMEM] + [VMEM] * 4,
        out_specs=(VMEM, VMEM),
        out_shape=(jax.ShapeDtypeStruct((rows, features), jnp.float32), blocks(features + LANES)),
        compiler_params=params(8),
        name="norm",
    )(experts_idx, attn_parts, x_in, norm_gain.reshape(1, features), w_router)
    received = exchange(message)
    expert = (lax.axis_index("dev") // (devices // expert_count)).astype(jnp.int32)
    partial = pl.pallas_call(
        lambda *refs: expert_kernel(expert_count, *refs),
        in_specs=[SMEM] + [VMEM] * 4,
        out_specs=VMEM,
        out_shape=blocks(features),
        scratch_shapes=[pltpu.VMEM((devices * rows, units), jnp.bfloat16)],
        compiler_params=params(8),
        name="experts",
    )(
        expert.reshape(1),
        received,
        *[pltpu.with_memory_space_constraint(w, pltpu.VMEM) for w in (w_gate, w_up, w_down)],
    )
    parts = exchange(partial)
    return pl.pallas_call(
        final_kernel,
        in_specs=[VMEM] * 2,
        out_specs=VMEM,
        out_shape=jax.ShapeDtypeStruct(x_in.shape, jnp.bfloat16),
        compiler_params=params(8),
        name="final",
    )(resid, parts)


def solution(mesh):
    return jax.shard_map(
        local,
        mesh=mesh,
        in_specs=(
            P(None, ("groups", "dev"), None),
            P(None, ("groups", "dev"), None),
            P(None, ("groups", "dev"), None, None),
            P(None, ("groups", "dev"), None, None),
            P(None, ("groups", "dev"), None),
            P(None, ("groups", "dev"), None),
            P(None, ("groups", "dev")),
            P("dev", None),
            P(),
            P(),
            P(None, ("groups", "dev"), None),
            P(None, "dev"),
            P(None, "dev"),
            P("dev", None),
        ),
        out_specs=P(None, ("groups", "dev"), None),
        check_vma=False,
    )
```

time: 94.2 us -> 96 us (1.019)
  matrix products: 21.6 us -> 0 us
  local copies, waits for them, and re-layouts: 9.35 us -> 23.1 us
  Pallas kernels: 0 us -> 12.7 us
  other arithmetic: 3.33 us -> 0 us
    unnamed x5 -> x25, local copies, waits for them, and re-layouts: 0.08 us -> 22.4 us
    dot_general x7 -> x0, matrix products: 21.6 us -> none  [the longest x1 12.7 us: local(): jnp.dot(hidden, w_down, preferred_element_type=jnp.float32) * my_weight]
    pallas_call x0 -> x5, Pallas kernels: none -> 12.7 us  [the longest x1 6.76 us: local(): pl.pallas_call(lambda *refs: expert_kernel(expert_count, *refs), in_specs...]
    another operation x4 -> x0, local copies, waits for them, and re-layouts: 3.79 us -> none  [the longest x1 1.17 us: attend_rows(): v_heads = values_cache.reshape(row_count, cache_len, KVH, HD)]
    reduce_sum x8 -> x0, other arithmetic: 1.75 us -> none  [the longest x1 0.86 us: local(): mean_square = jnp.mean(resid * resid, axis=-1, keepdims=True)]
    convert_element_type x3 -> x0, local copies, waits for them, and re-layouts: 1.55 us -> none  [the longest x1 0.76 us: local(): flat(x_in).astype(jnp.float32)]
    convert_element_type x5 -> x0, other arithmetic: 1.44 us -> none  [the longest x1 0.69 us: local(): norm_gain.astype(jnp.float32)]
where the time goes in v2:
time: 96 us; the launch traced here: 95.1 us
  blocking collectives  29.4 us (31%)
  local copies, waits for them, and re-layouts  23.1 us (24%)
  waiting for transfers between devices  22.7 us (24%)
  Pallas kernels  12.7 us (13%)
  starting transfers between devices  7.11 us (7%)
    all_to_all x2, blocking collectives, exchange(): lax.all_to_all(blocks, 'dev', split_axis=0, concat_axis=0, tiled=True)  29.4 us
    all_to_all x2, waiting for transfers between devices, exchange(): lax.all_to_all(blocks, 'dev', split_axis=0, concat_axis=0, tiled=True)  22.7 us
    unnamed x25, local copies, waits for them, and re-layouts  22.4 us
    all_to_all x2, starting transfers between devices, exchange(): lax.all_to_all(blocks, 'dev', split_axis=0, concat_axis=0, tiled=True)  7.11 us
    pallas_call x1, Pallas kernels, local(): pl.pallas_call(lambda *refs: expert_kernel(expert_count, *refs), in_specs...  6.76 us
    pallas_call x1, Pallas kernels, local(): pl.pallas_call(attend_kernel, in_specs=[SMEM] + [VMEM] * 5, out_specs=VME...  2.22 us
    pallas_call x1, Pallas kernels, local(): pl.pallas_call(norm_kernel, in_specs=[SMEM] + [VMEM] * 4, out_specs=(VMEM...  1.95 us
  transfers between devices with their start and end apart: 2, of which 2 were waited for; matrix products, arithmetic and copies ran while one was open for 2% of the time, Pallas kernels for 0%

profile of v2, /device:TPU:0, one launch (start us, length us, event | category | flops | bytes accessed | tf_op | source)
XLA Modules:
  0.0 95.1 jit_solution(18193227136253813454)
XLA Ops:
  0.0 0.0 copy-start.4
  0.0 1.0 %copy-done.4 = bf16[2,2,128,512]{3,2,1,0:T(8,128)(2,1)S(1)} copy-done((bf16[2,2,128,512]{3,2,1,0:T(8,128)(2,1)S(1)}, bf16[2,2,128,512]{3,2,1,0:T(8,128)(2,1)}, u32[]{:S(2)}) %copy-start.4) | copy-done | bytes 524312
  1.0 0.0 copy-start.5
  1.0 1.0 %copy-done.5 = bf16[2,2,128,512]{3,2,1,0:T(8,128)(2,1)S(1)} copy-done((bf16[2,2,128,512]{3,2,1,0:T(8,128)(2,1)S(1)}, bf16[2,2,128,512]{3,2,1,0:T(8,128)(2,1)}, u32[]{:S(2)}) %copy-start.5) | copy-done | bytes 524312
  2.1 0.0 copy-start.6
  2.1 0.7 copy-done.6
  2.8 0.0 copy-start.8
  2.8 0.7 copy-done.8
  3.5 0.0 copy-start.9
  3.5 0.7 copy-done.9
  4.2 0.0 copy-start.11
  4.2 0.7 copy-done.11
  4.9 2.2 %attend.1 = bf16[16,4,192]{2,1,0:T(4,128)(2,1)S(1)} custom-call(s32[2,2]{1,0:T(2,128)S(1)} %copy-done.11, bf16[2,2,3072]{2,1,0:T(2,128)(2,1)S(1)} %copy-done.6, bf16[2,2,128,512]{3,2,1,0:T(8,128)(2,1)S(1)} %copy-done.4, bf16[2,2,128,512]{3,2,1,0:T(8,128)(2,1)S(1)} %copy-done.5, bf16[2,2,512]{2,1,0:T(2,128)(2,1)S(1)} %copy-done.8, ...), custom_call_target="tpu_custom_call" | custom-call | tf_op jit(solution)/shard_map/attend/pallas_call | solution.py:191
  7.1 13.8 %all_to_all.20.x_ref = bf16[16,4,192]{2,1,0:T(4,128)(2,1)S(1)} all-to-all(bf16[16,4,192]{2,1,0:T(4,128)(2,1)S(1)} %attend.1), channel_id=1, replica_groups=mesh['groups'=2,'dev'=16] {'dev'}, dimensions={0} | all-to-all | bytes 49152 | tf_op jit(solution)/shard_map/all_to_all | solution.py:163
  20.9 0.0 copy-start.3
  20.9 1.3 %copy-done.3 = bf16[192,3072]{1,0:T(8,128)(2,1)S(1)} copy-done((bf16[192,3072]{1,0:T(8,128)(2,1)S(1)}, bf16[192,3072]{1,0:T(8,128)(2,1)}, u32[]{:S(2)}) %copy-start.3) | copy-done | bytes 1179672
  22.2 1.1 %project.1 = bf16[16,4,3072]{2,1,0:T(4,128)(2,1)} custom-call(bf16[16,4,192]{2,1,0:T(4,128)(2,1)S(1)} %all_to_all.20.x_ref, bf16[192,3072]{1,0:T(8,128)(2,1)S(1)} %copy-done.3), custom_call_target="tpu_custom_call" | custom-call | tf_op jit(solution)/shard_map/project/pallas_call | solution.py:200
  23.3 3.6 %all-to-all-start.1 = ((bf16[16,4,3072]{2,1,0:T(4,128)(2,1)}), bf16[16,4,3072]{2,1,0:T(4,128)(2,1)S(1)}, u32[]{:S(2)}, u32[]{:S(2)}) async-start(bf16[16,4,3072]{2,1,0:T(4,128)(2,1)} %project.1), calls=%async_computation.1 | async-start | bytes 786432 | tf_op jit(solution)/shard_map/all_to_all | solution.py:163
  26.9 0.7 reshape.6.gain_ref
  27.6 1.2 %copy.15.router_ref = bf16[3072,4]{1,0:T(8,128)(2,1)S(1)} copy(bf16[3072,4]{0,1:T(4,128)(2,1)} %param.23) | data formatting | bytes 49152 | tf_op args[9]
  28.7 10.3 %all-to-all-done.1.parts_ref = bf16[16,4,3072]{2,1,0:T(4,128)(2,1)S(1)} async-done(((bf16[16,4,3072]{2,1,0:T(4,128)(2,1)}), bf16[16,4,3072]{2,1,0:T(4,128)(2,1)S(1)}, u32[]{:S(2)}, u32[]{:S(2)}) %all-to-all-start.1) | async-done | bytes 393248 | tf_op jit(solution)/shard_map/all_to_all | solution.py:163
  39.0 0.0 copy-start.7
  39.0 0.7 copy-done.7
  39.7 0.0 copy-start.10
  39.8 0.7 copy-done.10
  40.4 1.9 %norm.1 = (f32[4,3072]{1,0:T(4,128)S(1)}, bf16[16,4,3200]{2,1,0:T(4,128)(2,1)}) custom-call(s32[2,2,2]{2,1,0:T(2,128)S(1)} %copy-done.10, bf16[16,4,3072]{2,1,0:T(4,128)(2,1)S(1)} %all-to-all-done.1.parts_ref, bf16[2,2,3072]{2,1,0:T(2,128)(2,1)S(1)} %copy-done.7, bf16[1,3072]{1,0:T(2,128)(2,1)S(1)} %reshape.6.gain_ref, bf16[3072,4]{1,0:T(8,128)(2,1)S(1)} %copy.15.router_ref), custom_call_target="tpu_custom_call" | custom-call | tf_op jit(solution)/shard_map/norm/pallas_call | solution.py:209
  42.4 3.6 %all-to-all-start.2 = ((bf16[16,4,3200]{2,1,0:T(4,128)(2,1)}), bf16[16,4,3200]{2,1,0:T(4,128)(2,1)S(1)}, u32[]{:S(2)}, u32[]{:S(2)}) async-start(bf16[16,4,3200]{2,1,0:T(4,128)(2,1)} %get-tuple-element.8), calls=%async_computation.2 | async-start | bytes 819200 | tf_op jit(solution)/shard_map/all_to_all | solution.py:163
  46.0 12.4 %all-to-all-done.2.refs_1_ = bf16[16,4,3200]{2,1,0:T(4,128)(2,1)S(1)} async-done(((bf16[16,4,3200]{2,1,0:T(4,128)(2,1)}), bf16[16,4,3200]{2,1,0:T(4,128)(2,1)S(1)}, u32[]{:S(2)}, u32[]{:S(2)}) %all-to-all-start.2) | async-done | bytes 409632 | tf_op jit(solution)/shard_map/all_to_all | solution.py:163
  58.4 0.0 copy-start
  58.4 4.6 %copy-done = bf16[3072,2048]{1,0:T(8,128)(2,1)S(1)} copy-done((bf16[3072,2048]{1,0:T(8,128)(2,1)S(1)}, bf16[3072,2048]{1,0:T(8,128)(2,1)}, u32[]{:S(2)}) %copy-start) | copy-done | bytes 12582936
  62.9 0.0 copy-start.1
  62.9 4.6 %copy-done.1 = bf16[3072,2048]{1,0:T(8,128)(2,1)S(1)} copy-done((bf16[3072,2048]{1,0:T(8,128)(2,1)S(1)}, bf16[3072,2048]{1,0:T(8,128)(2,1)}, u32[]{:S(2)}) %copy-start.1) | copy-done | bytes 12582936
  67.5 0.0 copy-start.2
  67.5 4.6 %copy-done.2 = bf16[2048,3072]{1,0:T(8,128)(2,1)S(1)} copy-done((bf16[2048,3072]{1,0:T(8,128)(2,1)S(1)}, bf16[2048,3072]{1,0:T(8,128)(2,1)}, u32[]{:S(2)}) %copy-start.2) | copy-done | bytes 12582936
  72.1 6.8 %experts.1 = bf16[16,4,3072]{2,1,0:T(4,128)(2,1)S(1)} custom-call(s32[1]{0:T(128)} %bitcast.refs_0_, bf16[16,4,3200]{2,1,0:T(4,128)(2,1)S(1)} %all-to-all-done.2.refs_1_, bf16[3072,2048]{1,0:T(8,128)(2,1)S(1)} %copy-done, bf16[3072,2048]{1,0:T(8,128)(2,1)S(1)} %copy-done.1, bf16[2048,3072]{1,0:T(8,128)(2,1)S(1)} %copy-done.2), custom_call_target="tpu_custom_call" | custom-call | tf_op jit(solution)/shard_map/experts/pallas_call | solution.py:219
  78.9 15.6 %all_to_all.21.parts_ref = bf16[16,4,3072]{2,1,0:T(4,128)(2,1)S(1)} all-to-all(bf16[16,4,3072]{2,1,0:T(4,128)(2,1)S(1)} %experts.1), channel_id=1, replica_groups=mesh['groups'=2,'dev'=16] {'dev'}, dimensions={0} | all-to-all | bytes 786432 | tf_op jit(solution)/shard_map/all_to_all | solution.py:163
  94.4 0.7 final.1
Async XLA Ops:
  0.0 1.0 %copy-start.4 = (bf16[2,2,128,512]{3,2,1,0:T(8,128)(2,1)S(1)}, bf16[2,2,128,512]{3,2,1,0:T(8,128)(2,1)}, u32[]{:S(2)}) copy-start(bf16[2,2,128,512]{3,2,1,0:T(8,128)(2,1)} %k_ref.1) | copy-start | bytes 1572868
  1.0 1.0 %copy-start.5 = (bf16[2,2,128,512]{3,2,1,0:T(8,128)(2,1)S(1)}, bf16[2,2,128,512]{3,2,1,0:T(8,128)(2,1)}, u32[]{:S(2)}) copy-start(bf16[2,2,128,512]{3,2,1,0:T(8,128)(2,1)} %v_ref.1) | copy-start | bytes 1572868
  2.1 0.7 copy-start.6
  2.8 0.7 copy-start.8
  3.5 0.7 copy-start.9
  4.2 0.7 copy-start.11
  20.9 1.3 %copy-start.3 = (bf16[192,3072]{1,0:T(8,128)(2,1)S(1)}, bf16[192,3072]{1,0:T(8,128)(2,1)}, u32[]{:S(2)}) copy-start(bf16[192,3072]{1,0:T(8,128)(2,1)} %w_ref.1) | copy-start | bytes 3538948
  23.3 15.7 %all-to-all-start.1 = ((bf16[16,4,3072]{2,1,0:T(4,128)(2,1)}), bf16[16,4,3072]{2,1,0:T(4,128)(2,1)S(1)}, u32[]{:S(2)}, u32[]{:S(2)}) async-start(bf16[16,4,3072]{2,1,0:T(4,128)(2,1)} %project.1), calls=%async_computation.1 | async-start | bytes 786432 | tf_op jit(solution)/shard_map/all_to_all | solution.py:163
  39.0 0.7 copy-start.7
  39.7 0.7 copy-start.10
  42.4 16.0 %all-to-all-start.2 = ((bf16[16,4,3200]{2,1,0:T(4,128)(2,1)}), bf16[16,4,3200]{2,1,0:T(4,128)(2,1)S(1)}, u32[]{:S(2)}, u32[]{:S(2)}) async-start(bf16[16,4,3200]{2,1,0:T(4,128)(2,1)} %get-tuple-element.8), calls=%async_computation.2 | async-start | bytes 819200 | tf_op jit(solution)/shard_map/all_to_all | solution.py:163
  58.4 4.6 %copy-start = (bf16[3072,2048]{1,0:T(8,128)(2,1)S(1)}, bf16[3072,2048]{1,0:T(8,128)(2,1)}, u32[]{:S(2)}) copy-start(bf16[3072,2048]{1,0:T(8,128)(2,1)} %refs_2_.1) | copy-start | bytes 37748740
  62.9 4.6 %copy-start.1 = (bf16[3072,2048]{1,0:T(8,128)(2,1)S(1)}, bf16[3072,2048]{1,0:T(8,128)(2,1)}, u32[]{:S(2)}) copy-start(bf16[3072,2048]{1,0:T(8,128)(2,1)} %refs_3_.1) | copy-start | bytes 37748740
  67.5 4.6 %copy-start.2 = (bf16[2048,3072]{1,0:T(8,128)(2,1)S(1)}, bf16[2048,3072]{1,0:T(8,128)(2,1)}, u32[]{:S(2)}) copy-start(bf16[2048,3072]{1,0:T(8,128)(2,1)} %refs_4_.1) | copy-start | bytes 37748740

commit v3 on v2

v3 whole, which is shorter than its diff:
```python
import math

import jax
import jax.numpy as jnp
from jax import lax
from jax.experimental import pallas as pl
from jax.experimental.pallas import tpu as pltpu
from jax.sharding import PartitionSpec as P

QH = 24
KVH = 4
HD = 128
LANES = 128
CHUNK = 512
MIB = 1 << 20

VMEM = pl.BlockSpec(memory_space=pltpu.VMEM)
SMEM = pl.BlockSpec(memory_space=pltpu.SMEM)
HBM = pl.BlockSpec(memory_space=pltpu.HBM)
ANY = pl.BlockSpec(memory_space=pl.ANY)


def params(mib):
    return pltpu.CompilerParams(vmem_limit_bytes=mib * MIB)


def attend_kernel(len_ref, *refs):
    operands, out_ref, buffers, sems = refs[:5], refs[5], refs[6:11], refs[11]
    copies = [
        pltpu.make_async_copy(operands[i], buffers[i], sems.at[i])
        for i in range(len(operands))
    ]
    for copy in copies:
        copy.start()
    for copy in copies:
        copy.wait()
    q_ref, k_ref, v_ref, nk_ref, nv_ref = buffers
    batches, sessions = q_ref.shape[:2]
    cache_len = k_ref.shape[2]
    width = KVH * HD
    per_kv = QH // KVH
    scale = 1.0 / math.sqrt(HD)
    head = lax.broadcasted_iota(jnp.int32, (QH, width), 0) // per_kv
    lane = lax.broadcasted_iota(jnp.int32, (QH, width), 1) // HD
    own_kv = head == lane
    slot = lax.broadcasted_iota(jnp.int32, (QH, cache_len), 1)
    rows = []
    for m in range(batches):
        q_all = q_ref[m].astype(jnp.float32)
        nk_all = nk_ref[m].astype(jnp.float32)
        nv_all = nv_ref[m].astype(jnp.float32)
        for s in range(sessions):
            q_row = q_all[s : s + 1]
            q_heads = jnp.concatenate([q_row[:, h * HD : (h + 1) * HD] for h in range(QH)], axis=0)
            q_wide = jnp.where(own_kv, jnp.concatenate([q_heads] * KVH, axis=1), 0.0)
            scores = (
                lax.dot_general(
                    q_wide.astype(jnp.bfloat16),
                    k_ref[m, s],
                    (((1,), (1,)), ((), ())),
                    preferred_element_type=jnp.float32,
                )
                * scale
            )
            own_score = jnp.sum(q_wide * nk_all[s : s + 1], axis=1, keepdims=True) * scale
            live = slot < len_ref[m, s]
            peak = jnp.maximum(
                jnp.max(jnp.where(live, scores, -jnp.inf), axis=1, keepdims=True), own_score
            )
            mass = jnp.where(live, jnp.exp(scores - peak), 0.0)
            own_mass = jnp.exp(own_score - peak)
            total = jnp.sum(mass, axis=1, keepdims=True) + own_mass
            probs = (mass / total).astype(jnp.bfloat16)
            own_prob = (own_mass / total).astype(jnp.bfloat16).astype(jnp.float32)
            wide = jnp.dot(probs, v_ref[m, s], preferred_element_type=jnp.float32)
            wide = jnp.where(own_kv, wide + own_prob * nv_all[s : s + 1], 0.0)
            heads = wide[:, :HD]
            for k in range(1, KVH):
                heads = heads + wide[:, k * HD : (k + 1) * HD]
            rows.append(jnp.concatenate([heads[h : h + 1] for h in range(QH)], axis=1))
    attention = jnp.concatenate(rows, axis=0).astype(jnp.bfloat16)
    devices, _, part = out_ref.shape
    for d in range(devices):
        out_ref[d] = attention[:, d * part : (d + 1) * part]


PIECES = 4


def fetch_kernel(cuts, *refs):
    count = len(cuts)
    sources, targets, token, sems = refs[:count], refs[-count - 2 : -2], refs[-2], refs[-1]
    token[...] = jnp.zeros(token.shape, token.dtype)
    copies = []
    for source, target, cut in zip(sources, targets, cuts):
        if cut is None:
            copies.append(pltpu.make_async_copy(source, target, sems.at[len(copies)]))
        else:
            size = cut[1] // PIECES
            for at in range(0, cut[1], size):
                copies.append(
                    pltpu.make_async_copy(
                        source.at[pl.ds(cut[0] + at, size)],
                        target.at[pl.ds(at, size)],
                        sems.at[len(copies)],
                    )
                )
    for copy in copies:
        copy.start()
    for copy in copies:
        copy.wait()


def fetch(arrays, cuts, after, name):
    shapes = [a.shape if c is None else (c[1],) + a.shape[1:] for a, c in zip(arrays, cuts)]
    total = 2 * sum(math.prod(shape) for shape in shapes)
    copies = sum(1 if c is None else PIECES for c in cuts)
    return pl.pallas_call(
        lambda *refs: fetch_kernel(cuts, *refs),
        in_specs=[HBM] * len(arrays) + [ANY],
        out_specs=[VMEM] * (len(arrays) + 1),
        out_shape=[pltpu.VMEM(shape, a.dtype) for shape, a in zip(shapes, arrays)]
        + [jax.ShapeDtypeStruct((8, LANES), jnp.float32)],
        scratch_shapes=[pltpu.SemaphoreType.DMA((copies,))],
        compiler_params=params(8),
        cost_estimate=pl.CostEstimate(flops=0, bytes_accessed=total, transcendentals=0),
        name=name,
    )(*[far(a) for a in arrays], after)


def far(array):
    return pltpu.with_memory_space_constraint(array, pltpu.HBM)


def here(array):
    return pltpu.with_memory_space_constraint(array, pltpu.VMEM)


def rows_of(ref, order):
    blocks = [ref[d].astype(jnp.float32) for d in order]
    return jnp.concatenate(blocks, axis=0)


def send_blocks(refs, value, cut, rows):
    at = 0
    for ref in refs:
        for k in range(ref.shape[0]):
            ref[k, :, cut] = value[at : at + rows].astype(ref.dtype)
            at += rows


def project_kernel(order, x_ref, w_ref, *out_refs):
    rows, features = out_refs[0].shape[1:]
    me = lax.axis_index("dev")
    inputs = rows_of(x_ref, [me ^ k for k in order]).astype(jnp.bfloat16)
    for start in range(0, features, CHUNK):
        cut = slice(start, start + CHUNK)
        part = jnp.dot(inputs, w_ref[:, cut], preferred_element_type=jnp.float32)
        send_blocks(out_refs, part, cut, rows)


def total_of(refs):
    total = refs[0][...].astype(jnp.float32)
    for ref in refs[1:]:
        total = total + ref[...].astype(jnp.float32)
    return total


def fold_kernel(count, outs, *refs):
    total = total_of(refs[:count])
    at = 0
    for ref in refs[-outs:]:
        ref[...] = total[at : at + ref.shape[0]].astype(ref.dtype)
        at += ref.shape[0]


def fold(parts, outs, idle):
    blocks, rows, features = parts[0].shape
    shape = (blocks // outs, rows, features)
    return pl.pallas_call(
        lambda *refs: fold_kernel(len(parts), outs, *refs),
        in_specs=[VMEM] * len(parts) + [HBM] * len(idle),
        out_specs=[VMEM] * outs,
        out_shape=[jax.ShapeDtypeStruct(shape, jnp.float32)]
        + [jax.ShapeDtypeStruct(shape, jnp.bfloat16)] * (outs - 1),
        compiler_params=params(8),
        name="fold",
    )(*parts, *[far(a) for a in idle])


def norm_kernel(idx_ref, x_ref, gain_ref, router_ref, *refs):
    resid_ref, out_ref = refs[-2:]
    batches, sessions, features = x_ref.shape
    experts = router_ref.shape[0]
    rows = batches * sessions
    x_rows = jnp.concatenate([x_ref[m].astype(jnp.float32) for m in range(batches)], axis=0)
    resid = x_rows + total_of(refs[:-2])[0]
    resid_ref[...] = resid
    mean_square = jnp.mean(resid * resid, axis=1, keepdims=True)
    normed = (resid * lax.rsqrt(mean_square + 1e-05) * gain_ref[...].astype(jnp.float32).reshape(1, features)).astype(
        jnp.bfloat16
    )
    logits = lax.dot_general(
        normed, router_ref[...], (((1,), (1,)), ((), ())), preferred_element_type=jnp.float32
    )
    row = lax.broadcasted_iota(jnp.int32, (rows, experts), 0)
    column = lax.broadcasted_iota(jnp.int32, (rows, experts), 1)
    member = row < 0
    for m in range(batches):
        for s in range(sessions):
            for k in range(idx_ref.shape[2]):
                member = member | ((row == m * sessions + s) & (column == idx_ref[m, s, k]))
    peak = jnp.max(jnp.where(member, logits, -jnp.inf), axis=1, keepdims=True)
    mass = jnp.where(member, jnp.exp(logits - peak), 0.0)
    weights = mass / jnp.sum(mass, axis=1, keepdims=True)
    high = weights.astype(jnp.bfloat16).astype(jnp.float32)
    low = weights - high
    extra = jnp.concatenate(
        [high, low, jnp.zeros((rows, LANES - 2 * experts), jnp.float32)], axis=1
    ).astype(jnp.bfloat16)
    out_ref[0, :, :features] = normed
    out_ref[0, :, features:] = extra


def expert_kernel(expert_count, near_ref, far_ref, gate, up, down, *refs):
    out_refs, hidden = refs[:-1], refs[-1]
    rows, features = out_refs[0].shape[1:]
    units = hidden.shape[1]
    near, other = [[ref[d].astype(jnp.float32) for d in range(ref.shape[0])] for ref in (near_ref, far_ref)]
    blocks = near + other
    order, kept = scatter_order(len(blocks)), gather_order(len(blocks))
    whole = jnp.concatenate([blocks[kept.index(k)] for k in order], axis=0)
    inputs = whole[:, :features].astype(jnp.bfloat16)
    packed = whole[:, features:]
    expert = lax.div(lax.axis_index("dev"), len(blocks) // expert_count)
    lane = lax.broadcasted_iota(jnp.int32, packed.shape, 1)
    mine = (lane % expert_count == expert) & (lane < 2 * expert_count)
    weight = jnp.sum(jnp.where(mine, packed, 0.0), axis=1, keepdims=True)

    def product(weights, cut):
        return jnp.dot(inputs, weights[:, cut], preferred_element_type=jnp.float32)

    for start in range(0, units, CHUNK):
        cut = slice(start, start + CHUNK)
        hidden[:, cut] = (jax.nn.silu(product(gate, cut)) * product(up, cut)).astype(jnp.bfloat16)
    for start in range(0, features, CHUNK):
        cut = slice(start, start + CHUNK)
        part = jnp.dot(hidden[...], down[:, cut], preferred_element_type=jnp.float32)
        send_blocks(out_refs, part * weight, cut, rows)


def stages_of(devices):
    stages, bit = [], 2
    while bit < devices:
        if bit > 2 and 2 * bit < devices:
            stages.append((bit, 2 * bit, 3 * bit))
            bit *= 4
        else:
            stages.append((bit,))
            bit *= 2
    return stages


def gather_order(devices):
    order = [0]
    for masks in stages_of(devices):
        order = order + [mask ^ k for mask in masks for k in order]
    return order + [1 ^ k for k in order]


def scatter_order(devices):
    order = [0]
    for masks in reversed([(1,)] + stages_of(devices)):
        order = order + [mask ^ k for mask in masks for k in order]
    return order


def hop(blocks, mask):
    devices = lax.axis_size("dev")
    return lax.ppermute(blocks, "dev", [(i, i ^ mask) for i in range(devices)])


def gather(block, idle):
    for masks in stages_of(lax.axis_size("dev")):
        block = join([block] + [hop(block, mask) for mask in masks], idle)
    return block, hop(block, 1)


def join_kernel(count, *refs):
    size = refs[0].shape[0]
    for k in range(count):
        refs[-1][k * size : (k + 1) * size] = refs[k][...]


def join(parts, idle):
    shape = (len(parts) * parts[0].shape[0],) + parts[0].shape[1:]
    return pl.pallas_call(
        lambda *refs: join_kernel(len(parts), *refs),
        in_specs=[VMEM] * len(parts) + [HBM] * len(idle),
        out_specs=VMEM,
        out_shape=jax.ShapeDtypeStruct(shape, parts[0].dtype),
        compiler_params=params(8),
        name="join",
    )(*parts, *[far(a) for a in idle])


def scatter(keep, sends, idle):
    stages = [(1,)] + stages_of(lax.axis_size("dev"))
    for step, masks in enumerate(stages):
        parts = [keep] + [hop(block, mask) for block, mask in zip(sends, masks)]
        if step + 1 < len(stages):
            keep, *sends = fold(parts, len(stages[step + 1]) + 1, idle)
    return parts


def final_kernel(*refs):
    resid_ref, out_ref = refs[0], refs[-1]
    batches, sessions, _ = out_ref.shape
    mixed = resid_ref[...] + total_of(refs[1:-1])[0]
    for m in range(batches):
        out_ref[m] = mixed[m * sessions : (m + 1) * sessions].astype(jnp.bfloat16)


def exchange(blocks):
    return lax.all_to_all(blocks, "dev", split_axis=0, concat_axis=0, tiled=True)


def local(
    x_in,
    queries,
    cache_keys,
    cache_values,
    new_keys,
    new_values,
    lengths,
    w_out,
    norm_gain,
    w_router,
    experts_idx,
    w_gate,
    w_up,
    w_down,
):
    devices = lax.axis_size("dev")
    expert_count = w_router.shape[1]
    batches, sessions, features = x_in.shape
    rows = batches * sessions
    units = w_gate.shape[1]

    def blocks(width):
        return jax.ShapeDtypeStruct((devices, rows, width), jnp.bfloat16)

    operands = [queries, cache_keys, cache_values, new_keys, new_values]
    heads = pl.pallas_call(
        attend_kernel,
        in_specs=[SMEM] + [HBM] * 5,
        out_specs=VMEM,
        out_shape=blocks(w_out.shape[0]),
        scratch_shapes=[pltpu.VMEM(a.shape, a.dtype) for a in operands]
        + [pltpu.SemaphoreType.DMA((len(operands),))],
        compiler_params=params(8),
        name="attend",
    )(lengths, *[pltpu.with_memory_space_constraint(a, pltpu.HBM) for a in operands])
    head_blocks = exchange(heads)
    (out_here, _) = fetch([w_out], [None], heads, "fetch_out")
    halves = [jax.ShapeDtypeStruct((devices // 2, rows, features), t) for t in (jnp.float32, jnp.bfloat16)]
    keep, send = pl.pallas_call(
        lambda *refs: project_kernel(scatter_order(devices), *refs),
        in_specs=[VMEM] * 2,
        out_specs=[VMEM] * 2,
        out_shape=halves,
        compiler_params=params(8),
        name="project",
    )(head_blocks, here(out_here))
    attn_parts = scatter(keep, [send], [w_gate])
    resid, message = pl.pallas_call(
        norm_kernel,
        in_specs=[SMEM] + [VMEM] * (3 + len(attn_parts)),
        out_specs=(VMEM, VMEM),
        out_shape=(
            pltpu.VMEM((rows, features), jnp.float32),
            jax.ShapeDtypeStruct((1, rows, features + LANES), jnp.bfloat16),
        ),
        compiler_params=params(8),
        name="norm",
    )(experts_idx, here(x_in), norm_gain, jnp.transpose(w_router), *attn_parts)
    near, other = gather(message, [w_gate])
    keep, send = pl.pallas_call(
        lambda *refs: expert_kernel(expert_count, *refs),
        in_specs=[VMEM] * 5,
        out_specs=[VMEM] * 2,
        out_shape=halves,
        scratch_shapes=[
            pltpu.VMEM((devices * rows, units), jnp.bfloat16),
        ],
        compiler_params=params(8),
        name="experts",
    )(near, other, here(w_gate), here(w_up), here(w_down))
    parts = scatter(keep, [send], [])
    return pl.pallas_call(
        final_kernel,
        in_specs=[VMEM] * (1 + len(parts)),
        out_specs=VMEM,
        out_shape=jax.ShapeDtypeStruct(x_in.shape, jnp.bfloat16),
        compiler_params=params(8),
        name="final",
    )(resid, *parts)


def solution(mesh):
    return jax.shard_map(
        local,
        mesh=mesh,
        in_specs=(
            P(None, ("groups", "dev"), None),
            P(None, ("groups", "dev"), None),
            P(None, ("groups", "dev"), None, None),
            P(None, ("groups", "dev"), None, None),
            P(None, ("groups", "dev"), None),
            P(None, ("groups", "dev"), None),
            P(None, ("groups", "dev")),
            P("dev", None),
            P(),
            P(),
            P(None, ("groups", "dev"), None),
            P(None, "dev"),
            P(None, "dev"),
            P("dev", None),
        ),
        out_specs=P(None, ("groups", "dev"), None),
        check_vma=False,
    )
```

time: 96 us -> 69.5 us (0.72)
  blocking collectives: 29.4 us -> 0 us
  local copies, waits for them, and re-layouts: 23.1 us -> 0.74 us
  starting transfers between devices: 7.11 us -> 22.5 us
  waiting for transfers between devices: 22.7 us -> 30.8 us
  Pallas kernels: 12.7 us -> 14.9 us
    all_to_all x2 -> x0, blocking collectives: 29.4 us -> none  [exchange(): lax.all_to_all(blocks, 'dev', split_axis=0, concat_axis=0, tiled=True)]
    ppermute x0 -> x15, waiting for transfers between devices: none -> 26.1 us  [hop(): return lax.ppermute(blocks, 'dev', [(i, i ^ mask) for i in range(devices)])]
    unnamed x25 -> x28, local copies, waits for them, and re-layouts: 22.4 us -> 0.74 us
    all_to_all x2 -> x1, waiting for transfers between devices: 22.7 us -> 4.75 us  [exchange(): lax.all_to_all(blocks, 'dev', split_axis=0, concat_axis=0, tiled=True)]
    ppermute x0 -> x15, starting transfers between devices: none -> 15.1 us  [hop(): return lax.ppermute(blocks, 'dev', [(i, i ^ mask) for i in range(devices)])]
    pallas_call x4 -> x11, Pallas kernels: 5.94 us -> 8.24 us  [the longest x1 4.09 us: local(): pl.pallas_call(attend_kernel, in_specs=[SMEM] + [HBM] * 5, out_specs=VMEM...]
    all_to_all x2 -> x1, starting transfers between devices: 7.11 us -> 7.4 us  [exchange(): lax.all_to_all(blocks, 'dev', split_axis=0, concat_axis=0, tiled=True)]
  transfers between devices with their start and end apart: 2 -> 16, of which waited for: 2 -> 13; matrix products, arithmetic and copies ran while one was open for 2% -> 0% of each run, Pallas kernels for 0% -> 3%
where the time goes in v3:
time: 69.5 us; the launch traced here: 69.2 us
  waiting for transfers between devices  30.8 us (44%)
  starting transfers between devices  22.5 us (32%)
  Pallas kernels  14.9 us (21%)
  local copies, waits for them, and re-layouts  0.74 us (1%)
    ppermute x15, waiting for transfers between devices, hop(): return lax.ppermute(blocks, 'dev', [(i, i ^ mask) for i in range(devices)])  26.1 us
    ppermute x15, starting transfers between devices, hop(): return lax.ppermute(blocks, 'dev', [(i, i ^ mask) for i in range(devices)])  15.1 us
    all_to_all x1, starting transfers between devices, exchange(): lax.all_to_all(blocks, 'dev', split_axis=0, concat_axis=0, tiled=True)  7.4 us
    pallas_call x1, Pallas kernels, local(): pl.pallas_call(lambda *refs: expert_kernel(expert_count, *refs), in_specs...  6.68 us
    all_to_all x1, waiting for transfers between devices, exchange(): lax.all_to_all(blocks, 'dev', split_axis=0, concat_axis=0, tiled=True)  4.75 us
    pallas_call x1, Pallas kernels, local(): pl.pallas_call(attend_kernel, in_specs=[SMEM] + [HBM] * 5, out_specs=VMEM...  4.09 us
    pallas_call x1, Pallas kernels, fetch(): pl.pallas_call(lambda *refs: fetch_kernel(cuts, *refs), in_specs=[HBM] *...  1.87 us
  transfers between devices with their start and end apart: 16, of which 13 were waited for; matrix products, arithmetic and copies ran while one was open for 0% of the time, Pallas kernels for 3%

profile of v3, /device:TPU:0, one launch (start us, length us, event | category | flops | bytes accessed | tf_op | source)
XLA Modules:
  0.0 69.2 jit_solution(4672035576598363892)
XLA Ops:
  0.0 0.7 copy-done.4
  0.7 4.1 %attend.1.refs_1_ = bf16[16,4,192]{2,1,0:T(4,128)(2,1)} custom-call(s32[2,2]{1,0:T(2,128)S(1)} %copy-done.4, bf16[2,2,3072]{2,1,0:T(2,128)(2,1)} %refs_0_.2, bf16[2,2,128,512]{3,2,1,0:T(8,128)(2,1)} %refs_1_.1, bf16[2,2,128,512]{3,2,1,0:T(8,128)(2,1)} %refs_2_.5, bf16[2,2,512]{2,1,0:T(2,128)(2,1)} %refs_3_.2, bf16[2,2,512]{2,1,0:T(2,128)(2,1)} %refs_4_.3), custom_call_target="tpu_custom_call" | custom-call | tf_op jit(solution)/shard_map/attend/pallas_call | solution.py:354
  4.8 7.4 %all-to-all-start = ((bf16[16,4,192]{2,1,0:T(4,128)(2,1)}), bf16[16,4,192]{2,1,0:T(4,128)(2,1)S(1)}, u32[]{:S(2)}, u32[]{:S(2)}) async-start(bf16[16,4,192]{2,1,0:T(4,128)(2,1)} %attend.1.refs_1_), calls=%async_computation | async-start | bytes 65536 | tf_op jit(solution)/shard_map/all_to_all | solution.py:325
  12.2 1.9 %fetch_out.1 = (bf16[192,3072]{1,0:T(8,128)(2,1)S(1)}, f32[8,128]{1,0:T(8,128)}) custom-call(bf16[192,3072]{1,0:T(8,128)(2,1)} %refs_0_.3, bf16[16,4,192]{2,1,0:T(4,128)(2,1)} %attend.1.refs_1_), custom_call_target="tpu_custom_call" | custom-call | bytes 1179648 | tf_op jit(solution)/shard_map/fetch_out/pallas_call | solution.py:118
  14.1 4.8 %all-to-all-done.refs_0_ = bf16[16,4,192]{2,1,0:T(4,128)(2,1)S(1)} async-done(((bf16[16,4,192]{2,1,0:T(4,128)(2,1)}), bf16[16,4,192]{2,1,0:T(4,128)(2,1)S(1)}, u32[]{:S(2)}, u32[]{:S(2)}) %all-to-all-start) | async-done | bytes 24608 | tf_op jit(solution)/shard_map/all_to_all | solution.py:325
  18.8 0.3 project.1
  19.2 0.1 collective-permute-start
  19.2 1.4 %collective-permute-done.refs_1_ = bf16[8,4,3072]{2,1,0:T(4,128)(2,1)S(1)} collective-permute-done((bf16[8,4,3072]{2,1,0:T(4,128)(2,1)S(1)}, bf16[8,4,3072]{2,1,0:T(4,128)(2,1)S(1)}, u32[]{:S(2)}, u32[]{:S(2)}) %collective-permute-start) | collective-permute-done | bytes 196640 | tf_op jit(solution)/shard_map/ppermute | solution.py:280
  20.7 0.0 slice-start.3
  20.7 0.0 slice-start.6
  20.7 0.1 fold.4
  20.8 0.4 collective-permute-start.1
  21.2 4.5 %collective-permute-done.1.refs_1_ = bf16[4,4,3072]{2,1,0:T(4,128)(2,1)S(1)} collective-permute-done((bf16[4,4,3072]{2,1,0:T(4,128)(2,1)S(1)}, bf16[4,4,3072]{2,1,0:T(4,128)(2,1)S(1)}, u32[]{:S(2)}, u32[]{:S(2)}) %collective-permute-start.1) | collective-permute-done | bytes 98336 | tf_op jit(solution)/shard_map/ppermute | solution.py:280
  25.7 0.4 collective-permute-start.2
  26.1 0.7 %collective-permute-start.3 = (bf16[1,4,3072]{2,1,0:T(4,128)(2,1)S(1)}, bf16[1,4,3072]{2,1,0:T(4,128)(2,1)S(1)}, u32[]{:S(2)}, u32[]{:S(2)}) collective-permute-start(bf16[1,4,3072]{2,1,0:T(4,128)(2,1)S(1)} %get-tuple-element.31), channel_id=1, source_target_pairs={{0,8},{1,9},{2,10},{3,11},{4,12},{5,13},{6,14},{7,15},{8,0},{9,1},... | collective-permute-start | bytes 73736 | tf_op jit(solution)/shard_map/ppermute | solution.py:280
  26.8 3.4 %collective-permute-start.4 = (bf16[1,4,3072]{2,1,0:T(4,128)(2,1)S(1)}, bf16[1,4,3072]{2,1,0:T(4,128)(2,1)S(1)}, u32[]{:S(2)}, u32[]{:S(2)}) collective-permute-start(bf16[1,4,3072]{2,1,0:T(4,128)(2,1)S(1)} %get-tuple-element.32), channel_id=1, source_target_pairs={{0,12},{1,13},{2,14},{3,15},{4,8},{5,9},{6,10},{7,11},{8,4},{9,5},... | collective-permute-start | bytes 73736 | tf_op jit(solution)/shard_map/ppermute | solution.py:280
  30.2 0.0 collective-permute-done.2.refs_1_
  30.2 0.7 collective-permute-done.3.refs_2_
  30.9 1.6 %collective-permute-done.4.refs_3_ = bf16[1,4,3072]{2,1,0:T(4,128)(2,1)S(1)} collective-permute-done((bf16[1,4,3072]{2,1,0:T(4,128)(2,1)S(1)}, bf16[1,4,3072]{2,1,0:T(4,128)(2,1)S(1)}, u32[]{:S(2)}, u32[]{:S(2)}) %collective-permute-start.4) | collective-permute-done | bytes 24608 | tf_op jit(solution)/shard_map/ppermute | solution.py:280
  32.4 0.0 copy-done
  32.4 0.0 copy-done.1
  32.4 0.0 copy-done.2
  32.5 0.0 copy-done.3
  32.5 1.1 %norm.1 = (f32[4,3072]{1,0:T(4,128)S(1)}, bf16[1,4,3200]{2,1,0:T(4,128)(2,1)S(1)}) custom-call(s32[2,2,2]{2,1,0:T(2,128)S(1)} %copy-done.3, bf16[2,2,3072]{2,1,0:T(2,128)(2,1)S(1)} %copy-done, bf16[3072]{0:T(1024)(128)(2,1)S(1)} %copy-done.2, bf16[4,3072]{1,0:T(4,128)(2,1)S(1)} %bitcast.7, f32[1,4,3072]{2,1,0:T(4,128)S(1)} %get-tuple-element.29.refs_0_, ...), custom_call_target="tpu_custom_call" | custom-call | tf_op jit(solution)/shard_map/norm/pallas_call | solution.py:376
  33.6 0.0 slice-start.8
  33.6 0.6 collective-permute-start.5
  34.2 3.3 %collective-permute-done.5.refs_1_ = bf16[1,4,3200]{2,1,0:T(4,128)(2,1)S(1)} collective-permute-done((bf16[1,4,3200]{2,1,0:T(4,128)(2,1)S(1)}, bf16[1,4,3200]{2,1,0:T(4,128)(2,1)S(1)}, u32[]{:S(2)}, u32[]{:S(2)}) %collective-permute-start.5) | collective-permute-done | bytes 25632 | tf_op jit(solution)/shard_map/ppermute | solution.py:280
  37.5 3.4 %collective-permute-start.8 = (bf16[2,4,3200]{2,1,0:T(4,128)(2,1)S(1)}, bf16[2,4,3200]{2,1,0:T(4,128)(2,1)S(1)}, u32[]{:S(2)}, u32[]{:S(2)}) collective-permute-start(bf16[2,4,3200]{2,1,0:T(4,128)(2,1)S(1)} %join.2.refs_0_), channel_id=1, source_target_pairs={{0,12},{1,13},{2,14},{3,15},{4,8},{5,9},{6,10},{7,11},{8,4},{9,5},... | collective-permute-start | bytes 153608 | tf_op jit(solution)/shard_map/ppermute | solution.py:280
  40.9 0.0 collective-permute-start.7
  40.9 1.0 %collective-permute-start.6 = (bf16[2,4,3200]{2,1,0:T(4,128)(2,1)S(1)}, bf16[2,4,3200]{2,1,0:T(4,128)(2,1)S(1)}, u32[]{:S(2)}, u32[]{:S(2)}) collective-permute-start(bf16[2,4,3200]{2,1,0:T(4,128)(2,1)S(1)} %join.2.refs_0_), channel_id=1, source_target_pairs={{0,4},{1,5},{2,6},{3,7},{4,0},{5,1},{6,2},{7,3},{8,12},{9,13},{10,... | collective-permute-start | bytes 153608 | tf_op jit(solution)/shard_map/ppermute | solution.py:280
  41.9 1.5 %collective-permute-done.8.refs_3_ = bf16[2,4,3200]{2,1,0:T(4,128)(2,1)S(1)} collective-permute-done((bf16[2,4,3200]{2,1,0:T(4,128)(2,1)S(1)}, bf16[2,4,3200]{2,1,0:T(4,128)(2,1)S(1)}, u32[]{:S(2)}, u32[]{:S(2)}) %collective-permute-start.8) | collective-permute-done | bytes 51232 | tf_op jit(solution)/shard_map/ppermute | solution.py:280
  43.5 2.5 %collective-permute-done.7.refs_2_ = bf16[2,4,3200]{2,1,0:T(4,128)(2,1)S(1)} collective-permute-done((bf16[2,4,3200]{2,1,0:T(4,128)(2,1)S(1)}, bf16[2,4,3200]{2,1,0:T(4,128)(2,1)S(1)}, u32[]{:S(2)}, u32[]{:S(2)}) %collective-permute-start.7) | collective-permute-done | bytes 51232 | tf_op jit(solution)/shard_map/ppermute | solution.py:280
  45.9 0.0 collective-permute-done.6.refs_1_
  45.9 0.1 collective-permute-start.9
  46.0 1.4 %collective-permute-done.9.refs_1_ = bf16[8,4,3200]{2,1,0:T(4,128)(2,1)S(1)} collective-permute-done((bf16[8,4,3200]{2,1,0:T(4,128)(2,1)S(1)}, bf16[8,4,3200]{2,1,0:T(4,128)(2,1)S(1)}, u32[]{:S(2)}, u32[]{:S(2)}) %collective-permute-start.9) | collective-permute-done | bytes 204832 | tf_op jit(solution)/shard_map/ppermute | solution.py:280
  47.6 6.7 %experts.1 = (f32[8,4,3072]{2,1,0:T(4,128)S(1)}, bf16[8,4,3072]{2,1,0:T(4,128)(2,1)S(1)}) custom-call(bf16[8,4,3200]{2,1,0:T(4,128)(2,1)S(1)} %join.3.refs_0_, bf16[8,4,3200]{2,1,0:T(4,128)(2,1)S(1)} %collective-permute-done.9.refs_1_, bf16[3072,2048]{1,0:T(8,128)(2,1)S(1)} %bitcast.2, bf16[3072,2048]{1,0:T(8,128)(2,1)S(1)} %bitcast.4, ...), custom_call_target="tpu_custom_call" | custom-call | tf_op jit(solution)/shard_map/experts/pallas_call | solution.py:388
  54.2 0.2 collective-permute-start.10
  54.4 1.3 %collective-permute-done.10.refs_1_ = bf16[8,4,3072]{2,1,0:T(4,128)(2,1)S(1)} collective-permute-done((bf16[8,4,3072]{2,1,0:T(4,128)(2,1)S(1)}, bf16[8,4,3072]{2,1,0:T(4,128)(2,1)S(1)}, u32[]{:S(2)}, u32[]{:S(2)}) %collective-permute-start.10) | collective-permute-done | bytes 196640 | tf_op jit(solution)/shard_map/ppermute | solution.py:280
  55.8 0.1 fold.6
  55.8 0.4 collective-permute-start.11
  56.2 4.5 %collective-permute-done.11.refs_1_ = bf16[4,4,3072]{2,1,0:T(4,128)(2,1)S(1)} collective-permute-done((bf16[4,4,3072]{2,1,0:T(4,128)(2,1)S(1)}, bf16[4,4,3072]{2,1,0:T(4,128)(2,1)S(1)}, u32[]{:S(2)}, u32[]{:S(2)}) %collective-permute-start.11) | collective-permute-done | bytes 98336 | tf_op jit(solution)/shard_map/ppermute | solution.py:280
  60.8 0.3 collective-permute-start.12
  61.1 1.9 %collective-permute-start.13 = (bf16[1,4,3072]{2,1,0:T(4,128)(2,1)S(1)}, bf16[1,4,3072]{2,1,0:T(4,128)(2,1)S(1)}, u32[]{:S(2)}, u32[]{:S(2)}) collective-permute-start(bf16[1,4,3072]{2,1,0:T(4,128)(2,1)S(1)} %get-tuple-element.41), channel_id=1, source_target_pairs={{0,8},{1,9},{2,10},{3,11},{4,12},{5,13},{6,14},{7,15},{8,0},{9,1},... | collective-permute-start | bytes 73736 | tf_op jit(solution)/shard_map/ppermute | solution.py:280
  63.0 2.3 %collective-permute-start.14 = (bf16[1,4,3072]{2,1,0:T(4,128)(2,1)S(1)}, bf16[1,4,3072]{2,1,0:T(4,128)(2,1)S(1)}, u32[]{:S(2)}, u32[]{:S(2)}) collective-permute-start(bf16[1,4,3072]{2,1,0:T(4,128)(2,1)S(1)} %get-tuple-element.42), channel_id=1, source_target_pairs={{0,12},{1,13},{2,14},{3,15},{4,8},{5,9},{6,10},{7,11},{8,4},{9,5},... | collective-permute-start | bytes 73736 | tf_op jit(solution)/shard_map/ppermute | solution.py:280
  65.2 0.0 collective-permute-done.12.refs_2_
  65.2 0.7 %collective-permute-done.13.refs_3_ = bf16[1,4,3072]{2,1,0:T(4,128)(2,1)S(1)} collective-permute-done((bf16[1,4,3072]{2,1,0:T(4,128)(2,1)S(1)}, bf16[1,4,3072]{2,1,0:T(4,128)(2,1)S(1)}, u32[]{:S(2)}, u32[]{:S(2)}) %collective-permute-start.13) | collective-permute-done | bytes 24608 | tf_op jit(solution)/shard_map/ppermute | solution.py:280
  65.9 2.7 %collective-permute-done.14.refs_4_ = bf16[1,4,3072]{2,1,0:T(4,128)(2,1)S(1)} collective-permute-done((bf16[1,4,3072]{2,1,0:T(4,128)(2,1)S(1)}, bf16[1,4,3072]{2,1,0:T(4,128)(2,1)S(1)}, u32[]{:S(2)}, u32[]{:S(2)}) %collective-permute-start.14) | collective-permute-done | bytes 24608 | tf_op jit(solution)/shard_map/ppermute | solution.py:280
  68.6 0.6 final.1
  (27 shorter events, 0.1 us)
Async XLA Ops:
  0.0 0.7 copy-start.4
  4.8 14.0 %all-to-all-start = ((bf16[16,4,192]{2,1,0:T(4,128)(2,1)}), bf16[16,4,192]{2,1,0:T(4,128)(2,1)S(1)}, u32[]{:S(2)}, u32[]{:S(2)}) async-start(bf16[16,4,192]{2,1,0:T(4,128)(2,1)} %attend.1.refs_1_), calls=%async_computation | async-start | bytes 65536 | tf_op jit(solution)/shard_map/all_to_all | solution.py:325
  19.2 1.5 %collective-permute-start = (bf16[8,4,3072]{2,1,0:T(4,128)(2,1)S(1)}, bf16[8,4,3072]{2,1,0:T(4,128)(2,1)S(1)}, u32[]{:S(2)}, u32[]{:S(2)}) collective-permute-start(bf16[8,4,3072]{2,1,0:T(4,128)(2,1)S(1)} %get-tuple-element.26), channel_id=1, source_target_pairs={{0,1},{1,0},{2,3},{3,2},{4,5},{5,4},{6,7},{7,6},{8,9},{9,8},{10,11... | collective-permute-start | bytes 589832 | tf_op jit(solution)/shard_map/ppermute | solution.py:280
  20.7 11.8 %copy-start = (bf16[2,2,3072]{2,1,0:T(2,128)(2,1)S(1)}, bf16[2,2,3072]{2,1,0:T(2,128)(2,1)}, u32[]{:S(2)}) copy-start(bf16[2,2,3072]{2,1,0:T(2,128)(2,1)} %x_ref.1) | copy-start | bytes 73732
  20.7 11.8 %copy-start.1 = (bf16[3072,4]{0,1:T(4,128)(2,1)S(1)}, bf16[3072,4]{0,1:T(4,128)(2,1)}, u32[]{:S(2)}) copy-start(bf16[3072,4]{0,1:T(4,128)(2,1)} %param.23) | copy-start | bytes 73732
  20.7 11.8 %copy-start.2 = (bf16[3072]{0:T(1024)(128)(2,1)S(1)}, bf16[3072]{0:T(1024)(128)(2,1)}, u32[]{:S(2)}) copy-start(bf16[3072]{0:T(1024)(128)(2,1)} %gain_ref.1) | copy-start | bytes 18436
  20.7 11.8 %copy-start.3 = (s32[2,2,2]{2,1,0:T(2,128)S(1)}, s32[2,2,2]{2,1,0:T(2,128)}, u32[]{:S(2)}) copy-start(s32[2,2,2]{2,1,0:T(2,128)} %idx_ref.1) | copy-start | bytes 100
  20.7 26.8 %slice-start.3 = ((s8[12582912]{0:T(1024)(128)(4,1)}), s8[4194304]{0:T(1024)(128)(4,1)S(1)}, s32[]{:S(2)}) async-start(s8[12582912]{0:T(1024)(128)(4,1)} %bitcast.3), calls=%async_computation.4 | async-start | bytes 8388608
  20.7 26.8 %slice-start.6 = ((s8[12582912]{0:T(1024)(128)(4,1)}), s8[4194304]{0:T(1024)(128)(4,1)S(1)}, s32[]{:S(2)}) async-start(s8[12582912]{0:T(1024)(128)(4,1)} %bitcast.5), calls=%async_computation.7 | async-start | bytes 8388608
  20.8 4.9 %collective-permute-start.1 = (bf16[4,4,3072]{2,1,0:T(4,128)(2,1)S(1)}, bf16[4,4,3072]{2,1,0:T(4,128)(2,1)S(1)}, u32[]{:S(2)}, u32[]{:S(2)}) collective-permute-start(bf16[4,4,3072]{2,1,0:T(4,128)(2,1)S(1)} %get-tuple-element.28), channel_id=1, source_target_pairs={{0,2},{1,3},{2,0},{3,1},{4,6},{5,7},{6,4},{7,5},{8,10},{9,11},{10,... | collective-permute-start | bytes 294920 | tf_op jit(solution)/shard_map/ppermute | solution.py:280
  25.7 21.8 %slice-start.4 = ((s8[12582912]{0:T(1024)(128)(4,1)}), s8[4194304]{0:T(1024)(128)(4,1)S(1)}, s32[]{:S(2)}) async-start(s8[12582912]{0:T(1024)(128)(4,1)} %bitcast.3), calls=%async_computation.5 | async-start | bytes 8388608
  25.7 21.8 %slice-start.7 = ((s8[12582912]{0:T(1024)(128)(4,1)}), s8[4194304]{0:T(1024)(128)(4,1)S(1)}, s32[]{:S(2)}) async-start(s8[12582912]{0:T(1024)(128)(4,1)} %bitcast.5), calls=%async_computation.8 | async-start | bytes 8388608
  25.7 4.5 %collective-permute-start.2 = (bf16[1,4,3072]{2,1,0:T(4,128)(2,1)S(1)}, bf16[1,4,3072]{2,1,0:T(4,128)(2,1)S(1)}, u32[]{:S(2)}, u32[]{:S(2)}) collective-permute-start(bf16[1,4,3072]{2,1,0:T(4,128)(2,1)S(1)} %get-tuple-element.30), channel_id=1, source_target_pairs={{0,4},{1,5},{2,6},{3,7},{4,0},{5,1},{6,2},{7,3},{8,12},{9,13},{10,... | collective-permute-start | bytes 73736 | tf_op jit(solution)/shard_map/ppermute | solution.py:280
  26.1 4.7 %collective-permute-start.3 = (bf16[1,4,3072]{2,1,0:T(4,128)(2,1)S(1)}, bf16[1,4,3072]{2,1,0:T(4,128)(2,1)S(1)}, u32[]{:S(2)}, u32[]{:S(2)}) collective-permute-start(bf16[1,4,3072]{2,1,0:T(4,128)(2,1)S(1)} %get-tuple-element.31), channel_id=1, source_target_pairs={{0,8},{1,9},{2,10},{3,11},{4,12},{5,13},{6,14},{7,15},{8,0},{9,1},... | collective-permute-start | bytes 73736 | tf_op jit(solution)/shard_map/ppermute | solution.py:280
  26.8 5.6 %collective-permute-start.4 = (bf16[1,4,3072]{2,1,0:T(4,128)(2,1)S(1)}, bf16[1,4,3072]{2,1,0:T(4,128)(2,1)S(1)}, u32[]{:S(2)}, u32[]{:S(2)}) collective-permute-start(bf16[1,4,3072]{2,1,0:T(4,128)(2,1)S(1)} %get-tuple-element.32), channel_id=1, source_target_pairs={{0,12},{1,13},{2,14},{3,15},{4,8},{5,9},{6,10},{7,11},{8,4},{9,5},... | collective-permute-start | bytes 73736 | tf_op jit(solution)/shard_map/ppermute | solution.py:280
  33.5 13.9 %slice-start = ((s8[12582912]{0:T(1024)(128)(4,1)}), s8[4194304]{0:T(1024)(128)(4,1)S(1)}, s32[]{:S(2)}) async-start(s8[12582912]{0:T(1024)(128)(4,1)} %bitcast.1), calls=%async_computation.1 | async-start | bytes 8388608
  33.6 13.9 %slice-start.1 = ((s8[12582912]{0:T(1024)(128)(4,1)}), s8[4194304]{0:T(1024)(128)(4,1)S(1)}, s32[]{:S(2)}) async-start(s8[12582912]{0:T(1024)(128)(4,1)} %bitcast.1), calls=%async_computation.2 | async-start | bytes 8388608
  33.6 14.0 %slice-start.5 = ((s8[12582912]{0:T(1024)(128)(4,1)}), s8[4194304]{0:T(1024)(128)(4,1)S(1)}, s32[]{:S(2)}) async-start(s8[12582912]{0:T(1024)(128)(4,1)} %bitcast.3), calls=%async_computation.6 | async-start | bytes 8388608
  33.6 13.9 %slice-start.8 = ((s8[12582912]{0:T(1024)(128)(4,1)}), s8[4194304]{0:T(1024)(128)(4,1)S(1)}, s32[]{:S(2)}) async-start(s8[12582912]{0:T(1024)(128)(4,1)} %bitcast.5), calls=%async_computation.9 | async-start | bytes 8388608
  33.6 3.9 %collective-permute-start.5 = (bf16[1,4,3200]{2,1,0:T(4,128)(2,1)S(1)}, bf16[1,4,3200]{2,1,0:T(4,128)(2,1)S(1)}, u32[]{:S(2)}, u32[]{:S(2)}) collective-permute-start(bf16[1,4,3200]{2,1,0:T(4,128)(2,1)S(1)} %get-tuple-element.34.refs_0_), channel_id=1, source_target_pairs={{0,2},{1,3},{2,0},{3,1},{4,6},{5,7},{6,4},{7,5},{8,10},{9,11},{10,... | collective-permute-start | bytes 76808 | tf_op jit(solution)/shard_map/ppermute | solution.py:280
  37.5 10.0 %slice-start.2 = ((s8[12582912]{0:T(1024)(128)(4,1)}), s8[4194304]{0:T(1024)(128)(4,1)S(1)}, s32[]{:S(2)}) async-start(s8[12582912]{0:T(1024)(128)(4,1)} %bitcast.1), calls=%async_computation.3 | async-start | bytes 8388608
  37.5 6.0 %collective-permute-start.8 = (bf16[2,4,3200]{2,1,0:T(4,128)(2,1)S(1)}, bf16[2,4,3200]{2,1,0:T(4,128)(2,1)S(1)}, u32[]{:S(2)}, u32[]{:S(2)}) collective-permute-start(bf16[2,4,3200]{2,1,0:T(4,128)(2,1)S(1)} %join.2.refs_0_), channel_id=1, source_target_pairs={{0,12},{1,13},{2,14},{3,15},{4,8},{5,9},{6,10},{7,11},{8,4},{9,5},... | collective-permute-start | bytes 153608 | tf_op jit(solution)/shard_map/ppermute | solution.py:280
  40.9 5.0 %collective-permute-start.7 = (bf16[2,4,3200]{2,1,0:T(4,128)(2,1)S(1)}, bf16[2,4,3200]{2,1,0:T(4,128)(2,1)S(1)}, u32[]{:S(2)}, u32[]{:S(2)}) collective-permute-start(bf16[2,4,3200]{2,1,0:T(4,128)(2,1)S(1)} %join.2.refs_0_), channel_id=1, source_target_pairs={{0,8},{1,9},{2,10},{3,11},{4,12},{5,13},{6,14},{7,15},{8,0},{9,1},... | collective-permute-start | bytes 153608 | tf_op jit(solution)/shard_map/ppermute | solution.py:280
  40.9 5.0 %collective-permute-start.6 = (bf16[2,4,3200]{2,1,0:T(4,128)(2,1)S(1)}, bf16[2,4,3200]{2,1,0:T(4,128)(2,1)S(1)}, u32[]{:S(2)}, u32[]{:S(2)}) collective-permute-start(bf16[2,4,3200]{2,1,0:T(4,128)(2,1)S(1)} %join.2.refs_0_), channel_id=1, source_target_pairs={{0,4},{1,5},{2,6},{3,7},{4,0},{5,1},{6,2},{7,3},{8,12},{9,13},{10,... | collective-permute-start | bytes 153608 | tf_op jit(solution)/shard_map/ppermute | solution.py:280
  45.9 1.5 %collective-permute-start.9 = (bf16[8,4,3200]{2,1,0:T(4,128)(2,1)S(1)}, bf16[8,4,3200]{2,1,0:T(4,128)(2,1)S(1)}, u32[]{:S(2)}, u32[]{:S(2)}) collective-permute-start(bf16[8,4,3200]{2,1,0:T(4,128)(2,1)S(1)} %join.3.refs_0_), channel_id=1, source_target_pairs={{0,1},{1,0},{2,3},{3,2},{4,5},{5,4},{6,7},{7,6},{8,9},{9,8},{10,11... | collective-permute-start | bytes 614408 | tf_op jit(solution)/shard_map/ppermute | solution.py:280
  54.2 1.5 %collective-permute-start.10 = (bf16[8,4,3072]{2,1,0:T(4,128)(2,1)S(1)}, bf16[8,4,3072]{2,1,0:T(4,128)(2,1)S(1)}, u32[]{:S(2)}, u32[]{:S(2)}) collective-permute-start(bf16[8,4,3072]{2,1,0:T(4,128)(2,1)S(1)} %get-tuple-element.36), channel_id=1, source_target_pairs={{0,1},{1,0},{2,3},{3,2},{4,5},{5,4},{6,7},{7,6},{8,9},{9,8},{10,11... | collective-permute-start | bytes 589832 | tf_op jit(solution)/shard_map/ppermute | solution.py:280
  55.8 4.9 %collective-permute-start.11 = (bf16[4,4,3072]{2,1,0:T(4,128)(2,1)S(1)}, bf16[4,4,3072]{2,1,0:T(4,128)(2,1)S(1)}, u32[]{:S(2)}, u32[]{:S(2)}) collective-permute-start(bf16[4,4,3072]{2,1,0:T(4,128)(2,1)S(1)} %get-tuple-element.38), channel_id=1, source_target_pairs={{0,2},{1,3},{2,0},{3,1},{4,6},{5,7},{6,4},{7,5},{8,10},{9,11},{10,... | collective-permute-start | bytes 294920 | tf_op jit(solution)/shard_map/ppermute | solution.py:280
  60.8 4.5 %collective-permute-start.12 = (bf16[1,4,3072]{2,1,0:T(4,128)(2,1)S(1)}, bf16[1,4,3072]{2,1,0:T(4,128)(2,1)S(1)}, u32[]{:S(2)}, u32[]{:S(2)}) collective-permute-start(bf16[1,4,3072]{2,1,0:T(4,128)(2,1)S(1)} %get-tuple-element.40), channel_id=1, source_target_pairs={{0,4},{1,5},{2,6},{3,7},{4,0},{5,1},{6,2},{7,3},{8,12},{9,13},{10,... | collective-permute-start | bytes 73736 | tf_op jit(solution)/shard_map/ppermute | solution.py:280
  61.1 4.9 %collective-permute-start.13 = (bf16[1,4,3072]{2,1,0:T(4,128)(2,1)S(1)}, bf16[1,4,3072]{2,1,0:T(4,128)(2,1)S(1)}, u32[]{:S(2)}, u32[]{:S(2)}) collective-permute-start(bf16[1,4,3072]{2,1,0:T(4,128)(2,1)S(1)} %get-tuple-element.41), channel_id=1, source_target_pairs={{0,8},{1,9},{2,10},{3,11},{4,12},{5,13},{6,14},{7,15},{8,0},{9,1},... | collective-permute-start | bytes 73736 | tf_op jit(solution)/shard_map/ppermute | solution.py:280
  63.0 5.6 %collective-permute-start.14 = (bf16[1,4,3072]{2,1,0:T(4,128)(2,1)S(1)}, bf16[1,4,3072]{2,1,0:T(4,128)(2,1)S(1)}, u32[]{:S(2)}, u32[]{:S(2)}) collective-permute-start(bf16[1,4,3072]{2,1,0:T(4,128)(2,1)S(1)} %get-tuple-element.42), channel_id=1, source_target_pairs={{0,12},{1,13},{2,14},{3,15},{4,8},{5,9},{6,10},{7,11},{8,4},{9,5},... | collective-permute-start | bytes 73736 | tf_op jit(solution)/shard_map/ppermute | solution.py:280

commit v4 on v3

--- a/solution.py
+++ b/solution.py
@@ -24,60 +24,81 @@
     return pltpu.CompilerParams(vmem_limit_bytes=mib * MIB)
 
 
-def attend_kernel(len_ref, *refs):
-    operands, out_ref, buffers, sems = refs[:5], refs[5], refs[6:11], refs[11]
+def attend_kernel(*refs):
+    count = (len(refs) - 2) // 2
+    operands, out_ref, buffers, sems = refs[:count], refs[count], refs[count + 1 : -1], refs[-1]
     copies = [
-        pltpu.make_async_copy(operands[i], buffers[i], sems.at[i])
-        for i in range(len(operands))
+        pltpu.make_async_copy(source, target, sems.at[i])
+        for i, (source, target) in enumerate(zip(operands, buffers))
     ]
     for copy in copies:
         copy.start()
     for copy in copies:
         copy.wait()
-    q_ref, k_ref, v_ref, nk_ref, nv_ref = buffers
+    len_ref, q_ref, nk_ref, k_ref, nv_ref, v_ref = buffers
     batches, sessions = q_ref.shape[:2]
+    places = [(m, s) for m in range(batches) for s in range(sessions)]
     cache_len = k_ref.shape[2]
     width = KVH * HD
     per_kv = QH // KVH
     scale = 1.0 / math.sqrt(HD)
     head = lax.broadcasted_iota(jnp.int32, (QH, width), 0) // per_kv
     lane = lax.broadcasted_iota(jnp.int32, (QH, width), 1) // HD
-    own_kv = head == lane
+    own_kv = jnp.concatenate([head == lane] * len(places), axis=0)
     slot = lax.broadcasted_iota(jnp.int32, (QH, cache_len), 1)
-    rows = []
-    for m in range(batches):
-        q_all = q_ref[m].astype(jnp.float32)
-        nk_all = nk_ref[m].astype(jnp.float32)
-        nv_all = nv_ref[m].astype(jnp.float32)
-        for s in range(sessions):
-            q_row = q_all[s : s + 1]
-            q_heads = jnp.concatenate([q_row[:, h * HD : (h + 1) * HD] for h in range(QH)], axis=0)
-            q_wide = jnp.where(own_kv, jnp.concatenate([q_heads] * KVH, axis=1), 0.0)
-            scores = (
-                lax.dot_general(
-                    q_wide.astype(jnp.bfloat16),
-                    k_ref[m, s],
-                    (((1,), (1,)), ((), ())),
-                    preferred_element_type=jnp.float32,
-                )
-                * scale
+
+    def each(piece):
+        return jnp.concatenate([piece(m, s) for m, s in places], axis=0)
+
+    def spread(ref):
+        full = [ref[m].astype(jnp.float32) for m in range(batches)]
+        return each(lambda m, s: jnp.broadcast_to(full[m][s : s + 1], (QH, width)))
+
+    q_all = [q_ref[m].astype(jnp.float32) for m in range(batches)]
+    q_heads = jnp.concatenate(
+        [q_all[m][s : s + 1, h * HD : (h + 1) * HD] for m, s in places for h in range(QH)], axis=0
+    )
+    q_wide = jnp.where(own_kv, jnp.concatenate([q_heads] * KVH, axis=1), 0.0)
+    q_narrow = q_wide.astype(jnp.bfloat16)
+    scores = scale * jnp.concatenate(
+        [
+            lax.dot_general(
+                q_narrow[n * QH : (n + 1) * QH],
+                k_ref[m, s],
+                (((1,), (1,)), ((), ())),
+                preferred_element_type=jnp.float32,
             )
-            own_score = jnp.sum(q_wide * nk_all[s : s + 1], axis=1, keepdims=True) * scale
-            live = slot < len_ref[m, s]
-            peak = jnp.maximum(
-                jnp.max(jnp.where(live, scores, -jnp.inf), axis=1, keepdims=True), own_score
+            for n, (m, s) in enumerate(places)
+        ],
+        axis=0,
+    )
+    own_score = jnp.sum(q_wide * spread(nk_ref), axis=1, keepdims=True) * scale
+    live = each(lambda m, s: slot - len_ref[m, s : s + 1][:, None]) < 0
+    peak = jnp.maximum(
+        jnp.max(jnp.where(live, scores, -jnp.inf), axis=1, keepdims=True), own_score
+    )
+    mass = jnp.where(live, jnp.exp(scores - peak), 0.0)
+    own_mass = jnp.exp(own_score - peak)
+    total = jnp.sum(mass, axis=1, keepdims=True) + own_mass
+    probs = (mass / total).astype(jnp.bfloat16)
+    own_prob = (own_mass / total).astype(jnp.bfloat16).astype(jnp.float32)
+    wide = jnp.concatenate(
+        [
+            jnp.dot(
+                probs[n * QH : (n + 1) * QH], v_ref[m, s], preferred_element_type=jnp.float32
             )
-            mass = jnp.where(live, jnp.exp(scores - peak), 0.0)
-            own_mass = jnp.exp(own_score - peak)
-            total = jnp.sum(mass, axis=1, keepdims=True) + own_mass
-            probs = (mass / total).astype(jnp.bfloat16)
-            own_prob = (own_mass / total).astype(jnp.bfloat16).astype(jnp.float32)
-            wide = jnp.dot(probs, v_ref[m, s], preferred_element_type=jnp.float32)
-            wide = jnp.where(own_kv, wide + own_prob * nv_all[s : s + 1], 0.0)
-            heads = wide[:, :HD]
-            for k in range(1, KVH):
-                heads = heads + wide[:, k * HD : (k + 1) * HD]
-            rows.append(jnp.concatenate([heads[h : h + 1] for h in range(QH)], axis=1))
+            for n, (m, s) in enumerate(places)
+        ],
+        axis=0,
+    )
+    wide = jnp.where(own_kv, wide + own_prob * spread(nv_ref), 0.0)
+    heads = wide[:, :HD]
+    for k in range(1, KVH):
+        heads = heads + wide[:, k * HD : (k + 1) * HD]
+    rows = [
+        jnp.concatenate([heads[n * QH + h : n * QH + h + 1] for h in range(QH)], axis=1)
+        for n in range(len(places))
+    ]
     attention = jnp.concatenate(rows, axis=0).astype(jnp.bfloat16)
     devices, _, part = out_ref.shape
     for d in range(devices):
@@ -350,17 +371,17 @@
     def blocks(width):
         return jax.ShapeDtypeStruct((devices, rows, width), jnp.bfloat16)
 
-    operands = [queries, cache_keys, cache_values, new_keys, new_values]
+    operands = [lengths, queries, new_keys, cache_keys, new_values, cache_values]
     heads = pl.pallas_call(
         attend_kernel,
-        in_specs=[SMEM] + [HBM] * 5,
+        in_specs=[HBM] * len(operands),
         out_specs=VMEM,
         out_shape=blocks(w_out.shape[0]),
         scratch_shapes=[pltpu.VMEM(a.shape, a.dtype) for a in operands]
         + [pltpu.SemaphoreType.DMA((len(operands),))],
         compiler_params=params(8),
         name="attend",
-    )(lengths, *[pltpu.with_memory_space_constraint(a, pltpu.HBM) for a in operands])
+    )(*[far(a) for a in operands])
     head_blocks = exchange(heads)
     (out_here, _) = fetch([w_out], [None], heads, "fetch_out")
     halves = [jax.ShapeDtypeStruct((devices // 2, rows, features), t) for t in (jnp.float32, jnp.bfloat16)]

time: 69.5 us -> 67.3 us (0.968)
  Pallas kernels: 14.9 us -> 13.4 us
    pallas_call x1, Pallas kernels: 4.09 us -> 2.6 us  [local(): pl.pallas_call(attend_kernel, in_specs=[HBM] * len(operands), out_specs=V...]
where the time goes in v4:
time: 67.3 us; the launch traced here: 67.1 us
  waiting for transfers between devices  30.8 us (46%)
  starting transfers between devices  22.5 us (33%)
  Pallas kernels  13.4 us (20%)
    ppermute x15, waiting for transfers between devices, hop(): return lax.ppermute(blocks, 'dev', [(i, i ^ mask) for i in range(devices)])  26.1 us
    ppermute x15, starting transfers between devices, hop(): return lax.ppermute(blocks, 'dev', [(i, i ^ mask) for i in range(devices)])  15.1 us
    all_to_all x1, starting transfers between devices, exchange(): lax.all_to_all(blocks, 'dev', split_axis=0, concat_axis=0, tiled=True)  7.4 us
    pallas_call x1, Pallas kernels, local(): pl.pallas_call(lambda *refs: expert_kernel(expert_count, *refs), in_specs...  6.68 us
    all_to_all x1, waiting for transfers between devices, exchange(): lax.all_to_all(blocks, 'dev', split_axis=0, concat_axis=0, tiled=True)  4.75 us
    pallas_call x1, Pallas kernels, local(): pl.pallas_call(attend_kernel, in_specs=[HBM] * len(operands), out_specs=V...  2.6 us
    pallas_call x1, Pallas kernels, fetch(): pl.pallas_call(lambda *refs: fetch_kernel(cuts, *refs), in_specs=[HBM] *...  1.87 us
  transfers between devices with their start and end apart: 16, of which 13 were waited for; matrix products, arithmetic and copies ran while one was open for 0% of the time, Pallas kernels for 3%

profile of v4, /device:TPU:0, one launch (start us, length us, event | category | flops | bytes accessed | tf_op | source)
XLA Modules:
  0.0 67.1 jit_solution(13950322613573813423)
XLA Ops:
  0.0 2.6 %attend.1.refs_1_ = bf16[16,4,192]{2,1,0:T(4,128)(2,1)} custom-call(s32[2,2]{1,0:T(2,128)} %refs_0_.2, bf16[2,2,3072]{2,1,0:T(2,128)(2,1)} %refs_1_.1, bf16[2,2,512]{2,1,0:T(2,128)(2,1)} %refs_2_.5, bf16[2,2,128,512]{3,2,1,0:T(8,128)(2,1)} %refs_3_.2, bf16[2,2,512]{2,1,0:T(2,128)(2,1)} %refs_4_.3, bf16[2,2,128,512]{3,2,1,0:T(8,128)(2,1)} %refs_5_.1), custom_call_target="tpu_custom_call" | custom-call | tf_op jit(solution)/shard_map/attend/pallas_call | solution.py:375
  2.6 7.4 %all-to-all-start = ((bf16[16,4,192]{2,1,0:T(4,128)(2,1)}), bf16[16,4,192]{2,1,0:T(4,128)(2,1)S(1)}, u32[]{:S(2)}, u32[]{:S(2)}) async-start(bf16[16,4,192]{2,1,0:T(4,128)(2,1)} %attend.1.refs_1_), calls=%async_computation | async-start | bytes 65536 | tf_op jit(solution)/shard_map/all_to_all | solution.py:346
  10.0 1.9 %fetch_out.1 = (bf16[192,3072]{1,0:T(8,128)(2,1)S(1)}, f32[8,128]{1,0:T(8,128)}) custom-call(bf16[192,3072]{1,0:T(8,128)(2,1)} %refs_0_.3, bf16[16,4,192]{2,1,0:T(4,128)(2,1)} %attend.1.refs_1_), custom_call_target="tpu_custom_call" | custom-call | bytes 1179648 | tf_op jit(solution)/shard_map/fetch_out/pallas_call | solution.py:139
  11.9 4.8 %all-to-all-done.refs_0_ = bf16[16,4,192]{2,1,0:T(4,128)(2,1)S(1)} async-done(((bf16[16,4,192]{2,1,0:T(4,128)(2,1)}), bf16[16,4,192]{2,1,0:T(4,128)(2,1)S(1)}, u32[]{:S(2)}, u32[]{:S(2)}) %all-to-all-start) | async-done | bytes 24608 | tf_op jit(solution)/shard_map/all_to_all | solution.py:346
  16.6 0.3 project.1
  17.0 0.1 collective-permute-start
  17.1 1.4 %collective-permute-done.refs_1_ = bf16[8,4,3072]{2,1,0:T(4,128)(2,1)S(1)} collective-permute-done((bf16[8,4,3072]{2,1,0:T(4,128)(2,1)S(1)}, bf16[8,4,3072]{2,1,0:T(4,128)(2,1)S(1)}, u32[]{:S(2)}, u32[]{:S(2)}) %collective-permute-start) | collective-permute-done | bytes 196640 | tf_op jit(solution)/shard_map/ppermute | solution.py:301
  18.5 0.0 slice-start.3
  18.5 0.0 slice-start.6
  18.5 0.1 fold.4
  18.6 0.4 collective-permute-start.1
  19.0 4.5 %collective-permute-done.1.refs_1_ = bf16[4,4,3072]{2,1,0:T(4,128)(2,1)S(1)} collective-permute-done((bf16[4,4,3072]{2,1,0:T(4,128)(2,1)S(1)}, bf16[4,4,3072]{2,1,0:T(4,128)(2,1)S(1)}, u32[]{:S(2)}, u32[]{:S(2)}) %collective-permute-start.1) | collective-permute-done | bytes 98336 | tf_op jit(solution)/shard_map/ppermute | solution.py:301
  23.5 0.4 collective-permute-start.2
  24.0 0.7 %collective-permute-start.3 = (bf16[1,4,3072]{2,1,0:T(4,128)(2,1)S(1)}, bf16[1,4,3072]{2,1,0:T(4,128)(2,1)S(1)}, u32[]{:S(2)}, u32[]{:S(2)}) collective-permute-start(bf16[1,4,3072]{2,1,0:T(4,128)(2,1)S(1)} %get-tuple-element.31), channel_id=1, source_target_pairs={{0,8},{1,9},{2,10},{3,11},{4,12},{5,13},{6,14},{7,15},{8,0},{9,1},... | collective-permute-start | bytes 73736 | tf_op jit(solution)/shard_map/ppermute | solution.py:301
  24.6 3.4 %collective-permute-start.4 = (bf16[1,4,3072]{2,1,0:T(4,128)(2,1)S(1)}, bf16[1,4,3072]{2,1,0:T(4,128)(2,1)S(1)}, u32[]{:S(2)}, u32[]{:S(2)}) collective-permute-start(bf16[1,4,3072]{2,1,0:T(4,128)(2,1)S(1)} %get-tuple-element.32), channel_id=1, source_target_pairs={{0,12},{1,13},{2,14},{3,15},{4,8},{5,9},{6,10},{7,11},{8,4},{9,5},... | collective-permute-start | bytes 73736 | tf_op jit(solution)/shard_map/ppermute | solution.py:301
  28.0 0.0 collective-permute-done.2.refs_1_
  28.0 0.7 %collective-permute-done.3.refs_2_ = bf16[1,4,3072]{2,1,0:T(4,128)(2,1)S(1)} collective-permute-done((bf16[1,4,3072]{2,1,0:T(4,128)(2,1)S(1)}, bf16[1,4,3072]{2,1,0:T(4,128)(2,1)S(1)}, u32[]{:S(2)}, u32[]{:S(2)}) %collective-permute-start.3) | collective-permute-done | bytes 24608 | tf_op jit(solution)/shard_map/ppermute | solution.py:301
  28.7 1.6 %collective-permute-done.4.refs_3_ = bf16[1,4,3072]{2,1,0:T(4,128)(2,1)S(1)} collective-permute-done((bf16[1,4,3072]{2,1,0:T(4,128)(2,1)S(1)}, bf16[1,4,3072]{2,1,0:T(4,128)(2,1)S(1)}, u32[]{:S(2)}, u32[]{:S(2)}) %collective-permute-start.4) | collective-permute-done | bytes 24608 | tf_op jit(solution)/shard_map/ppermute | solution.py:301
  30.3 0.0 copy-done
  30.3 0.0 copy-done.1
  30.3 0.0 copy-done.2
  30.3 0.0 copy-done.3
  30.3 1.1 %norm.1 = (f32[4,3072]{1,0:T(4,128)S(1)}, bf16[1,4,3200]{2,1,0:T(4,128)(2,1)S(1)}) custom-call(s32[2,2,2]{2,1,0:T(2,128)S(1)} %copy-done.3, bf16[2,2,3072]{2,1,0:T(2,128)(2,1)S(1)} %copy-done, bf16[3072]{0:T(1024)(128)(2,1)S(1)} %copy-done.2, bf16[4,3072]{1,0:T(4,128)(2,1)S(1)} %bitcast.7, f32[1,4,3072]{2,1,0:T(4,128)S(1)} %get-tuple-element.29.refs_0_, ...), custom_call_target="tpu_custom_call" | custom-call | tf_op jit(solution)/shard_map/norm/pallas_call | solution.py:397
  31.4 0.0 slice-start.8
  31.4 0.6 collective-permute-start.5
  32.0 3.3 %collective-permute-done.5.refs_1_ = bf16[1,4,3200]{2,1,0:T(4,128)(2,1)S(1)} collective-permute-done((bf16[1,4,3200]{2,1,0:T(4,128)(2,1)S(1)}, bf16[1,4,3200]{2,1,0:T(4,128)(2,1)S(1)}, u32[]{:S(2)}, u32[]{:S(2)}) %collective-permute-start.5) | collective-permute-done | bytes 25632 | tf_op jit(solution)/shard_map/ppermute | solution.py:301
  35.3 3.4 %collective-permute-start.8 = (bf16[2,4,3200]{2,1,0:T(4,128)(2,1)S(1)}, bf16[2,4,3200]{2,1,0:T(4,128)(2,1)S(1)}, u32[]{:S(2)}, u32[]{:S(2)}) collective-permute-start(bf16[2,4,3200]{2,1,0:T(4,128)(2,1)S(1)} %join.2.refs_0_), channel_id=1, source_target_pairs={{0,12},{1,13},{2,14},{3,15},{4,8},{5,9},{6,10},{7,11},{8,4},{9,5},... | collective-permute-start | bytes 153608 | tf_op jit(solution)/shard_map/ppermute | solution.py:301
  38.7 0.0 collective-permute-start.7
  38.7 1.0 %collective-permute-start.6 = (bf16[2,4,3200]{2,1,0:T(4,128)(2,1)S(1)}, bf16[2,4,3200]{2,1,0:T(4,128)(2,1)S(1)}, u32[]{:S(2)}, u32[]{:S(2)}) collective-permute-start(bf16[2,4,3200]{2,1,0:T(4,128)(2,1)S(1)} %join.2.refs_0_), channel_id=1, source_target_pairs={{0,4},{1,5},{2,6},{3,7},{4,0},{5,1},{6,2},{7,3},{8,12},{9,13},{10,... | collective-permute-start | bytes 153608 | tf_op jit(solution)/shard_map/ppermute | solution.py:301
  39.8 1.5 %collective-permute-done.8.refs_3_ = bf16[2,4,3200]{2,1,0:T(4,128)(2,1)S(1)} collective-permute-done((bf16[2,4,3200]{2,1,0:T(4,128)(2,1)S(1)}, bf16[2,4,3200]{2,1,0:T(4,128)(2,1)S(1)}, u32[]{:S(2)}, u32[]{:S(2)}) %collective-permute-start.8) | collective-permute-done | bytes 51232 | tf_op jit(solution)/shard_map/ppermute | solution.py:301
  41.3 2.5 %collective-permute-done.7.refs_2_ = bf16[2,4,3200]{2,1,0:T(4,128)(2,1)S(1)} collective-permute-done((bf16[2,4,3200]{2,1,0:T(4,128)(2,1)S(1)}, bf16[2,4,3200]{2,1,0:T(4,128)(2,1)S(1)}, u32[]{:S(2)}, u32[]{:S(2)}) %collective-permute-start.7) | collective-permute-done | bytes 51232 | tf_op jit(solution)/shard_map/ppermute | solution.py:301
  43.8 0.0 collective-permute-done.6.refs_1_
  43.8 0.1 collective-permute-start.9
  43.9 1.4 %collective-permute-done.9.refs_1_ = bf16[8,4,3200]{2,1,0:T(4,128)(2,1)S(1)} collective-permute-done((bf16[8,4,3200]{2,1,0:T(4,128)(2,1)S(1)}, bf16[8,4,3200]{2,1,0:T(4,128)(2,1)S(1)}, u32[]{:S(2)}, u32[]{:S(2)}) %collective-permute-start.9) | collective-permute-done | bytes 204832 | tf_op jit(solution)/shard_map/ppermute | solution.py:301
  45.3 0.0 slice-done.6
  45.4 6.7 %experts.1 = (f32[8,4,3072]{2,1,0:T(4,128)S(1)}, bf16[8,4,3072]{2,1,0:T(4,128)(2,1)S(1)}) custom-call(bf16[8,4,3200]{2,1,0:T(4,128)(2,1)S(1)} %join.3.refs_0_, bf16[8,4,3200]{2,1,0:T(4,128)(2,1)S(1)} %collective-permute-done.9.refs_1_, bf16[3072,2048]{1,0:T(8,128)(2,1)S(1)} %bitcast.2, bf16[3072,2048]{1,0:T(8,128)(2,1)S(1)} %bitcast.4, ...), custom_call_target="tpu_custom_call" | custom-call | tf_op jit(solution)/shard_map/experts/pallas_call | solution.py:409
  52.1 0.2 collective-permute-start.10
  52.3 1.3 %collective-permute-done.10.refs_1_ = bf16[8,4,3072]{2,1,0:T(4,128)(2,1)S(1)} collective-permute-done((bf16[8,4,3072]{2,1,0:T(4,128)(2,1)S(1)}, bf16[8,4,3072]{2,1,0:T(4,128)(2,1)S(1)}, u32[]{:S(2)}, u32[]{:S(2)}) %collective-permute-start.10) | collective-permute-done | bytes 196640 | tf_op jit(solution)/shard_map/ppermute | solution.py:301
  53.6 0.1 fold.6
  53.6 0.4 collective-permute-start.11
  54.1 4.5 %collective-permute-done.11.refs_1_ = bf16[4,4,3072]{2,1,0:T(4,128)(2,1)S(1)} collective-permute-done((bf16[4,4,3072]{2,1,0:T(4,128)(2,1)S(1)}, bf16[4,4,3072]{2,1,0:T(4,128)(2,1)S(1)}, u32[]{:S(2)}, u32[]{:S(2)}) %collective-permute-start.11) | collective-permute-done | bytes 98336 | tf_op jit(solution)/shard_map/ppermute | solution.py:301
  58.6 0.3 collective-permute-start.12
  58.9 1.9 %collective-permute-start.13 = (bf16[1,4,3072]{2,1,0:T(4,128)(2,1)S(1)}, bf16[1,4,3072]{2,1,0:T(4,128)(2,1)S(1)}, u32[]{:S(2)}, u32[]{:S(2)}) collective-permute-start(bf16[1,4,3072]{2,1,0:T(4,128)(2,1)S(1)} %get-tuple-element.41), channel_id=1, source_target_pairs={{0,8},{1,9},{2,10},{3,11},{4,12},{5,13},{6,14},{7,15},{8,0},{9,1},... | collective-permute-start | bytes 73736 | tf_op jit(solution)/shard_map/ppermute | solution.py:301
  60.8 2.3 %collective-permute-start.14 = (bf16[1,4,3072]{2,1,0:T(4,128)(2,1)S(1)}, bf16[1,4,3072]{2,1,0:T(4,128)(2,1)S(1)}, u32[]{:S(2)}, u32[]{:S(2)}) collective-permute-start(bf16[1,4,3072]{2,1,0:T(4,128)(2,1)S(1)} %get-tuple-element.42), channel_id=1, source_target_pairs={{0,12},{1,13},{2,14},{3,15},{4,8},{5,9},{6,10},{7,11},{8,4},{9,5},... | collective-permute-start | bytes 73736 | tf_op jit(solution)/shard_map/ppermute | solution.py:301
  63.0 0.0 collective-permute-done.12.refs_2_
  63.0 0.7 %collective-permute-done.13.refs_3_ = bf16[1,4,3072]{2,1,0:T(4,128)(2,1)S(1)} collective-permute-done((bf16[1,4,3072]{2,1,0:T(4,128)(2,1)S(1)}, bf16[1,4,3072]{2,1,0:T(4,128)(2,1)S(1)}, u32[]{:S(2)}, u32[]{:S(2)}) %collective-permute-start.13) | collective-permute-done | bytes 24608 | tf_op jit(solution)/shard_map/ppermute | solution.py:301
  63.8 2.7 %collective-permute-done.14.refs_4_ = bf16[1,4,3072]{2,1,0:T(4,128)(2,1)S(1)} collective-permute-done((bf16[1,4,3072]{2,1,0:T(4,128)(2,1)S(1)}, bf16[1,4,3072]{2,1,0:T(4,128)(2,1)S(1)}, u32[]{:S(2)}, u32[]{:S(2)}) %collective-permute-start.14) | collective-permute-done | bytes 24608 | tf_op jit(solution)/shard_map/ppermute | solution.py:301
  66.4 0.6 final.1
  (25 shorter events, 0.1 us)
Async XLA Ops:
  2.6 14.0 %all-to-all-start = ((bf16[16,4,192]{2,1,0:T(4,128)(2,1)}), bf16[16,4,192]{2,1,0:T(4,128)(2,1)S(1)}, u32[]{:S(2)}, u32[]{:S(2)}) async-start(bf16[16,4,192]{2,1,0:T(4,128)(2,1)} %attend.1.refs_1_), calls=%async_computation | async-start | bytes 65536 | tf_op jit(solution)/shard_map/all_to_all | solution.py:346
  17.0 1.5 %collective-permute-start = (bf16[8,4,3072]{2,1,0:T(4,128)(2,1)S(1)}, bf16[8,4,3072]{2,1,0:T(4,128)(2,1)S(1)}, u32[]{:S(2)}, u32[]{:S(2)}) collective-permute-start(bf16[8,4,3072]{2,1,0:T(4,128)(2,1)S(1)} %get-tuple-element.26), channel_id=1, source_target_pairs={{0,1},{1,0},{2,3},{3,2},{4,5},{5,4},{6,7},{7,6},{8,9},{9,8},{10,11... | collective-permute-start | bytes 589832 | tf_op jit(solution)/shard_map/ppermute | solution.py:301
  18.5 11.8 %copy-start = (bf16[2,2,3072]{2,1,0:T(2,128)(2,1)S(1)}, bf16[2,2,3072]{2,1,0:T(2,128)(2,1)}, u32[]{:S(2)}) copy-start(bf16[2,2,3072]{2,1,0:T(2,128)(2,1)} %x_ref.1) | copy-start | bytes 73732
  18.5 11.8 %copy-start.1 = (bf16[3072,4]{0,1:T(4,128)(2,1)S(1)}, bf16[3072,4]{0,1:T(4,128)(2,1)}, u32[]{:S(2)}) copy-start(bf16[3072,4]{0,1:T(4,128)(2,1)} %param.23) | copy-start | bytes 73732
  18.5 11.8 %copy-start.2 = (bf16[3072]{0:T(1024)(128)(2,1)S(1)}, bf16[3072]{0:T(1024)(128)(2,1)}, u32[]{:S(2)}) copy-start(bf16[3072]{0:T(1024)(128)(2,1)} %gain_ref.1) | copy-start | bytes 18436
  18.5 11.8 %copy-start.3 = (s32[2,2,2]{2,1,0:T(2,128)S(1)}, s32[2,2,2]{2,1,0:T(2,128)}, u32[]{:S(2)}) copy-start(s32[2,2,2]{2,1,0:T(2,128)} %idx_ref.1) | copy-start | bytes 100
  18.5 26.8 %slice-start.3 = ((s8[12582912]{0:T(1024)(128)(4,1)}), s8[4194304]{0:T(1024)(128)(4,1)S(1)}, s32[]{:S(2)}) async-start(s8[12582912]{0:T(1024)(128)(4,1)} %bitcast.3), calls=%async_computation.4 | async-start | bytes 8388608
  18.5 26.8 %slice-start.6 = ((s8[12582912]{0:T(1024)(128)(4,1)}), s8[4194304]{0:T(1024)(128)(4,1)S(1)}, s32[]{:S(2)}) async-start(s8[12582912]{0:T(1024)(128)(4,1)} %bitcast.5), calls=%async_computation.7 | async-start | bytes 8388608
  18.6 4.9 %collective-permute-start.1 = (bf16[4,4,3072]{2,1,0:T(4,128)(2,1)S(1)}, bf16[4,4,3072]{2,1,0:T(4,128)(2,1)S(1)}, u32[]{:S(2)}, u32[]{:S(2)}) collective-permute-start(bf16[4,4,3072]{2,1,0:T(4,128)(2,1)S(1)} %get-tuple-element.28), channel_id=1, source_target_pairs={{0,2},{1,3},{2,0},{3,1},{4,6},{5,7},{6,4},{7,5},{8,10},{9,11},{10,... | collective-permute-start | bytes 294920 | tf_op jit(solution)/shard_map/ppermute | solution.py:301
  23.5 21.8 %slice-start.4 = ((s8[12582912]{0:T(1024)(128)(4,1)}), s8[4194304]{0:T(1024)(128)(4,1)S(1)}, s32[]{:S(2)}) async-start(s8[12582912]{0:T(1024)(128)(4,1)} %bitcast.3), calls=%async_computation.5 | async-start | bytes 8388608
  23.5 21.8 %slice-start.7 = ((s8[12582912]{0:T(1024)(128)(4,1)}), s8[4194304]{0:T(1024)(128)(4,1)S(1)}, s32[]{:S(2)}) async-start(s8[12582912]{0:T(1024)(128)(4,1)} %bitcast.5), calls=%async_computation.8 | async-start | bytes 8388608
  23.5 4.5 %collective-permute-start.2 = (bf16[1,4,3072]{2,1,0:T(4,128)(2,1)S(1)}, bf16[1,4,3072]{2,1,0:T(4,128)(2,1)S(1)}, u32[]{:S(2)}, u32[]{:S(2)}) collective-permute-start(bf16[1,4,3072]{2,1,0:T(4,128)(2,1)S(1)} %get-tuple-element.30), channel_id=1, source_target_pairs={{0,4},{1,5},{2,6},{3,7},{4,0},{5,1},{6,2},{7,3},{8,12},{9,13},{10,... | collective-permute-start | bytes 73736 | tf_op jit(solution)/shard_map/ppermute | solution.py:301
  24.0 4.7 %collective-permute-start.3 = (bf16[1,4,3072]{2,1,0:T(4,128)(2,1)S(1)}, bf16[1,4,3072]{2,1,0:T(4,128)(2,1)S(1)}, u32[]{:S(2)}, u32[]{:S(2)}) collective-permute-start(bf16[1,4,3072]{2,1,0:T(4,128)(2,1)S(1)} %get-tuple-element.31), channel_id=1, source_target_pairs={{0,8},{1,9},{2,10},{3,11},{4,12},{5,13},{6,14},{7,15},{8,0},{9,1},... | collective-permute-start | bytes 73736 | tf_op jit(solution)/shard_map/ppermute | solution.py:301
  24.6 5.6 %collective-permute-start.4 = (bf16[1,4,3072]{2,1,0:T(4,128)(2,1)S(1)}, bf16[1,4,3072]{2,1,0:T(4,128)(2,1)S(1)}, u32[]{:S(2)}, u32[]{:S(2)}) collective-permute-start(bf16[1,4,3072]{2,1,0:T(4,128)(2,1)S(1)} %get-tuple-element.32), channel_id=1, source_target_pairs={{0,12},{1,13},{2,14},{3,15},{4,8},{5,9},{6,10},{7,11},{8,4},{9,5},... | collective-permute-start | bytes 73736 | tf_op jit(solution)/shard_map/ppermute | solution.py:301
  31.4 13.9 %slice-start = ((s8[12582912]{0:T(1024)(128)(4,1)}), s8[4194304]{0:T(1024)(128)(4,1)S(1)}, s32[]{:S(2)}) async-start(s8[12582912]{0:T(1024)(128)(4,1)} %bitcast.1), calls=%async_computation.1 | async-start | bytes 8388608
  31.4 13.9 %slice-start.1 = ((s8[12582912]{0:T(1024)(128)(4,1)}), s8[4194304]{0:T(1024)(128)(4,1)S(1)}, s32[]{:S(2)}) async-start(s8[12582912]{0:T(1024)(128)(4,1)} %bitcast.1), calls=%async_computation.2 | async-start | bytes 8388608
  31.4 14.0 %slice-start.5 = ((s8[12582912]{0:T(1024)(128)(4,1)}), s8[4194304]{0:T(1024)(128)(4,1)S(1)}, s32[]{:S(2)}) async-start(s8[12582912]{0:T(1024)(128)(4,1)} %bitcast.3), calls=%async_computation.6 | async-start | bytes 8388608
  31.4 13.9 %slice-start.8 = ((s8[12582912]{0:T(1024)(128)(4,1)}), s8[4194304]{0:T(1024)(128)(4,1)S(1)}, s32[]{:S(2)}) async-start(s8[12582912]{0:T(1024)(128)(4,1)} %bitcast.5), calls=%async_computation.9 | async-start | bytes 8388608
  31.4 3.9 %collective-permute-start.5 = (bf16[1,4,3200]{2,1,0:T(4,128)(2,1)S(1)}, bf16[1,4,3200]{2,1,0:T(4,128)(2,1)S(1)}, u32[]{:S(2)}, u32[]{:S(2)}) collective-permute-start(bf16[1,4,3200]{2,1,0:T(4,128)(2,1)S(1)} %get-tuple-element.34.refs_0_), channel_id=1, source_target_pairs={{0,2},{1,3},{2,0},{3,1},{4,6},{5,7},{6,4},{7,5},{8,10},{9,11},{10,... | collective-permute-start | bytes 76808 | tf_op jit(solution)/shard_map/ppermute | solution.py:301
  35.3 10.0 %slice-start.2 = ((s8[12582912]{0:T(1024)(128)(4,1)}), s8[4194304]{0:T(1024)(128)(4,1)S(1)}, s32[]{:S(2)}) async-start(s8[12582912]{0:T(1024)(128)(4,1)} %bitcast.1), calls=%async_computation.3 | async-start | bytes 8388608
  35.3 6.0 %collective-permute-start.8 = (bf16[2,4,3200]{2,1,0:T(4,128)(2,1)S(1)}, bf16[2,4,3200]{2,1,0:T(4,128)(2,1)S(1)}, u32[]{:S(2)}, u32[]{:S(2)}) collective-permute-start(bf16[2,4,3200]{2,1,0:T(4,128)(2,1)S(1)} %join.2.refs_0_), channel_id=1, source_target_pairs={{0,12},{1,13},{2,14},{3,15},{4,8},{5,9},{6,10},{7,11},{8,4},{9,5},... | collective-permute-start | bytes 153608 | tf_op jit(solution)/shard_map/ppermute | solution.py:301
  38.7 5.0 %collective-permute-start.7 = (bf16[2,4,3200]{2,1,0:T(4,128)(2,1)S(1)}, bf16[2,4,3200]{2,1,0:T(4,128)(2,1)S(1)}, u32[]{:S(2)}, u32[]{:S(2)}) collective-permute-start(bf16[2,4,3200]{2,1,0:T(4,128)(2,1)S(1)} %join.2.refs_0_), channel_id=1, source_target_pairs={{0,8},{1,9},{2,10},{3,11},{4,12},{5,13},{6,14},{7,15},{8,0},{9,1},... | collective-permute-start | bytes 153608 | tf_op jit(solution)/shard_map/ppermute | solution.py:301
  38.7 5.0 %collective-permute-start.6 = (bf16[2,4,3200]{2,1,0:T(4,128)(2,1)S(1)}, bf16[2,4,3200]{2,1,0:T(4,128)(2,1)S(1)}, u32[]{:S(2)}, u32[]{:S(2)}) collective-permute-start(bf16[2,4,3200]{2,1,0:T(4,128)(2,1)S(1)} %join.2.refs_0_), channel_id=1, source_target_pairs={{0,4},{1,5},{2,6},{3,7},{4,0},{5,1},{6,2},{7,3},{8,12},{9,13},{10,... | collective-permute-start | bytes 153608 | tf_op jit(solution)/shard_map/ppermute | solution.py:301
  43.8 1.5 %collective-permute-start.9 = (bf16[8,4,3200]{2,1,0:T(4,128)(2,1)S(1)}, bf16[8,4,3200]{2,1,0:T(4,128)(2,1)S(1)}, u32[]{:S(2)}, u32[]{:S(2)}) collective-permute-start(bf16[8,4,3200]{2,1,0:T(4,128)(2,1)S(1)} %join.3.refs_0_), channel_id=1, source_target_pairs={{0,1},{1,0},{2,3},{3,2},{4,5},{5,4},{6,7},{7,6},{8,9},{9,8},{10,11... | collective-permute-start | bytes 614408 | tf_op jit(solution)/shard_map/ppermute | solution.py:301
  52.1 1.5 %collective-permute-start.10 = (bf16[8,4,3072]{2,1,0:T(4,128)(2,1)S(1)}, bf16[8,4,3072]{2,1,0:T(4,128)(2,1)S(1)}, u32[]{:S(2)}, u32[]{:S(2)}) collective-permute-start(bf16[8,4,3072]{2,1,0:T(4,128)(2,1)S(1)} %get-tuple-element.36), channel_id=1, source_target_pairs={{0,1},{1,0},{2,3},{3,2},{4,5},{5,4},{6,7},{7,6},{8,9},{9,8},{10,11... | collective-permute-start | bytes 589832 | tf_op jit(solution)/shard_map/ppermute | solution.py:301
  53.6 4.9 %collective-permute-start.11 = (bf16[4,4,3072]{2,1,0:T(4,128)(2,1)S(1)}, bf16[4,4,3072]{2,1,0:T(4,128)(2,1)S(1)}, u32[]{:S(2)}, u32[]{:S(2)}) collective-permute-start(bf16[4,4,3072]{2,1,0:T(4,128)(2,1)S(1)} %get-tuple-element.38), channel_id=1, source_target_pairs={{0,2},{1,3},{2,0},{3,1},{4,6},{5,7},{6,4},{7,5},{8,10},{9,11},{10,... | collective-permute-start | bytes 294920 | tf_op jit(solution)/shard_map/ppermute | solution.py:301
  58.6 4.5 %collective-permute-start.12 = (bf16[1,4,3072]{2,1,0:T(4,128)(2,1)S(1)}, bf16[1,4,3072]{2,1,0:T(4,128)(2,1)S(1)}, u32[]{:S(2)}, u32[]{:S(2)}) collective-permute-start(bf16[1,4,3072]{2,1,0:T(4,128)(2,1)S(1)} %get-tuple-element.40), channel_id=1, source_target_pairs={{0,4},{1,5},{2,6},{3,7},{4,0},{5,1},{6,2},{7,3},{8,12},{9,13},{10,... | collective-permute-start | bytes 73736 | tf_op jit(solution)/shard_map/ppermute | solution.py:301
  58.9 4.9 %collective-permute-start.13 = (bf16[1,4,3072]{2,1,0:T(4,128)(2,1)S(1)}, bf16[1,4,3072]{2,1,0:T(4,128)(2,1)S(1)}, u32[]{:S(2)}, u32[]{:S(2)}) collective-permute-start(bf16[1,4,3072]{2,1,0:T(4,128)(2,1)S(1)} %get-tuple-element.41), channel_id=1, source_target_pairs={{0,8},{1,9},{2,10},{3,11},{4,12},{5,13},{6,14},{7,15},{8,0},{9,1},... | collective-permute-start | bytes 73736 | tf_op jit(solution)/shard_map/ppermute | solution.py:301
  60.8 5.6 %collective-permute-start.14 = (bf16[1,4,3072]{2,1,0:T(4,128)(2,1)S(1)}, bf16[1,4,3072]{2,1,0:T(4,128)(2,1)S(1)}, u32[]{:S(2)}, u32[]{:S(2)}) collective-permute-start(bf16[1,4,3072]{2,1,0:T(4,128)(2,1)S(1)} %get-tuple-element.42), channel_id=1, source_target_pairs={{0,12},{1,13},{2,14},{3,15},{4,8},{5,9},{6,10},{7,11},{8,4},{9,5},... | collective-permute-start | bytes 73736 | tf_op jit(solution)/shard_map/ppermute | solution.py:301

commit v5 on v4

--- a/solution.py
+++ b/solution.py
@@ -209,38 +209,56 @@
     )(*parts, *[far(a) for a in idle])
 
 
-def norm_kernel(idx_ref, x_ref, gain_ref, router_ref, *refs):
-    resid_ref, out_ref = refs[-2:]
+def share_kernel(count, idx_ref, x_ref, *refs):
+    keep_ref, out_ref = refs[-2:]
     batches, sessions, features = x_ref.shape
-    experts = router_ref.shape[0]
     rows = batches * sessions
+    total = total_of(refs[:count])
     x_rows = jnp.concatenate([x_ref[m].astype(jnp.float32) for m in range(batches)], axis=0)
-    resid = x_rows + total_of(refs[:-2])[0]
-    resid_ref[...] = resid
-    mean_square = jnp.mean(resid * resid, axis=1, keepdims=True)
-    normed = (resid * lax.rsqrt(mean_square + 1e-05) * gain_ref[...].astype(jnp.float32).reshape(1, features)).astype(
-        jnp.bfloat16
-    )
-    logits = lax.dot_general(
-        normed, router_ref[...], (((1,), (1,)), ((), ())), preferred_element_type=jnp.float32
-    )
-    row = lax.broadcasted_iota(jnp.int32, (rows, experts), 0)
-    column = lax.broadcasted_iota(jnp.int32, (rows, experts), 1)
-    member = row < 0
+    own = total[0] + x_rows
+    row = lax.broadcasted_iota(jnp.int32, (rows, LANES), 0)
+    column = lax.broadcasted_iota(jnp.int32, (rows, LANES), 1)
+    member = jnp.zeros((rows, LANES), jnp.float32)
     for m in range(batches):
         for s in range(sessions):
             for k in range(idx_ref.shape[2]):
-                member = member | ((row == m * sessions + s) & (column == idx_ref[m, s, k]))
+                hit = (row == m * sessions + s) & (column == idx_ref[m, s, k])
+                member = jnp.where(hit, 1.0, member)
+    keep_ref[0] = own
+    keep_ref[1] = total[1]
+    out_ref[0, :, :features] = own.astype(jnp.bfloat16)
+    out_ref[1, :, :features] = total[1].astype(jnp.bfloat16)
+    out_ref[0, :, features:] = member.astype(jnp.bfloat16)
+    out_ref[1, :, features:] = jnp.zeros((rows, LANES), jnp.bfloat16)
+
+
+def norm_kernel(gain_ref, router_ref, keep_ref, sent_ref, got_ref, *refs):
+    resid_ref, out_ref = refs[-2:]
+    rows, features = resid_ref.shape
+    experts = router_ref.shape[0]
+    got = got_ref[...].astype(jnp.float32)
+    own = keep_ref[0] + got[1, :, :features]
+    resid_ref[...] = own
+    resid = jnp.concatenate([own, keep_ref[1] + got[0, :, :features]], axis=0)
+    marks = jnp.concatenate([sent_ref[0, :, features:].astype(jnp.float32), got[0, :, features:]], axis=0)
+    member = marks[:, :experts] > 0.5
+    mean_square = jnp.mean(resid * resid, axis=1, keepdims=True)
+    gain = gain_ref[...].astype(jnp.float32).reshape(1, features)
+    normed = (resid * lax.rsqrt(mean_square + 1e-05) * gain).astype(jnp.bfloat16)
+    logits = lax.dot_general(
+        normed, router_ref[...], (((1,), (1,)), ((), ())), preferred_element_type=jnp.float32
+    )
     peak = jnp.max(jnp.where(member, logits, -jnp.inf), axis=1, keepdims=True)
     mass = jnp.where(member, jnp.exp(logits - peak), 0.0)
     weights = mass / jnp.sum(mass, axis=1, keepdims=True)
     high = weights.astype(jnp.bfloat16).astype(jnp.float32)
     low = weights - high
     extra = jnp.concatenate(
-        [high, low, jnp.zeros((rows, LANES - 2 * experts), jnp.float32)], axis=1
-    ).astype(jnp.bfloat16)
-    out_ref[0, :, :features] = normed
-    out_ref[0, :, features:] = extra
+        [high, low, jnp.zeros((2 * rows, LANES - 2 * experts), jnp.float32)], axis=1
+    )
+    for n in range(2):
+        out_ref[n, :, :features] = normed[n * rows : (n + 1) * rows]
+        out_ref[n, :, features:] = extra[n * rows : (n + 1) * rows].astype(jnp.bfloat16)
 
 
 def expert_kernel(expert_count, near_ref, far_ref, gate, up, down, *refs):
@@ -289,9 +307,14 @@
     return order + [1 ^ k for k in order]
 
 
+def scatter_stages(devices):
+    stages = stages_of(devices)
+    return [(1,)] + stages[1:] + stages[:1]
+
+
 def scatter_order(devices):
     order = [0]
-    for masks in reversed([(1,)] + stages_of(devices)):
+    for masks in reversed(scatter_stages(devices)):
         order = order + [mask ^ k for mask in masks for k in order]
     return order
 
@@ -302,7 +325,7 @@
 
 
 def gather(block, idle):
-    for masks in stages_of(lax.axis_size("dev")):
+    for masks in stages_of(lax.axis_size("dev"))[1:]:
         block = join([block] + [hop(block, mask) for mask in masks], idle)
     return block, hop(block, 1)
 
@@ -325,8 +348,7 @@
     )(*parts, *[far(a) for a in idle])
 
 
-def scatter(keep, sends, idle):
-    stages = [(1,)] + stages_of(lax.axis_size("dev"))
+def scatter(keep, sends, idle, stages):
     for step, masks in enumerate(stages):
         parts = [keep] + [hop(block, mask) for block, mask in zip(sends, masks)]
         if step + 1 < len(stages):
@@ -393,18 +415,25 @@
         compiler_params=params(8),
         name="project",
     )(head_blocks, here(out_here))
-    attn_parts = scatter(keep, [send], [w_gate])
+    stages = scatter_stages(devices)
+    attn_parts = scatter(keep, [send], [w_gate], stages[:-1])
+    wide = jax.ShapeDtypeStruct((2, rows, features + LANES), jnp.bfloat16)
+    keep, send = pl.pallas_call(
+        lambda *refs: share_kernel(len(attn_parts), *refs),
+        in_specs=[SMEM] + [VMEM] * (1 + len(attn_parts)) + [HBM],
+        out_specs=(VMEM, VMEM),
+        out_shape=(jax.ShapeDtypeStruct((2, rows, features), jnp.float32), wide),
+        compiler_params=params(8),
+        name="share",
+    )(experts_idx, here(x_in), *attn_parts, far(w_gate))
     resid, message = pl.pallas_call(
         norm_kernel,
-        in_specs=[SMEM] + [VMEM] * (3 + len(attn_parts)),
+        in_specs=[VMEM] * 5 + [HBM],
         out_specs=(VMEM, VMEM),
-        out_shape=(
-            pltpu.VMEM((rows, features), jnp.float32),
-            jax.ShapeDtypeStruct((1, rows, features + LANES), jnp.bfloat16),
-        ),
+        out_shape=(pltpu.VMEM((rows, features), jnp.float32), wide),
         compiler_params=params(8),
         name="norm",
-    )(experts_idx, here(x_in), norm_gain, jnp.transpose(w_router), *attn_parts)
+    )(norm_gain, jnp.transpose(w_router), keep, send, hop(send, stages[-1][0]), far(w_gate))
     near, other = gather(message, [w_gate])
     keep, send = pl.pallas_call(
         lambda *refs: expert_kernel(expert_count, *refs),
@@ -417,7 +446,7 @@
         compiler_params=params(8),
         name="experts",
     )(near, other, here(w_gate), here(w_up), here(w_down))
-    parts = scatter(keep, [send], [])
+    parts = scatter(keep, [send], [], stages)
     return pl.pallas_call(
         final_kernel,
         in_specs=[VMEM] * (1 + len(parts)),

time: 67.3 us -> 62.7 us (0.932)
  waiting for transfers between devices: 30.8 us -> 26.6 us
    ppermute x15 -> x14, waiting for transfers between devices: 26.1 us -> 21.9 us  [hop(): return lax.ppermute(blocks, 'dev', [(i, i ^ mask) for i in range(devices)])]
    ppermute x15 -> x14, starting transfers between devices: 15.1 us -> 14.7 us  [hop(): return lax.ppermute(blocks, 'dev', [(i, i ^ mask) for i in range(devices)])]
  transfers between devices with their start and end apart: 16 -> 15, of which waited for: 13 -> 12; matrix products, arithmetic and copies ran while one was open for 0% -> 0% of each run, Pallas kernels for 3% -> 3%
where the time goes in v5:
time: 62.7 us; the launch traced here: 62.4 us
  waiting for transfers between devices  26.6 us (42%)
  starting transfers between devices  22.1 us (35%)
  Pallas kernels  13.4 us (21%)
    ppermute x14, waiting for transfers between devices, hop(): return lax.ppermute(blocks, 'dev', [(i, i ^ mask) for i in range(devices)])  21.9 us
    ppermute x14, starting transfers between devices, hop(): return lax.ppermute(blocks, 'dev', [(i, i ^ mask) for i in range(devices)])  14.7 us
    all_to_all x1, starting transfers between devices, exchange(): lax.all_to_all(blocks, 'dev', split_axis=0, concat_axis=0, tiled=True)  7.4 us
    pallas_call x1, Pallas kernels, local(): pl.pallas_call(lambda *refs: expert_kernel(expert_count, *refs), in_specs...  6.68 us
    all_to_all x1, waiting for transfers between devices, exchange(): lax.all_to_all(blocks, 'dev', split_axis=0, concat_axis=0, tiled=True)  4.75 us
    pallas_call x1, Pallas kernels, local(): pl.pallas_call(attend_kernel, in_specs=[HBM] * len(operands), out_specs=V...  2.61 us
    pallas_call x1, Pallas kernels, fetch(): pl.pallas_call(lambda *refs: fetch_kernel(cuts, *refs), in_specs=[HBM] *...  1.87 us
  transfers between devices with their start and end apart: 15, of which 12 were waited for; matrix products, arithmetic and copies ran while one was open for 0% of the time, Pallas kernels for 3%

profile of v5, /device:TPU:0, one launch (start us, length us, event | category | flops | bytes accessed | tf_op | source)
XLA Modules:
  0.0 62.4 jit_solution(10139517862098434358)
XLA Ops:
  0.0 2.6 %attend.1.refs_1_ = bf16[16,4,192]{2,1,0:T(4,128)(2,1)} custom-call(s32[2,2]{1,0:T(2,128)} %refs_0_.4, bf16[2,2,3072]{2,1,0:T(2,128)(2,1)} %refs_1_.2, bf16[2,2,512]{2,1,0:T(2,128)(2,1)} %refs_2_.3, bf16[2,2,128,512]{3,2,1,0:T(8,128)(2,1)} %refs_3_.2, bf16[2,2,512]{2,1,0:T(2,128)(2,1)} %refs_4_.3, bf16[2,2,128,512]{3,2,1,0:T(8,128)(2,1)} %refs_5_.1), custom_call_target="tpu_custom_call" | custom-call | tf_op jit(solution)/shard_map/attend/pallas_call | solution.py:397
  2.6 7.4 %all-to-all-start = ((bf16[16,4,192]{2,1,0:T(4,128)(2,1)}), bf16[16,4,192]{2,1,0:T(4,128)(2,1)S(1)}, u32[]{:S(2)}, u32[]{:S(2)}) async-start(bf16[16,4,192]{2,1,0:T(4,128)(2,1)} %attend.1.refs_1_), calls=%async_computation | async-start | bytes 65536 | tf_op jit(solution)/shard_map/all_to_all | solution.py:368
  10.0 1.9 %fetch_out.1 = (bf16[192,3072]{1,0:T(8,128)(2,1)S(1)}, f32[8,128]{1,0:T(8,128)}) custom-call(bf16[192,3072]{1,0:T(8,128)(2,1)} %refs_0_.5, bf16[16,4,192]{2,1,0:T(4,128)(2,1)} %attend.1.refs_1_), custom_call_target="tpu_custom_call" | custom-call | bytes 1179648 | tf_op jit(solution)/shard_map/fetch_out/pallas_call | solution.py:139
  11.9 4.8 %all-to-all-done.refs_0_ = bf16[16,4,192]{2,1,0:T(4,128)(2,1)S(1)} async-done(((bf16[16,4,192]{2,1,0:T(4,128)(2,1)}), bf16[16,4,192]{2,1,0:T(4,128)(2,1)S(1)}, u32[]{:S(2)}, u32[]{:S(2)}) %all-to-all-start) | async-done | bytes 24608 | tf_op jit(solution)/shard_map/all_to_all | solution.py:368
  16.7 0.3 project.1
  17.0 0.1 collective-permute-start
  17.1 1.4 %collective-permute-done.refs_1_ = bf16[8,4,3072]{2,1,0:T(4,128)(2,1)S(1)} collective-permute-done((bf16[8,4,3072]{2,1,0:T(4,128)(2,1)S(1)}, bf16[8,4,3072]{2,1,0:T(4,128)(2,1)S(1)}, u32[]{:S(2)}, u32[]{:S(2)}) %collective-permute-start) | collective-permute-done | bytes 196640 | tf_op jit(solution)/shard_map/ppermute | solution.py:324
  18.5 0.1 fold.3
  18.6 0.4 collective-permute-start.1
  19.0 0.7 %collective-permute-start.2 = (bf16[2,4,3072]{2,1,0:T(4,128)(2,1)S(1)}, bf16[2,4,3072]{2,1,0:T(4,128)(2,1)S(1)}, u32[]{:S(2)}, u32[]{:S(2)}) collective-permute-start(bf16[2,4,3072]{2,1,0:T(4,128)(2,1)S(1)} %get-tuple-element.29), channel_id=1, source_target_pairs={{0,8},{1,9},{2,10},{3,11},{4,12},{5,13},{6,14},{7,15},{8,0},{9,1},... | collective-permute-start | bytes 147464 | tf_op jit(solution)/shard_map/ppermute | solution.py:324
  19.7 3.4 %collective-permute-start.3 = (bf16[2,4,3072]{2,1,0:T(4,128)(2,1)S(1)}, bf16[2,4,3072]{2,1,0:T(4,128)(2,1)S(1)}, u32[]{:S(2)}, u32[]{:S(2)}) collective-permute-start(bf16[2,4,3072]{2,1,0:T(4,128)(2,1)S(1)} %get-tuple-element.30), channel_id=1, source_target_pairs={{0,12},{1,13},{2,14},{3,15},{4,8},{5,9},{6,10},{7,11},{8,4},{9,5},... | collective-permute-start | bytes 147464 | tf_op jit(solution)/shard_map/ppermute | solution.py:324
  23.1 0.2 collective-permute-done.1.refs_3_
  23.3 2.8 %collective-permute-done.2.refs_4_ = bf16[2,4,3072]{2,1,0:T(4,128)(2,1)S(1)} collective-permute-done((bf16[2,4,3072]{2,1,0:T(4,128)(2,1)S(1)}, bf16[2,4,3072]{2,1,0:T(4,128)(2,1)S(1)}, u32[]{:S(2)}, u32[]{:S(2)}) %collective-permute-start.2) | collective-permute-done | bytes 49184 | tf_op jit(solution)/shard_map/ppermute | solution.py:324
  26.1 0.0 collective-permute-done.3.refs_5_
  26.1 0.0 copy-done.3
  26.1 0.0 copy-done
  26.1 0.0 slice-start.4
  26.1 0.0 slice-start.7
  26.1 0.6 %share.1 = (f32[2,4,3072]{2,1,0:T(4,128)S(1)}, bf16[2,4,3200]{2,1,0:T(4,128)(2,1)S(1)}) custom-call(s32[2,2,2]{2,1,0:T(2,128)S(1)} %copy-done.3, bf16[2,2,3072]{2,1,0:T(2,128)(2,1)S(1)} %copy-done, f32[2,4,3072]{2,1,0:T(4,128)S(1)} %get-tuple-element.27.refs_2_, bf16[2,4,3072]{2,1,0:T(4,128)(2,1)S(1)} %collective-permute-done.1.refs_3_, ...), custom_call_target="tpu_custom_call" | custom-call | tf_op jit(solution)/shard_map/share/pallas_call | solution.py:421
  26.8 0.6 collective-permute-start.4
  27.4 3.6 %collective-permute-done.4.got_ref = bf16[2,4,3200]{2,1,0:T(4,128)(2,1)S(1)} collective-permute-done((bf16[2,4,3200]{2,1,0:T(4,128)(2,1)S(1)}, bf16[2,4,3200]{2,1,0:T(4,128)(2,1)S(1)}, u32[]{:S(2)}, u32[]{:S(2)}) %collective-permute-start.4) | collective-permute-done | bytes 51232 | tf_op jit(solution)/shard_map/ppermute | solution.py:324
  31.0 0.0 copy-done.1
  31.0 0.0 copy-done.2
  31.0 0.0 slice-start.5
  31.0 0.0 slice-start.8
  31.0 0.5 norm.1
  31.5 2.8 %collective-permute-start.7 = (bf16[2,4,3200]{2,1,0:T(4,128)(2,1)S(1)}, bf16[2,4,3200]{2,1,0:T(4,128)(2,1)S(1)}, u32[]{:S(2)}, u32[]{:S(2)}) collective-permute-start(bf16[2,4,3200]{2,1,0:T(4,128)(2,1)S(1)} %get-tuple-element.34.refs_0_), channel_id=1, source_target_pairs={{0,12},{1,13},{2,14},{3,15},{4,8},{5,9},{6,10},{7,11},{8,4},{9,5},... | collective-permute-start | bytes 153608 | tf_op jit(solution)/shard_map/ppermute | solution.py:324
  34.3 0.0 collective-permute-start.6
  34.3 1.6 %collective-permute-start.5 = (bf16[2,4,3200]{2,1,0:T(4,128)(2,1)S(1)}, bf16[2,4,3200]{2,1,0:T(4,128)(2,1)S(1)}, u32[]{:S(2)}, u32[]{:S(2)}) collective-permute-start(bf16[2,4,3200]{2,1,0:T(4,128)(2,1)S(1)} %get-tuple-element.34.refs_0_), channel_id=1, source_target_pairs={{0,4},{1,5},{2,6},{3,7},{4,0},{5,1},{6,2},{7,3},{8,12},{9,13},{10,... | collective-permute-start | bytes 153608 | tf_op jit(solution)/shard_map/ppermute | solution.py:324
  35.9 1.5 %collective-permute-done.7.refs_3_ = bf16[2,4,3200]{2,1,0:T(4,128)(2,1)S(1)} collective-permute-done((bf16[2,4,3200]{2,1,0:T(4,128)(2,1)S(1)}, bf16[2,4,3200]{2,1,0:T(4,128)(2,1)S(1)}, u32[]{:S(2)}, u32[]{:S(2)}) %collective-permute-start.7) | collective-permute-done | bytes 51232 | tf_op jit(solution)/shard_map/ppermute | solution.py:324
  37.4 1.9 %collective-permute-done.6.refs_2_ = bf16[2,4,3200]{2,1,0:T(4,128)(2,1)S(1)} collective-permute-done((bf16[2,4,3200]{2,1,0:T(4,128)(2,1)S(1)}, bf16[2,4,3200]{2,1,0:T(4,128)(2,1)S(1)}, u32[]{:S(2)}, u32[]{:S(2)}) %collective-permute-start.6) | collective-permute-done | bytes 51232 | tf_op jit(solution)/shard_map/ppermute | solution.py:324
  39.3 0.0 collective-permute-done.5.refs_1_
  39.4 0.1 collective-permute-start.8
  39.4 1.4 %collective-permute-done.8.refs_1_ = bf16[8,4,3200]{2,1,0:T(4,128)(2,1)S(1)} collective-permute-done((bf16[8,4,3200]{2,1,0:T(4,128)(2,1)S(1)}, bf16[8,4,3200]{2,1,0:T(4,128)(2,1)S(1)}, u32[]{:S(2)}, u32[]{:S(2)}) %collective-permute-start.8) | collective-permute-done | bytes 204832 | tf_op jit(solution)/shard_map/ppermute | solution.py:324
  40.9 0.0 slice-done.3
  41.0 6.7 %experts.1 = (f32[8,4,3072]{2,1,0:T(4,128)S(1)}, bf16[8,4,3072]{2,1,0:T(4,128)(2,1)S(1)}) custom-call(bf16[8,4,3200]{2,1,0:T(4,128)(2,1)S(1)} %join.1.refs_0_, bf16[8,4,3200]{2,1,0:T(4,128)(2,1)S(1)} %collective-permute-done.8.refs_1_, bf16[3072,2048]{1,0:T(8,128)(2,1)S(1)} %bitcast.2, bf16[3072,2048]{1,0:T(8,128)(2,1)S(1)} %bitcast.4, ...), custom_call_target="tpu_custom_call" | custom-call | tf_op jit(solution)/shard_map/experts/pallas_call | solution.py:438
  47.7 0.2 collective-permute-start.9
  47.9 1.3 %collective-permute-done.9.refs_1_ = bf16[8,4,3072]{2,1,0:T(4,128)(2,1)S(1)} collective-permute-done((bf16[8,4,3072]{2,1,0:T(4,128)(2,1)S(1)}, bf16[8,4,3072]{2,1,0:T(4,128)(2,1)S(1)}, u32[]{:S(2)}, u32[]{:S(2)}) %collective-permute-start.9) | collective-permute-done | bytes 196640 | tf_op jit(solution)/shard_map/ppermute | solution.py:324
  49.2 0.1 fold.4
  49.2 0.7 %collective-permute-start.10 = (bf16[2,4,3072]{2,1,0:T(4,128)(2,1)S(1)}, bf16[2,4,3072]{2,1,0:T(4,128)(2,1)S(1)}, u32[]{:S(2)}, u32[]{:S(2)}) collective-permute-start(bf16[2,4,3072]{2,1,0:T(4,128)(2,1)S(1)} %get-tuple-element.38), channel_id=1, source_target_pairs={{0,4},{1,5},{2,6},{3,7},{4,0},{5,1},{6,2},{7,3},{8,12},{9,13},{10,... | collective-permute-start | bytes 147464 | tf_op jit(solution)/shard_map/ppermute | solution.py:324
  50.0 1.9 %collective-permute-start.11 = (bf16[2,4,3072]{2,1,0:T(4,128)(2,1)S(1)}, bf16[2,4,3072]{2,1,0:T(4,128)(2,1)S(1)}, u32[]{:S(2)}, u32[]{:S(2)}) collective-permute-start(bf16[2,4,3072]{2,1,0:T(4,128)(2,1)S(1)} %get-tuple-element.39), channel_id=1, source_target_pairs={{0,8},{1,9},{2,10},{3,11},{4,12},{5,13},{6,14},{7,15},{8,0},{9,1},... | collective-permute-start | bytes 147464 | tf_op jit(solution)/shard_map/ppermute | solution.py:324
  51.9 1.8 %collective-permute-start.12 = (bf16[2,4,3072]{2,1,0:T(4,128)(2,1)S(1)}, bf16[2,4,3072]{2,1,0:T(4,128)(2,1)S(1)}, u32[]{:S(2)}, u32[]{:S(2)}) collective-permute-start(bf16[2,4,3072]{2,1,0:T(4,128)(2,1)S(1)} %get-tuple-element.40), channel_id=1, source_target_pairs={{0,12},{1,13},{2,14},{3,15},{4,8},{5,9},{6,10},{7,11},{8,4},{9,5},... | collective-permute-start | bytes 147464 | tf_op jit(solution)/shard_map/ppermute | solution.py:324
  53.7 0.0 collective-permute-done.10.refs_1_
  53.7 2.8 %collective-permute-done.11.refs_2_ = bf16[2,4,3072]{2,1,0:T(4,128)(2,1)S(1)} collective-permute-done((bf16[2,4,3072]{2,1,0:T(4,128)(2,1)S(1)}, bf16[2,4,3072]{2,1,0:T(4,128)(2,1)S(1)}, u32[]{:S(2)}, u32[]{:S(2)}) %collective-permute-start.11) | collective-permute-done | bytes 49184 | tf_op jit(solution)/shard_map/ppermute | solution.py:324
  56.6 1.3 %collective-permute-done.12.refs_3_ = bf16[2,4,3072]{2,1,0:T(4,128)(2,1)S(1)} collective-permute-done((bf16[2,4,3072]{2,1,0:T(4,128)(2,1)S(1)}, bf16[2,4,3072]{2,1,0:T(4,128)(2,1)S(1)}, u32[]{:S(2)}, u32[]{:S(2)}) %collective-permute-start.12) | collective-permute-done | bytes 49184 | tf_op jit(solution)/shard_map/ppermute | solution.py:324
  57.9 0.4 collective-permute-start.13
  58.3 3.5 %collective-permute-done.13.refs_2_ = bf16[1,4,3072]{2,1,0:T(4,128)(2,1)S(1)} collective-permute-done((bf16[1,4,3072]{2,1,0:T(4,128)(2,1)S(1)}, bf16[1,4,3072]{2,1,0:T(4,128)(2,1)S(1)}, u32[]{:S(2)}, u32[]{:S(2)}) %collective-permute-start.13) | collective-permute-done | bytes 24608 | tf_op jit(solution)/shard_map/ppermute | solution.py:324
  61.8 0.6 %final.1 = bf16[2,2,3072]{2,1,0:T(2,128)(2,1)} custom-call(f32[4,3072]{1,0:T(4,128)S(1)} %get-tuple-element.33.refs_0_, f32[1,4,3072]{2,1,0:T(4,128)S(1)} %get-tuple-element.41.refs_1_, bf16[1,4,3072]{2,1,0:T(4,128)(2,1)S(1)} %collective-permute-done.13.refs_2_), custom_call_target="tpu_custom_call" | custom-call | tf_op jit(solution)/shard_map/final/pallas_call | solution.py:450
  (22 shorter events, 0.1 us)
Async XLA Ops:
  0.0 26.1 %copy-start.3 = (s32[2,2,2]{2,1,0:T(2,128)S(1)}, s32[2,2,2]{2,1,0:T(2,128)}, u32[]{:S(2)}) copy-start(s32[2,2,2]{2,1,0:T(2,128)} %refs_0_.6) | copy-start | bytes 100
  0.0 26.1 %copy-start = (bf16[2,2,3072]{2,1,0:T(2,128)(2,1)S(1)}, bf16[2,2,3072]{2,1,0:T(2,128)(2,1)}, u32[]{:S(2)}) copy-start(bf16[2,2,3072]{2,1,0:T(2,128)(2,1)} %refs_1_.3) | copy-start | bytes 73732
  2.6 14.0 %all-to-all-start = ((bf16[16,4,192]{2,1,0:T(4,128)(2,1)}), bf16[16,4,192]{2,1,0:T(4,128)(2,1)S(1)}, u32[]{:S(2)}, u32[]{:S(2)}) async-start(bf16[16,4,192]{2,1,0:T(4,128)(2,1)} %attend.1.refs_1_), calls=%async_computation | async-start | bytes 65536 | tf_op jit(solution)/shard_map/all_to_all | solution.py:368
  17.0 1.5 %collective-permute-start = (bf16[8,4,3072]{2,1,0:T(4,128)(2,1)S(1)}, bf16[8,4,3072]{2,1,0:T(4,128)(2,1)S(1)}, u32[]{:S(2)}, u32[]{:S(2)}) collective-permute-start(bf16[8,4,3072]{2,1,0:T(4,128)(2,1)S(1)} %get-tuple-element.26), channel_id=1, source_target_pairs={{0,1},{1,0},{2,3},{3,2},{4,5},{5,4},{6,7},{7,6},{8,9},{9,8},{10,11... | collective-permute-start | bytes 589832 | tf_op jit(solution)/shard_map/ppermute | solution.py:324
  18.5 12.4 %copy-start.1 = (bf16[3072,4]{0,1:T(4,128)(2,1)S(1)}, bf16[3072,4]{0,1:T(4,128)(2,1)}, u32[]{:S(2)}) copy-start(bf16[3072,4]{0,1:T(4,128)(2,1)} %param.23) | copy-start | bytes 73732
  18.5 12.4 %copy-start.2 = (bf16[3072]{0:T(1024)(128)(2,1)S(1)}, bf16[3072]{0:T(1024)(128)(2,1)}, u32[]{:S(2)}) copy-start(bf16[3072]{0:T(1024)(128)(2,1)} %gain_ref.1) | copy-start | bytes 18436
  18.5 22.4 %slice-start.3 = ((s8[12582912]{0:T(1024)(128)(4,1)}), s8[4194304]{0:T(1024)(128)(4,1)S(1)}, s32[]{:S(2)}) async-start(s8[12582912]{0:T(1024)(128)(4,1)} %bitcast.3), calls=%async_computation.4 | async-start | bytes 8388608
  18.5 22.4 %slice-start.6 = ((s8[12582912]{0:T(1024)(128)(4,1)}), s8[4194304]{0:T(1024)(128)(4,1)S(1)}, s32[]{:S(2)}) async-start(s8[12582912]{0:T(1024)(128)(4,1)} %bitcast.5), calls=%async_computation.7 | async-start | bytes 8388608
  18.6 4.7 %collective-permute-start.1 = (bf16[2,4,3072]{2,1,0:T(4,128)(2,1)S(1)}, bf16[2,4,3072]{2,1,0:T(4,128)(2,1)S(1)}, u32[]{:S(2)}, u32[]{:S(2)}) collective-permute-start(bf16[2,4,3072]{2,1,0:T(4,128)(2,1)S(1)} %get-tuple-element.28), channel_id=1, source_target_pairs={{0,4},{1,5},{2,6},{3,7},{4,0},{5,1},{6,2},{7,3},{8,12},{9,13},{10,... | collective-permute-start | bytes 147464 | tf_op jit(solution)/shard_map/ppermute | solution.py:324
  19.0 7.1 %collective-permute-start.2 = (bf16[2,4,3072]{2,1,0:T(4,128)(2,1)S(1)}, bf16[2,4,3072]{2,1,0:T(4,128)(2,1)S(1)}, u32[]{:S(2)}, u32[]{:S(2)}) collective-permute-start(bf16[2,4,3072]{2,1,0:T(4,128)(2,1)S(1)} %get-tuple-element.29), channel_id=1, source_target_pairs={{0,8},{1,9},{2,10},{3,11},{4,12},{5,13},{6,14},{7,15},{8,0},{9,1},... | collective-permute-start | bytes 147464 | tf_op jit(solution)/shard_map/ppermute | solution.py:324
  19.7 6.4 %collective-permute-start.3 = (bf16[2,4,3072]{2,1,0:T(4,128)(2,1)S(1)}, bf16[2,4,3072]{2,1,0:T(4,128)(2,1)S(1)}, u32[]{:S(2)}, u32[]{:S(2)}) collective-permute-start(bf16[2,4,3072]{2,1,0:T(4,128)(2,1)S(1)} %get-tuple-element.30), channel_id=1, source_target_pairs={{0,12},{1,13},{2,14},{3,15},{4,8},{5,9},{6,10},{7,11},{8,4},{9,5},... | collective-permute-start | bytes 147464 | tf_op jit(solution)/shard_map/ppermute | solution.py:324
  26.1 14.8 %slice-start.4 = ((s8[12582912]{0:T(1024)(128)(4,1)}), s8[4194304]{0:T(1024)(128)(4,1)S(1)}, s32[]{:S(2)}) async-start(s8[12582912]{0:T(1024)(128)(4,1)} %bitcast.3), calls=%async_computation.5 | async-start | bytes 8388608
  26.1 14.8 %slice-start.7 = ((s8[12582912]{0:T(1024)(128)(4,1)}), s8[4194304]{0:T(1024)(128)(4,1)S(1)}, s32[]{:S(2)}) async-start(s8[12582912]{0:T(1024)(128)(4,1)} %bitcast.5), calls=%async_computation.8 | async-start | bytes 8388608
  26.8 4.2 %collective-permute-start.4 = (bf16[2,4,3200]{2,1,0:T(4,128)(2,1)S(1)}, bf16[2,4,3200]{2,1,0:T(4,128)(2,1)S(1)}, u32[]{:S(2)}, u32[]{:S(2)}) collective-permute-start(bf16[2,4,3200]{2,1,0:T(4,128)(2,1)S(1)} %get-tuple-element.32.sent_ref), channel_id=1, source_target_pairs={{0,2},{1,3},{2,0},{3,1},{4,6},{5,7},{6,4},{7,5},{8,10},{9,11},{10,... | collective-permute-start | bytes 153608 | tf_op jit(solution)/shard_map/ppermute | solution.py:324
  31.0 9.9 %slice-start = ((s8[12582912]{0:T(1024)(128)(4,1)}), s8[4194304]{0:T(1024)(128)(4,1)S(1)}, s32[]{:S(2)}) async-start(s8[12582912]{0:T(1024)(128)(4,1)} %bitcast.1), calls=%async_computation.1 | async-start | bytes 8388608
  31.0 10.0 %slice-start.1 = ((s8[12582912]{0:T(1024)(128)(4,1)}), s8[4194304]{0:T(1024)(128)(4,1)S(1)}, s32[]{:S(2)}) async-start(s8[12582912]{0:T(1024)(128)(4,1)} %bitcast.1), calls=%async_computation.2 | async-start | bytes 8388608
  31.0 10.0 %slice-start.5 = ((s8[12582912]{0:T(1024)(128)(4,1)}), s8[4194304]{0:T(1024)(128)(4,1)S(1)}, s32[]{:S(2)}) async-start(s8[12582912]{0:T(1024)(128)(4,1)} %bitcast.3), calls=%async_computation.6 | async-start | bytes 8388608
  31.0 10.0 %slice-start.8 = ((s8[12582912]{0:T(1024)(128)(4,1)}), s8[4194304]{0:T(1024)(128)(4,1)S(1)}, s32[]{:S(2)}) async-start(s8[12582912]{0:T(1024)(128)(4,1)} %bitcast.5), calls=%async_computation.9 | async-start | bytes 8388608
  31.5 9.5 %slice-start.2 = ((s8[12582912]{0:T(1024)(128)(4,1)}), s8[4194304]{0:T(1024)(128)(4,1)S(1)}, s32[]{:S(2)}) async-start(s8[12582912]{0:T(1024)(128)(4,1)} %bitcast.1), calls=%async_computation.3 | async-start | bytes 8388608
  31.5 5.9 %collective-permute-start.7 = (bf16[2,4,3200]{2,1,0:T(4,128)(2,1)S(1)}, bf16[2,4,3200]{2,1,0:T(4,128)(2,1)S(1)}, u32[]{:S(2)}, u32[]{:S(2)}) collective-permute-start(bf16[2,4,3200]{2,1,0:T(4,128)(2,1)S(1)} %get-tuple-element.34.refs_0_), channel_id=1, source_target_pairs={{0,12},{1,13},{2,14},{3,15},{4,8},{5,9},{6,10},{7,11},{8,4},{9,5},... | collective-permute-start | bytes 153608 | tf_op jit(solution)/shard_map/ppermute | solution.py:324
  34.3 5.0 %collective-permute-start.6 = (bf16[2,4,3200]{2,1,0:T(4,128)(2,1)S(1)}, bf16[2,4,3200]{2,1,0:T(4,128)(2,1)S(1)}, u32[]{:S(2)}, u32[]{:S(2)}) collective-permute-start(bf16[2,4,3200]{2,1,0:T(4,128)(2,1)S(1)} %get-tuple-element.34.refs_0_), channel_id=1, source_target_pairs={{0,8},{1,9},{2,10},{3,11},{4,12},{5,13},{6,14},{7,15},{8,0},{9,1},... | collective-permute-start | bytes 153608 | tf_op jit(solution)/shard_map/ppermute | solution.py:324
  34.3 5.0 %collective-permute-start.5 = (bf16[2,4,3200]{2,1,0:T(4,128)(2,1)S(1)}, bf16[2,4,3200]{2,1,0:T(4,128)(2,1)S(1)}, u32[]{:S(2)}, u32[]{:S(2)}) collective-permute-start(bf16[2,4,3200]{2,1,0:T(4,128)(2,1)S(1)} %get-tuple-element.34.refs_0_), channel_id=1, source_target_pairs={{0,4},{1,5},{2,6},{3,7},{4,0},{5,1},{6,2},{7,3},{8,12},{9,13},{10,... | collective-permute-start | bytes 153608 | tf_op jit(solution)/shard_map/ppermute | solution.py:324
  39.4 1.5 %collective-permute-start.8 = (bf16[8,4,3200]{2,1,0:T(4,128)(2,1)S(1)}, bf16[8,4,3200]{2,1,0:T(4,128)(2,1)S(1)}, u32[]{:S(2)}, u32[]{:S(2)}) collective-permute-start(bf16[8,4,3200]{2,1,0:T(4,128)(2,1)S(1)} %join.1.refs_0_), channel_id=1, source_target_pairs={{0,1},{1,0},{2,3},{3,2},{4,5},{5,4},{6,7},{7,6},{8,9},{9,8},{10,11... | collective-permute-start | bytes 614408 | tf_op jit(solution)/shard_map/ppermute | solution.py:324
  47.7 1.5 %collective-permute-start.9 = (bf16[8,4,3072]{2,1,0:T(4,128)(2,1)S(1)}, bf16[8,4,3072]{2,1,0:T(4,128)(2,1)S(1)}, u32[]{:S(2)}, u32[]{:S(2)}) collective-permute-start(bf16[8,4,3072]{2,1,0:T(4,128)(2,1)S(1)} %get-tuple-element.36), channel_id=1, source_target_pairs={{0,1},{1,0},{2,3},{3,2},{4,5},{5,4},{6,7},{7,6},{8,9},{9,8},{10,11... | collective-permute-start | bytes 589832 | tf_op jit(solution)/shard_map/ppermute | solution.py:324
  49.2 4.5 %collective-permute-start.10 = (bf16[2,4,3072]{2,1,0:T(4,128)(2,1)S(1)}, bf16[2,4,3072]{2,1,0:T(4,128)(2,1)S(1)}, u32[]{:S(2)}, u32[]{:S(2)}) collective-permute-start(bf16[2,4,3072]{2,1,0:T(4,128)(2,1)S(1)} %get-tuple-element.38), channel_id=1, source_target_pairs={{0,4},{1,5},{2,6},{3,7},{4,0},{5,1},{6,2},{7,3},{8,12},{9,13},{10,... | collective-permute-start | bytes 147464 | tf_op jit(solution)/shard_map/ppermute | solution.py:324
  50.0 6.6 %collective-permute-start.11 = (bf16[2,4,3072]{2,1,0:T(4,128)(2,1)S(1)}, bf16[2,4,3072]{2,1,0:T(4,128)(2,1)S(1)}, u32[]{:S(2)}, u32[]{:S(2)}) collective-permute-start(bf16[2,4,3072]{2,1,0:T(4,128)(2,1)S(1)} %get-tuple-element.39), channel_id=1, source_target_pairs={{0,8},{1,9},{2,10},{3,11},{4,12},{5,13},{6,14},{7,15},{8,0},{9,1},... | collective-permute-start | bytes 147464 | tf_op jit(solution)/shard_map/ppermute | solution.py:324
  51.9 6.0 %collective-permute-start.12 = (bf16[2,4,3072]{2,1,0:T(4,128)(2,1)S(1)}, bf16[2,4,3072]{2,1,0:T(4,128)(2,1)S(1)}, u32[]{:S(2)}, u32[]{:S(2)}) collective-permute-start(bf16[2,4,3072]{2,1,0:T(4,128)(2,1)S(1)} %get-tuple-element.40), channel_id=1, source_target_pairs={{0,12},{1,13},{2,14},{3,15},{4,8},{5,9},{6,10},{7,11},{8,4},{9,5},... | collective-permute-start | bytes 147464 | tf_op jit(solution)/shard_map/ppermute | solution.py:324
  57.9 3.9 %collective-permute-start.13 = (bf16[1,4,3072]{2,1,0:T(4,128)(2,1)S(1)}, bf16[1,4,3072]{2,1,0:T(4,128)(2,1)S(1)}, u32[]{:S(2)}, u32[]{:S(2)}) collective-permute-start(bf16[1,4,3072]{2,1,0:T(4,128)(2,1)S(1)} %get-tuple-element.42), channel_id=1, source_target_pairs={{0,2},{1,3},{2,0},{3,1},{4,6},{5,7},{6,4},{7,5},{8,10},{9,11},{10,... | collective-permute-start | bytes 73736 | tf_op jit(solution)/shard_map/ppermute | solution.py:324

commit v6 on v5

--- a/solution.py
+++ b/solution.py
@@ -170,13 +170,18 @@
             at += rows
 
 
-def project_kernel(order, x_ref, w_ref, *out_refs):
+def project_kernel(order, x_ref, w_ref, other_ref, _, *out_refs):
     rows, features = out_refs[0].shape[1:]
+    half = w_ref.shape[0]
     me = lax.axis_index("dev")
-    inputs = rows_of(x_ref, [me ^ k for k in order]).astype(jnp.bfloat16)
+    inputs = rows_of(x_ref, [lax.div(me ^ k, 2) for k in order])
+    even = lax.rem(me, 2) == 0
+    mine = jnp.where(even, inputs[:, :half], inputs[:, half:]).astype(jnp.bfloat16)
+    others = jnp.where(even, inputs[:, half:], inputs[:, :half]).astype(jnp.bfloat16)
     for start in range(0, features, CHUNK):
         cut = slice(start, start + CHUNK)
-        part = jnp.dot(inputs, w_ref[:, cut], preferred_element_type=jnp.float32)
+        part = jnp.dot(mine, w_ref[:, cut], preferred_element_type=jnp.float32)
+        part = part + jnp.dot(others, other_ref[:, cut], preferred_element_type=jnp.float32)
         send_blocks(out_refs, part, cut, rows)
 
 
@@ -313,8 +318,12 @@
 
 
 def scatter_order(devices):
+    return nested(scatter_stages(devices))
+
+
+def nested(stages):
     order = [0]
-    for masks in reversed(scatter_stages(devices)):
+    for masks in reversed(stages):
         order = order + [mask ^ k for mask in masks for k in order]
     return order
 
@@ -365,7 +374,11 @@
 
 
 def exchange(blocks):
-    return lax.all_to_all(blocks, "dev", split_axis=0, concat_axis=0, tiled=True)
+    devices = lax.axis_size("dev")
+    groups = [list(range(core, devices, 2)) for core in range(2)]
+    return lax.all_to_all(
+        blocks, "dev", split_axis=0, concat_axis=0, axis_index_groups=groups, tiled=True
+    )
 
 
 def local(
@@ -390,15 +403,12 @@
     rows = batches * sessions
     units = w_gate.shape[1]
 
-    def blocks(width):
-        return jax.ShapeDtypeStruct((devices, rows, width), jnp.bfloat16)
-
     operands = [lengths, queries, new_keys, cache_keys, new_values, cache_values]
     heads = pl.pallas_call(
         attend_kernel,
         in_specs=[HBM] * len(operands),
         out_specs=VMEM,
-        out_shape=blocks(w_out.shape[0]),
+        out_shape=jax.ShapeDtypeStruct((devices // 2, rows, 2 * w_out.shape[0]), jnp.bfloat16),
         scratch_shapes=[pltpu.VMEM(a.shape, a.dtype) for a in operands]
         + [pltpu.SemaphoreType.DMA((len(operands),))],
         compiler_params=params(8),
@@ -406,17 +416,20 @@
     )(*[far(a) for a in operands])
     head_blocks = exchange(heads)
     (out_here, _) = fetch([w_out], [None], heads, "fetch_out")
+    out_other = hop(w_out, 1)
     halves = [jax.ShapeDtypeStruct((devices // 2, rows, features), t) for t in (jnp.float32, jnp.bfloat16)]
-    keep, send = pl.pallas_call(
-        lambda *refs: project_kernel(scatter_order(devices), *refs),
-        in_specs=[VMEM] * 2,
-        out_specs=[VMEM] * 2,
-        out_shape=halves,
+    stages = scatter_stages(devices)
+    first = (devices // 2) // (len(stages[1]) + 1)
+    keep, *sends = pl.pallas_call(
+        lambda *refs: project_kernel(nested(stages[1:]), *refs),
+        in_specs=[VMEM] * 3 + [HBM],
+        out_specs=[VMEM] * (len(stages[1]) + 1),
+        out_shape=[jax.ShapeDtypeStruct((first, rows, features), jnp.float32)]
+        + [jax.ShapeDtypeStruct((first, rows, features), jnp.bfloat16)] * len(stages[1]),
         compiler_params=params(8),
         name="project",
-    )(head_blocks, here(out_here))
-    stages = scatter_stages(devices)
-    attn_parts = scatter(keep, [send], [w_gate], stages[:-1])
+    )(head_blocks, here(out_here), here(out_other), far(w_gate))
+    attn_parts = scatter(keep, sends, [w_gate], stages[1:-1])
     wide = jax.ShapeDtypeStruct((2, rows, features + LANES), jnp.bfloat16)
     keep, send = pl.pallas_call(
         lambda *refs: share_kernel(len(attn_parts), *refs),

time: 62.7 us -> 61 us (0.973)
  waiting for transfers between devices: 26.6 us -> 24.6 us
    ppermute x14, waiting for transfers between devices: 21.9 us -> 19.8 us  [hop(): return lax.ppermute(blocks, 'dev', [(i, i ^ mask) for i in range(devices)])]
    ppermute x14, starting transfers between devices: 14.7 us -> 15.5 us  [hop(): return lax.ppermute(blocks, 'dev', [(i, i ^ mask) for i in range(devices)])]
  transfers between devices with their start and end apart: 15 -> 15, of which waited for: 12 -> 12; matrix products, arithmetic and copies ran while one was open for 0% -> 0% of each run, Pallas kernels for 3% -> 7%
where the time goes in v6:
time: 61 us; the launch traced here: 60.8 us
  waiting for transfers between devices  24.6 us (40%)
  starting transfers between devices  22.3 us (37%)
  Pallas kernels  13.6 us (22%)
    ppermute x14, waiting for transfers between devices, hop(): return lax.ppermute(blocks, 'dev', [(i, i ^ mask) for i in range(devices)])  19.8 us
    ppermute x14, starting transfers between devices, hop(): return lax.ppermute(blocks, 'dev', [(i, i ^ mask) for i in range(devices)])  15.5 us
    all_to_all x1, starting transfers between devices, exchange(): lax.all_to_all(blocks, 'dev', split_axis=0, concat_axis=0, axis_index_gro...  6.87 us
    pallas_call x1, Pallas kernels, local(): pl.pallas_call(lambda *refs: expert_kernel(expert_count, *refs), in_specs...  6.68 us
    all_to_all x1, waiting for transfers between devices, exchange(): lax.all_to_all(blocks, 'dev', split_axis=0, concat_axis=0, axis_index_gro...  4.75 us
    pallas_call x1, Pallas kernels, local(): pl.pallas_call(attend_kernel, in_specs=[HBM] * len(operands), out_specs=V...  2.53 us
    pallas_call x1, Pallas kernels, fetch(): pl.pallas_call(lambda *refs: fetch_kernel(cuts, *refs), in_specs=[HBM] *...  1.87 us
  transfers between devices with their start and end apart: 15, of which 12 were waited for; matrix products, arithmetic and copies ran while one was open for 0% of the time, Pallas kernels for 7%

profile of v6, /device:TPU:0, one launch (start us, length us, event | category | flops | bytes accessed | tf_op | source)
XLA Modules:
  0.0 60.8 jit_solution(2682689546923097668)
XLA Ops:
  0.0 0.5 collective-permute-start
  0.5 2.5 %attend.1.refs_1_ = bf16[8,4,384]{2,1,0:T(4,128)(2,1)} custom-call(s32[2,2]{1,0:T(2,128)} %refs_0_.4, bf16[2,2,3072]{2,1,0:T(2,128)(2,1)} %refs_1_.2, bf16[2,2,512]{2,1,0:T(2,128)(2,1)} %refs_2_.2, bf16[2,2,128,512]{3,2,1,0:T(8,128)(2,1)} %refs_3_.3, bf16[2,2,512]{2,1,0:T(2,128)(2,1)} %refs_4_.3, bf16[2,2,128,512]{3,2,1,0:T(8,128)(2,1)} %refs_5_.1), custom_call_target="tpu_custom_call" | custom-call | tf_op jit(solution)/shard_map/attend/pallas_call | solution.py:407
  3.0 6.9 %all-to-all-start = ((bf16[8,4,384]{2,1,0:T(4,128)(2,1)}), bf16[8,4,384]{2,1,0:T(4,128)(2,1)S(1)}, u32[]{:S(2)}, u32[]{:S(2)}) async-start(bf16[8,4,384]{2,1,0:T(4,128)(2,1)} %attend.1.refs_1_), calls=%async_computation | async-start | bytes 49152 | tf_op jit(solution)/shard_map/all_to_all | solution.py:379
  9.9 1.9 %fetch_out.1 = (bf16[192,3072]{1,0:T(8,128)(2,1)S(1)}, f32[8,128]{1,0:T(8,128)}) custom-call(bf16[192,3072]{1,0:T(8,128)(2,1)} %refs_0_.5, bf16[8,4,384]{2,1,0:T(4,128)(2,1)} %attend.1.refs_1_), custom_call_target="tpu_custom_call" | custom-call | bytes 1179648 | tf_op jit(solution)/shard_map/fetch_out/pallas_call | solution.py:139
  11.7 4.7 %all-to-all-done.refs_0_ = bf16[8,4,384]{2,1,0:T(4,128)(2,1)S(1)} async-done(((bf16[8,4,384]{2,1,0:T(4,128)(2,1)}), bf16[8,4,384]{2,1,0:T(4,128)(2,1)S(1)}, u32[]{:S(2)}, u32[]{:S(2)}) %all-to-all-start) | async-done | bytes 24608 | tf_op jit(solution)/shard_map/all_to_all | solution.py:379
  16.5 0.0 collective-permute-done.refs_2_
  16.5 0.0 slice-start.6
  16.5 0.7 %project.1 = (f32[2,4,3072]{2,1,0:T(4,128)S(1)}, bf16[2,4,3072]{2,1,0:T(4,128)(2,1)S(1)}, bf16[2,4,3072]{2,1,0:T(4,128)(2,1)S(1)}, bf16[2,4,3072]{2,1,0:T(4,128)(2,1)S(1)}) custom-call(bf16[8,4,384]{2,1,0:T(4,128)(2,1)S(1)} %all-to-all-done.refs_0_, bf16[192,3072]{1,0:T(8,128)(2,1)S(1)} %get-tuple-element.22.refs_1_, ...), custom_call_target="tpu_custom_call" | custom-call | tf_op jit(solution)/shard_map/project/pallas_call | solution.py:423
  17.2 0.5 collective-permute-start.1
  17.7 0.7 %collective-permute-start.2 = (bf16[2,4,3072]{2,1,0:T(4,128)(2,1)S(1)}, bf16[2,4,3072]{2,1,0:T(4,128)(2,1)S(1)}, u32[]{:S(2)}, u32[]{:S(2)}) collective-permute-start(bf16[2,4,3072]{2,1,0:T(4,128)(2,1)S(1)} %get-tuple-element.25), channel_id=1, source_target_pairs={{0,8},{1,9},{2,10},{3,11},{4,12},{5,13},{6,14},{7,15},{8,0},{9,1},... | collective-permute-start | bytes 147464 | tf_op jit(solution)/shard_map/ppermute | solution.py:333
  18.4 3.3 %collective-permute-start.3 = (bf16[2,4,3072]{2,1,0:T(4,128)(2,1)S(1)}, bf16[2,4,3072]{2,1,0:T(4,128)(2,1)S(1)}, u32[]{:S(2)}, u32[]{:S(2)}) collective-permute-start(bf16[2,4,3072]{2,1,0:T(4,128)(2,1)S(1)} %get-tuple-element.26), channel_id=1, source_target_pairs={{0,12},{1,13},{2,14},{3,15},{4,8},{5,9},{6,10},{7,11},{8,4},{9,5},... | collective-permute-start | bytes 147464 | tf_op jit(solution)/shard_map/ppermute | solution.py:333
  21.6 0.0 collective-permute-done.1.refs_3_
  21.6 1.2 %collective-permute-done.2.refs_4_ = bf16[2,4,3072]{2,1,0:T(4,128)(2,1)S(1)} collective-permute-done((bf16[2,4,3072]{2,1,0:T(4,128)(2,1)S(1)}, bf16[2,4,3072]{2,1,0:T(4,128)(2,1)S(1)}, u32[]{:S(2)}, u32[]{:S(2)}) %collective-permute-start.2) | collective-permute-done | bytes 49184 | tf_op jit(solution)/shard_map/ppermute | solution.py:333
  22.9 1.4 %collective-permute-done.3.refs_5_ = bf16[2,4,3072]{2,1,0:T(4,128)(2,1)S(1)} collective-permute-done((bf16[2,4,3072]{2,1,0:T(4,128)(2,1)S(1)}, bf16[2,4,3072]{2,1,0:T(4,128)(2,1)S(1)}, u32[]{:S(2)}, u32[]{:S(2)}) %collective-permute-start.3) | collective-permute-done | bytes 49184 | tf_op jit(solution)/shard_map/ppermute | solution.py:333
  24.3 0.0 copy-done.3
  24.4 0.6 %share.1 = (f32[2,4,3072]{2,1,0:T(4,128)S(1)}, bf16[2,4,3200]{2,1,0:T(4,128)(2,1)S(1)}) custom-call(s32[2,2,2]{2,1,0:T(2,128)S(1)} %copy-done.3, bf16[2,2,3072]{2,1,0:T(2,128)(2,1)S(1)} %copy-done, f32[2,4,3072]{2,1,0:T(4,128)S(1)} %get-tuple-element.23.refs_2_, bf16[2,4,3072]{2,1,0:T(4,128)(2,1)S(1)} %collective-permute-done.1.refs_3_, ...), custom_call_target="tpu_custom_call" | custom-call | tf_op jit(solution)/shard_map/share/pallas_call | solution.py:434
  25.0 0.7 %collective-permute-start.4 = (bf16[2,4,3200]{2,1,0:T(4,128)(2,1)S(1)}, bf16[2,4,3200]{2,1,0:T(4,128)(2,1)S(1)}, u32[]{:S(2)}, u32[]{:S(2)}) collective-permute-start(bf16[2,4,3200]{2,1,0:T(4,128)(2,1)S(1)} %get-tuple-element.28.sent_ref), channel_id=1, source_target_pairs={{0,2},{1,3},{2,0},{3,1},{4,6},{5,7},{6,4},{7,5},{8,10},{9,11},{10,... | collective-permute-start | bytes 153608 | tf_op jit(solution)/shard_map/ppermute | solution.py:333
  25.7 3.5 %collective-permute-done.4.got_ref = bf16[2,4,3200]{2,1,0:T(4,128)(2,1)S(1)} collective-permute-done((bf16[2,4,3200]{2,1,0:T(4,128)(2,1)S(1)}, bf16[2,4,3200]{2,1,0:T(4,128)(2,1)S(1)}, u32[]{:S(2)}, u32[]{:S(2)}) %collective-permute-start.4) | collective-permute-done | bytes 51232 | tf_op jit(solution)/shard_map/ppermute | solution.py:333
  29.2 0.0 slice-start.5
  29.2 0.0 slice-start.8
  29.2 0.5 norm.1
  29.7 3.2 %collective-permute-start.7 = (bf16[2,4,3200]{2,1,0:T(4,128)(2,1)S(1)}, bf16[2,4,3200]{2,1,0:T(4,128)(2,1)S(1)}, u32[]{:S(2)}, u32[]{:S(2)}) collective-permute-start(bf16[2,4,3200]{2,1,0:T(4,128)(2,1)S(1)} %get-tuple-element.30.refs_0_), channel_id=1, source_target_pairs={{0,12},{1,13},{2,14},{3,15},{4,8},{5,9},{6,10},{7,11},{8,4},{9,5},... | collective-permute-start | bytes 153608 | tf_op jit(solution)/shard_map/ppermute | solution.py:333
  32.9 0.0 collective-permute-start.6
  32.9 1.2 %collective-permute-start.5 = (bf16[2,4,3200]{2,1,0:T(4,128)(2,1)S(1)}, bf16[2,4,3200]{2,1,0:T(4,128)(2,1)S(1)}, u32[]{:S(2)}, u32[]{:S(2)}) collective-permute-start(bf16[2,4,3200]{2,1,0:T(4,128)(2,1)S(1)} %get-tuple-element.30.refs_0_), channel_id=1, source_target_pairs={{0,4},{1,5},{2,6},{3,7},{4,0},{5,1},{6,2},{7,3},{8,12},{9,13},{10,... | collective-permute-start | bytes 153608 | tf_op jit(solution)/shard_map/ppermute | solution.py:333
  34.1 1.5 %collective-permute-done.7.refs_3_ = bf16[2,4,3200]{2,1,0:T(4,128)(2,1)S(1)} collective-permute-done((bf16[2,4,3200]{2,1,0:T(4,128)(2,1)S(1)}, bf16[2,4,3200]{2,1,0:T(4,128)(2,1)S(1)}, u32[]{:S(2)}, u32[]{:S(2)}) %collective-permute-start.7) | collective-permute-done | bytes 51232 | tf_op jit(solution)/shard_map/ppermute | solution.py:333
  35.6 2.3 %collective-permute-done.6.refs_2_ = bf16[2,4,3200]{2,1,0:T(4,128)(2,1)S(1)} collective-permute-done((bf16[2,4,3200]{2,1,0:T(4,128)(2,1)S(1)}, bf16[2,4,3200]{2,1,0:T(4,128)(2,1)S(1)}, u32[]{:S(2)}, u32[]{:S(2)}) %collective-permute-start.6) | collective-permute-done | bytes 51232 | tf_op jit(solution)/shard_map/ppermute | solution.py:333
  37.9 0.0 collective-permute-done.5.refs_1_
  38.0 0.1 collective-permute-start.8
  38.0 1.4 %collective-permute-done.8.refs_1_ = bf16[8,4,3200]{2,1,0:T(4,128)(2,1)S(1)} collective-permute-done((bf16[8,4,3200]{2,1,0:T(4,128)(2,1)S(1)}, bf16[8,4,3200]{2,1,0:T(4,128)(2,1)S(1)}, u32[]{:S(2)}, u32[]{:S(2)}) %collective-permute-start.8) | collective-permute-done | bytes 204832 | tf_op jit(solution)/shard_map/ppermute | solution.py:333
  39.5 0.0 slice-done.7
  39.5 0.0 slice-done
  39.5 0.0 slice-done.1
  39.5 0.0 slice-done.5
  39.5 0.0 slice-done.8
  39.5 0.0 slice-done.2
  39.6 6.7 %experts.1 = (f32[8,4,3072]{2,1,0:T(4,128)S(1)}, bf16[8,4,3072]{2,1,0:T(4,128)(2,1)S(1)}) custom-call(bf16[8,4,3200]{2,1,0:T(4,128)(2,1)S(1)} %join.1.refs_0_, bf16[8,4,3200]{2,1,0:T(4,128)(2,1)S(1)} %collective-permute-done.8.refs_1_, bf16[3072,2048]{1,0:T(8,128)(2,1)S(1)} %bitcast.2, bf16[3072,2048]{1,0:T(8,128)(2,1)S(1)} %bitcast.4, ...), custom_call_target="tpu_custom_call" | custom-call | tf_op jit(solution)/shard_map/experts/pallas_call | solution.py:451
  46.3 0.2 collective-permute-start.9
  46.5 1.3 %collective-permute-done.9.refs_1_ = bf16[8,4,3072]{2,1,0:T(4,128)(2,1)S(1)} collective-permute-done((bf16[8,4,3072]{2,1,0:T(4,128)(2,1)S(1)}, bf16[8,4,3072]{2,1,0:T(4,128)(2,1)S(1)}, u32[]{:S(2)}, u32[]{:S(2)}) %collective-permute-start.9) | collective-permute-done | bytes 196640 | tf_op jit(solution)/shard_map/ppermute | solution.py:333
  47.8 0.1 fold.2
  47.8 0.4 collective-permute-start.10
  48.2 2.0 %collective-permute-start.11 = (bf16[2,4,3072]{2,1,0:T(4,128)(2,1)S(1)}, bf16[2,4,3072]{2,1,0:T(4,128)(2,1)S(1)}, u32[]{:S(2)}, u32[]{:S(2)}) collective-permute-start(bf16[2,4,3072]{2,1,0:T(4,128)(2,1)S(1)} %get-tuple-element.35), channel_id=1, source_target_pairs={{0,8},{1,9},{2,10},{3,11},{4,12},{5,13},{6,14},{7,15},{8,0},{9,1},... | collective-permute-start | bytes 147464 | tf_op jit(solution)/shard_map/ppermute | solution.py:333
  50.2 2.1 %collective-permute-start.12 = (bf16[2,4,3072]{2,1,0:T(4,128)(2,1)S(1)}, bf16[2,4,3072]{2,1,0:T(4,128)(2,1)S(1)}, u32[]{:S(2)}, u32[]{:S(2)}) collective-permute-start(bf16[2,4,3072]{2,1,0:T(4,128)(2,1)S(1)} %get-tuple-element.36), channel_id=1, source_target_pairs={{0,12},{1,13},{2,14},{3,15},{4,8},{5,9},{6,10},{7,11},{8,4},{9,5},... | collective-permute-start | bytes 147464 | tf_op jit(solution)/shard_map/ppermute | solution.py:333
  52.3 0.2 collective-permute-done.10.refs_1_
  52.5 2.4 %collective-permute-done.11.refs_2_ = bf16[2,4,3072]{2,1,0:T(4,128)(2,1)S(1)} collective-permute-done((bf16[2,4,3072]{2,1,0:T(4,128)(2,1)S(1)}, bf16[2,4,3072]{2,1,0:T(4,128)(2,1)S(1)}, u32[]{:S(2)}, u32[]{:S(2)}) %collective-permute-start.11) | collective-permute-done | bytes 49184 | tf_op jit(solution)/shard_map/ppermute | solution.py:333
  54.9 1.3 %collective-permute-done.12.refs_3_ = bf16[2,4,3072]{2,1,0:T(4,128)(2,1)S(1)} collective-permute-done((bf16[2,4,3072]{2,1,0:T(4,128)(2,1)S(1)}, bf16[2,4,3072]{2,1,0:T(4,128)(2,1)S(1)}, u32[]{:S(2)}, u32[]{:S(2)}) %collective-permute-start.12) | collective-permute-done | bytes 49184 | tf_op jit(solution)/shard_map/ppermute | solution.py:333
  56.2 0.7 %collective-permute-start.13 = (bf16[1,4,3072]{2,1,0:T(4,128)(2,1)S(1)}, bf16[1,4,3072]{2,1,0:T(4,128)(2,1)S(1)}, u32[]{:S(2)}, u32[]{:S(2)}) collective-permute-start(bf16[1,4,3072]{2,1,0:T(4,128)(2,1)S(1)} %get-tuple-element.38), channel_id=1, source_target_pairs={{0,2},{1,3},{2,0},{3,1},{4,6},{5,7},{6,4},{7,5},{8,10},{9,11},{10,... | collective-permute-start | bytes 73736 | tf_op jit(solution)/shard_map/ppermute | solution.py:333
  56.9 3.2 %collective-permute-done.13.refs_2_ = bf16[1,4,3072]{2,1,0:T(4,128)(2,1)S(1)} collective-permute-done((bf16[1,4,3072]{2,1,0:T(4,128)(2,1)S(1)}, bf16[1,4,3072]{2,1,0:T(4,128)(2,1)S(1)}, u32[]{:S(2)}, u32[]{:S(2)}) %collective-permute-start.13) | collective-permute-done | bytes 24608 | tf_op jit(solution)/shard_map/ppermute | solution.py:333
  60.1 0.6 %final.1 = bf16[2,2,3072]{2,1,0:T(2,128)(2,1)} custom-call(f32[4,3072]{1,0:T(4,128)S(1)} %get-tuple-element.29.refs_0_, f32[1,4,3072]{2,1,0:T(4,128)S(1)} %get-tuple-element.37.refs_1_, bf16[1,4,3072]{2,1,0:T(4,128)(2,1)S(1)} %collective-permute-done.13.refs_2_), custom_call_target="tpu_custom_call" | custom-call | tf_op jit(solution)/shard_map/final/pallas_call | solution.py:463
  (21 shorter events, 0.1 us)
Async XLA Ops:
  0.0 24.3 %copy-start.3 = (s32[2,2,2]{2,1,0:T(2,128)S(1)}, s32[2,2,2]{2,1,0:T(2,128)}, u32[]{:S(2)}) copy-start(s32[2,2,2]{2,1,0:T(2,128)} %refs_0_.6) | copy-start | bytes 100
  0.0 24.3 %copy-start = (bf16[2,2,3072]{2,1,0:T(2,128)(2,1)S(1)}, bf16[2,2,3072]{2,1,0:T(2,128)(2,1)}, u32[]{:S(2)}) copy-start(bf16[2,2,3072]{2,1,0:T(2,128)(2,1)} %refs_1_.3) | copy-start | bytes 73732
  0.0 16.5 %collective-permute-start = (bf16[192,3072]{1,0:T(8,128)(2,1)}, bf16[192,3072]{1,0:T(8,128)(2,1)S(1)}, u32[]{:S(2)}, u32[]{:S(2)}) collective-permute-start(bf16[192,3072]{1,0:T(8,128)(2,1)} %refs_0_.5), channel_id=1, source_target_pairs={{0,1},{1,0},{2,3},{3,2},{4,5},{5,4},{6,7},{7,6},{8,9},{9,8},{10,11... | collective-permute-start | bytes 3538952 | tf_op jit(solution)/shard_map/ppermute | solution.py:333
  3.0 13.5 %all-to-all-start = ((bf16[8,4,384]{2,1,0:T(4,128)(2,1)}), bf16[8,4,384]{2,1,0:T(4,128)(2,1)S(1)}, u32[]{:S(2)}, u32[]{:S(2)}) async-start(bf16[8,4,384]{2,1,0:T(4,128)(2,1)} %attend.1.refs_1_), calls=%async_computation | async-start | bytes 49152 | tf_op jit(solution)/shard_map/all_to_all | solution.py:379
  16.5 12.7 %copy-start.1 = (bf16[3072,4]{0,1:T(4,128)(2,1)S(1)}, bf16[3072,4]{0,1:T(4,128)(2,1)}, u32[]{:S(2)}) copy-start(bf16[3072,4]{0,1:T(4,128)(2,1)} %param.23) | copy-start | bytes 73732
  16.5 12.7 %copy-start.2 = (bf16[3072]{0:T(1024)(128)(2,1)S(1)}, bf16[3072]{0:T(1024)(128)(2,1)}, u32[]{:S(2)}) copy-start(bf16[3072]{0:T(1024)(128)(2,1)} %gain_ref.1) | copy-start | bytes 18436
  16.5 23.0 %slice-start.3 = ((s8[12582912]{0:T(1024)(128)(4,1)}), s8[4194304]{0:T(1024)(128)(4,1)S(1)}, s32[]{:S(2)}) async-start(s8[12582912]{0:T(1024)(128)(4,1)} %bitcast.3), calls=%async_computation.4 | async-start | bytes 8388608
  16.5 23.0 %slice-start.6 = ((s8[12582912]{0:T(1024)(128)(4,1)}), s8[4194304]{0:T(1024)(128)(4,1)S(1)}, s32[]{:S(2)}) async-start(s8[12582912]{0:T(1024)(128)(4,1)} %bitcast.5), calls=%async_computation.7 | async-start | bytes 8388608
  17.2 4.5 %collective-permute-start.1 = (bf16[2,4,3072]{2,1,0:T(4,128)(2,1)S(1)}, bf16[2,4,3072]{2,1,0:T(4,128)(2,1)S(1)}, u32[]{:S(2)}, u32[]{:S(2)}) collective-permute-start(bf16[2,4,3072]{2,1,0:T(4,128)(2,1)S(1)} %get-tuple-element.24), channel_id=1, source_target_pairs={{0,4},{1,5},{2,6},{3,7},{4,0},{5,1},{6,2},{7,3},{8,12},{9,13},{10,... | collective-permute-start | bytes 147464 | tf_op jit(solution)/shard_map/ppermute | solution.py:333
  17.7 5.2 %collective-permute-start.2 = (bf16[2,4,3072]{2,1,0:T(4,128)(2,1)S(1)}, bf16[2,4,3072]{2,1,0:T(4,128)(2,1)S(1)}, u32[]{:S(2)}, u32[]{:S(2)}) collective-permute-start(bf16[2,4,3072]{2,1,0:T(4,128)(2,1)S(1)} %get-tuple-element.25), channel_id=1, source_target_pairs={{0,8},{1,9},{2,10},{3,11},{4,12},{5,13},{6,14},{7,15},{8,0},{9,1},... | collective-permute-start | bytes 147464 | tf_op jit(solution)/shard_map/ppermute | solution.py:333
  18.4 6.0 %collective-permute-start.3 = (bf16[2,4,3072]{2,1,0:T(4,128)(2,1)S(1)}, bf16[2,4,3072]{2,1,0:T(4,128)(2,1)S(1)}, u32[]{:S(2)}, u32[]{:S(2)}) collective-permute-start(bf16[2,4,3072]{2,1,0:T(4,128)(2,1)S(1)} %get-tuple-element.26), channel_id=1, source_target_pairs={{0,12},{1,13},{2,14},{3,15},{4,8},{5,9},{6,10},{7,11},{8,4},{9,5},... | collective-permute-start | bytes 147464 | tf_op jit(solution)/shard_map/ppermute | solution.py:333
  24.3 15.1 %slice-start.4 = ((s8[12582912]{0:T(1024)(128)(4,1)}), s8[4194304]{0:T(1024)(128)(4,1)S(1)}, s32[]{:S(2)}) async-start(s8[12582912]{0:T(1024)(128)(4,1)} %bitcast.3), calls=%async_computation.5 | async-start | bytes 8388608
  24.3 15.1 %slice-start.7 = ((s8[12582912]{0:T(1024)(128)(4,1)}), s8[4194304]{0:T(1024)(128)(4,1)S(1)}, s32[]{:S(2)}) async-start(s8[12582912]{0:T(1024)(128)(4,1)} %bitcast.5), calls=%async_computation.8 | async-start | bytes 8388608
  25.0 4.2 %collective-permute-start.4 = (bf16[2,4,3200]{2,1,0:T(4,128)(2,1)S(1)}, bf16[2,4,3200]{2,1,0:T(4,128)(2,1)S(1)}, u32[]{:S(2)}, u32[]{:S(2)}) collective-permute-start(bf16[2,4,3200]{2,1,0:T(4,128)(2,1)S(1)} %get-tuple-element.28.sent_ref), channel_id=1, source_target_pairs={{0,2},{1,3},{2,0},{3,1},{4,6},{5,7},{6,4},{7,5},{8,10},{9,11},{10,... | collective-permute-start | bytes 153608 | tf_op jit(solution)/shard_map/ppermute | solution.py:333
  29.2 10.3 %slice-start = ((s8[12582912]{0:T(1024)(128)(4,1)}), s8[4194304]{0:T(1024)(128)(4,1)S(1)}, s32[]{:S(2)}) async-start(s8[12582912]{0:T(1024)(128)(4,1)} %bitcast.1), calls=%async_computation.1 | async-start | bytes 8388608
  29.2 10.3 %slice-start.1 = ((s8[12582912]{0:T(1024)(128)(4,1)}), s8[4194304]{0:T(1024)(128)(4,1)S(1)}, s32[]{:S(2)}) async-start(s8[12582912]{0:T(1024)(128)(4,1)} %bitcast.1), calls=%async_computation.2 | async-start | bytes 8388608
  29.2 10.3 %slice-start.5 = ((s8[12582912]{0:T(1024)(128)(4,1)}), s8[4194304]{0:T(1024)(128)(4,1)S(1)}, s32[]{:S(2)}) async-start(s8[12582912]{0:T(1024)(128)(4,1)} %bitcast.3), calls=%async_computation.6 | async-start | bytes 8388608
  29.2 10.3 %slice-start.8 = ((s8[12582912]{0:T(1024)(128)(4,1)}), s8[4194304]{0:T(1024)(128)(4,1)S(1)}, s32[]{:S(2)}) async-start(s8[12582912]{0:T(1024)(128)(4,1)} %bitcast.5), calls=%async_computation.9 | async-start | bytes 8388608
  29.7 9.8 %slice-start.2 = ((s8[12582912]{0:T(1024)(128)(4,1)}), s8[4194304]{0:T(1024)(128)(4,1)S(1)}, s32[]{:S(2)}) async-start(s8[12582912]{0:T(1024)(128)(4,1)} %bitcast.1), calls=%async_computation.3 | async-start | bytes 8388608
  29.7 5.9 %collective-permute-start.7 = (bf16[2,4,3200]{2,1,0:T(4,128)(2,1)S(1)}, bf16[2,4,3200]{2,1,0:T(4,128)(2,1)S(1)}, u32[]{:S(2)}, u32[]{:S(2)}) collective-permute-start(bf16[2,4,3200]{2,1,0:T(4,128)(2,1)S(1)} %get-tuple-element.30.refs_0_), channel_id=1, source_target_pairs={{0,12},{1,13},{2,14},{3,15},{4,8},{5,9},{6,10},{7,11},{8,4},{9,5},... | collective-permute-start | bytes 153608 | tf_op jit(solution)/shard_map/ppermute | solution.py:333
  32.9 5.0 %collective-permute-start.6 = (bf16[2,4,3200]{2,1,0:T(4,128)(2,1)S(1)}, bf16[2,4,3200]{2,1,0:T(4,128)(2,1)S(1)}, u32[]{:S(2)}, u32[]{:S(2)}) collective-permute-start(bf16[2,4,3200]{2,1,0:T(4,128)(2,1)S(1)} %get-tuple-element.30.refs_0_), channel_id=1, source_target_pairs={{0,8},{1,9},{2,10},{3,11},{4,12},{5,13},{6,14},{7,15},{8,0},{9,1},... | collective-permute-start | bytes 153608 | tf_op jit(solution)/shard_map/ppermute | solution.py:333
  32.9 5.0 %collective-permute-start.5 = (bf16[2,4,3200]{2,1,0:T(4,128)(2,1)S(1)}, bf16[2,4,3200]{2,1,0:T(4,128)(2,1)S(1)}, u32[]{:S(2)}, u32[]{:S(2)}) collective-permute-start(bf16[2,4,3200]{2,1,0:T(4,128)(2,1)S(1)} %get-tuple-element.30.refs_0_), channel_id=1, source_target_pairs={{0,4},{1,5},{2,6},{3,7},{4,0},{5,1},{6,2},{7,3},{8,12},{9,13},{10,... | collective-permute-start | bytes 153608 | tf_op jit(solution)/shard_map/ppermute | solution.py:333
  38.0 1.5 %collective-permute-start.8 = (bf16[8,4,3200]{2,1,0:T(4,128)(2,1)S(1)}, bf16[8,4,3200]{2,1,0:T(4,128)(2,1)S(1)}, u32[]{:S(2)}, u32[]{:S(2)}) collective-permute-start(bf16[8,4,3200]{2,1,0:T(4,128)(2,1)S(1)} %join.1.refs_0_), channel_id=1, source_target_pairs={{0,1},{1,0},{2,3},{3,2},{4,5},{5,4},{6,7},{7,6},{8,9},{9,8},{10,11... | collective-permute-start | bytes 614408 | tf_op jit(solution)/shard_map/ppermute | solution.py:333
  46.3 1.5 %collective-permute-start.9 = (bf16[8,4,3072]{2,1,0:T(4,128)(2,1)S(1)}, bf16[8,4,3072]{2,1,0:T(4,128)(2,1)S(1)}, u32[]{:S(2)}, u32[]{:S(2)}) collective-permute-start(bf16[8,4,3072]{2,1,0:T(4,128)(2,1)S(1)} %get-tuple-element.32), channel_id=1, source_target_pairs={{0,1},{1,0},{2,3},{3,2},{4,5},{5,4},{6,7},{7,6},{8,9},{9,8},{10,11... | collective-permute-start | bytes 589832 | tf_op jit(solution)/shard_map/ppermute | solution.py:333
  47.8 4.7 %collective-permute-start.10 = (bf16[2,4,3072]{2,1,0:T(4,128)(2,1)S(1)}, bf16[2,4,3072]{2,1,0:T(4,128)(2,1)S(1)}, u32[]{:S(2)}, u32[]{:S(2)}) collective-permute-start(bf16[2,4,3072]{2,1,0:T(4,128)(2,1)S(1)} %get-tuple-element.34), channel_id=1, source_target_pairs={{0,4},{1,5},{2,6},{3,7},{4,0},{5,1},{6,2},{7,3},{8,12},{9,13},{10,... | collective-permute-start | bytes 147464 | tf_op jit(solution)/shard_map/ppermute | solution.py:333
  48.2 6.7 %collective-permute-start.11 = (bf16[2,4,3072]{2,1,0:T(4,128)(2,1)S(1)}, bf16[2,4,3072]{2,1,0:T(4,128)(2,1)S(1)}, u32[]{:S(2)}, u32[]{:S(2)}) collective-permute-start(bf16[2,4,3072]{2,1,0:T(4,128)(2,1)S(1)} %get-tuple-element.35), channel_id=1, source_target_pairs={{0,8},{1,9},{2,10},{3,11},{4,12},{5,13},{6,14},{7,15},{8,0},{9,1},... | collective-permute-start | bytes 147464 | tf_op jit(solution)/shard_map/ppermute | solution.py:333
  50.2 6.0 %collective-permute-start.12 = (bf16[2,4,3072]{2,1,0:T(4,128)(2,1)S(1)}, bf16[2,4,3072]{2,1,0:T(4,128)(2,1)S(1)}, u32[]{:S(2)}, u32[]{:S(2)}) collective-permute-start(bf16[2,4,3072]{2,1,0:T(4,128)(2,1)S(1)} %get-tuple-element.36), channel_id=1, source_target_pairs={{0,12},{1,13},{2,14},{3,15},{4,8},{5,9},{6,10},{7,11},{8,4},{9,5},... | collective-permute-start | bytes 147464 | tf_op jit(solution)/shard_map/ppermute | solution.py:333
  56.2 3.9 %collective-permute-start.13 = (bf16[1,4,3072]{2,1,0:T(4,128)(2,1)S(1)}, bf16[1,4,3072]{2,1,0:T(4,128)(2,1)S(1)}, u32[]{:S(2)}, u32[]{:S(2)}) collective-permute-start(bf16[1,4,3072]{2,1,0:T(4,128)(2,1)S(1)} %get-tuple-element.38), channel_id=1, source_target_pairs={{0,2},{1,3},{2,0},{3,1},{4,6},{5,7},{6,4},{7,5},{8,10},{9,11},{10,... | collective-permute-start | bytes 73736 | tf_op jit(solution)/shard_map/ppermute | solution.py:333

commit v7 on v6

--- a/solution.py
+++ b/solution.py
@@ -26,16 +26,17 @@
 
 def attend_kernel(*refs):
     count = (len(refs) - 2) // 2
-    operands, out_ref, buffers, sems = refs[:count], refs[count], refs[count + 1 : -1], refs[-1]
+    operands, out_ref, w_ref = refs[:count], refs[count], refs[count + 1]
+    buffers, sems = refs[count + 2 : -1] + (w_ref,), refs[-1]
     copies = [
         pltpu.make_async_copy(source, target, sems.at[i])
         for i, (source, target) in enumerate(zip(operands, buffers))
     ]
     for copy in copies:
         copy.start()
-    for copy in copies:
+    q_ref, k_ref, nk_ref, len_ref, v_ref, nv_ref, _ = buffers
+    for copy in copies[:4]:
         copy.wait()
-    len_ref, q_ref, nk_ref, k_ref, nv_ref, v_ref = buffers
     batches, sessions = q_ref.shape[:2]
     places = [(m, s) for m in range(batches) for s in range(sessions)]
     cache_len = k_ref.shape[2]
@@ -82,6 +83,8 @@
     total = jnp.sum(mass, axis=1, keepdims=True) + own_mass
     probs = (mass / total).astype(jnp.bfloat16)
     own_prob = (own_mass / total).astype(jnp.bfloat16).astype(jnp.float32)
+    for copy in copies[4:6]:
+        copy.wait()
     wide = jnp.concatenate(
         [
             jnp.dot(
@@ -103,50 +106,7 @@
     devices, _, part = out_ref.shape
     for d in range(devices):
         out_ref[d] = attention[:, d * part : (d + 1) * part]
-
-
-PIECES = 4
-
-
-def fetch_kernel(cuts, *refs):
-    count = len(cuts)
-    sources, targets, token, sems = refs[:count], refs[-count - 2 : -2], refs[-2], refs[-1]
-    token[...] = jnp.zeros(token.shape, token.dtype)
-    copies = []
-    for source, target, cut in zip(sources, targets, cuts):
-        if cut is None:
-            copies.append(pltpu.make_async_copy(source, target, sems.at[len(copies)]))
-        else:
-            size = cut[1] // PIECES
-            for at in range(0, cut[1], size):
-                copies.append(
-                    pltpu.make_async_copy(
-                        source.at[pl.ds(cut[0] + at, size)],
-                        target.at[pl.ds(at, size)],
-                        sems.at[len(copies)],
-                    )
-                )
-    for copy in copies:
-        copy.start()
-    for copy in copies:
-        copy.wait()
-
-
-def fetch(arrays, cuts, after, name):
-    shapes = [a.shape if c is None else (c[1],) + a.shape[1:] for a, c in zip(arrays, cuts)]
-    total = 2 * sum(math.prod(shape) for shape in shapes)
-    copies = sum(1 if c is None else PIECES for c in cuts)
-    return pl.pallas_call(
-        lambda *refs: fetch_kernel(cuts, *refs),
-        in_specs=[HBM] * len(arrays) + [ANY],
-        out_specs=[VMEM] * (len(arrays) + 1),
-        out_shape=[pltpu.VMEM(shape, a.dtype) for shape, a in zip(shapes, arrays)]
-        + [jax.ShapeDtypeStruct((8, LANES), jnp.float32)],
-        scratch_shapes=[pltpu.SemaphoreType.DMA((copies,))],
-        compiler_params=params(8),
-        cost_estimate=pl.CostEstimate(flops=0, bytes_accessed=total, transcendentals=0),
-        name=name,
-    )(*[far(a) for a in arrays], after)
+    copies[6].wait()
 
 
 def far(array):
@@ -403,19 +363,21 @@
     rows = batches * sessions
     units = w_gate.shape[1]
 
-    operands = [lengths, queries, new_keys, cache_keys, new_values, cache_values]
-    heads = pl.pallas_call(
+    operands = [queries, cache_keys, new_keys, lengths, cache_values, new_values, w_out]
+    heads, out_here = pl.pallas_call(
         attend_kernel,
         in_specs=[HBM] * len(operands),
-        out_specs=VMEM,
-        out_shape=jax.ShapeDtypeStruct((devices // 2, rows, 2 * w_out.shape[0]), jnp.bfloat16),
-        scratch_shapes=[pltpu.VMEM(a.shape, a.dtype) for a in operands]
+        out_specs=(VMEM, VMEM),
+        out_shape=(
+            jax.ShapeDtypeStruct((devices // 2, rows, 2 * w_out.shape[0]), jnp.bfloat16),
+            pltpu.VMEM(w_out.shape, w_out.dtype),
+        ),
+        scratch_shapes=[pltpu.VMEM(a.shape, a.dtype) for a in operands[:-1]]
         + [pltpu.SemaphoreType.DMA((len(operands),))],
         compiler_params=params(8),
         name="attend",
     )(*[far(a) for a in operands])
     head_blocks = exchange(heads)
-    (out_here, _) = fetch([w_out], [None], heads, "fetch_out")
     out_other = hop(w_out, 1)
     halves = [jax.ShapeDtypeStruct((devices // 2, rows, features), t) for t in (jnp.float32, jnp.bfloat16)]
     stages = scatter_stages(devices)

time: 61 us -> 60 us (0.984)
  blocking collectives: 0 us -> 13.3 us
  starting transfers between devices: 22.3 us -> 15.5 us
  waiting for transfers between devices: 24.6 us -> 19.8 us
  Pallas kernels: 13.6 us -> 11 us
    all_to_all x0 -> x1, blocking collectives: none -> 13.3 us  [exchange(): lax.all_to_all(blocks, 'dev', split_axis=0, concat_axis=0, axis_index_gro...]
    all_to_all x1 -> x0, starting transfers between devices: 6.87 us -> none  [exchange(): lax.all_to_all(blocks, 'dev', split_axis=0, concat_axis=0, axis_index_gro...]
    all_to_all x1 -> x0, waiting for transfers between devices: 4.75 us -> none  [exchange(): lax.all_to_all(blocks, 'dev', split_axis=0, concat_axis=0, axis_index_gro...]
    pallas_call x2 -> x1, Pallas kernels: 4.41 us -> 1.81 us  [local(): pl.pallas_call(attend_kernel, in_specs=[HBM] * len(operands), out_specs=(...]
  transfers between devices with their start and end apart: 15 -> 14, of which waited for: 12 -> 11; matrix products, arithmetic and copies ran while one was open for 0% -> 0% of each run, Pallas kernels for 7% -> 3%
where the time goes in v7:
time: 60 us; the launch traced here: 59.8 us
  waiting for transfers between devices  19.8 us (33%)
  starting transfers between devices  15.5 us (26%)
  blocking collectives  13.3 us (22%)
  Pallas kernels  11 us (18%)
    ppermute x14, waiting for transfers between devices, hop(): return lax.ppermute(blocks, 'dev', [(i, i ^ mask) for i in range(devices)])  19.8 us
    ppermute x14, starting transfers between devices, hop(): return lax.ppermute(blocks, 'dev', [(i, i ^ mask) for i in range(devices)])  15.5 us
    all_to_all x1, blocking collectives, exchange(): lax.all_to_all(blocks, 'dev', split_axis=0, concat_axis=0, axis_index_gro...  13.3 us
    pallas_call x1, Pallas kernels, local(): pl.pallas_call(lambda *refs: expert_kernel(expert_count, *refs), in_specs...  6.68 us
    pallas_call x1, Pallas kernels, local(): pl.pallas_call(attend_kernel, in_specs=[HBM] * len(operands), out_specs=(...  1.81 us
  transfers between devices with their start and end apart: 14, of which 11 were waited for; matrix products, arithmetic and copies ran while one was open for 0% of the time, Pallas kernels for 3%

profile of v7, /device:TPU:0, one launch (start us, length us, event | category | flops | bytes accessed | tf_op | source)
XLA Modules:
  0.0 59.8 jit_solution(17499675408579969148)
XLA Ops:
  0.0 0.5 collective-permute-start
  0.5 1.8 %attend.1 = (bf16[8,4,384]{2,1,0:T(4,128)(2,1)S(1)}, bf16[192,3072]{1,0:T(8,128)(2,1)S(1)}) custom-call(bf16[2,2,3072]{2,1,0:T(2,128)(2,1)} %refs_0_.3, bf16[2,2,128,512]{3,2,1,0:T(8,128)(2,1)} %refs_1_.2, bf16[2,2,512]{2,1,0:T(2,128)(2,1)} %refs_2_.2, s32[2,2]{1,0:T(2,128)} %refs_3_.3, bf16[2,2,128,512]{3,2,1,0:T(8,128)(2,1)} %refs_4_.3, ...), custom_call_target="tpu_custom_call" | custom-call | tf_op jit(solution)/shard_map/attend/pallas_call | solution.py:367
  2.3 13.3 %all_to_all.5.refs_0_ = bf16[8,4,384]{2,1,0:T(4,128)(2,1)S(1)} all-to-all(bf16[8,4,384]{2,1,0:T(4,128)(2,1)S(1)} %get-tuple-element.23), channel_id=1, replica_groups={{0,2,4,6,8,10,12,14},{1,3,5,7,9,11,13,15},{16,18,20,22,24,26,28,30},{17..., dimensions={0} | all-to-all | bytes 49152 | tf_op jit(solution)/shard_map/all_to_all | solution.py:339
  15.6 0.0 collective-permute-done.refs_2_
  15.6 0.0 slice-start.6
  15.6 0.7 %project.1 = (f32[2,4,3072]{2,1,0:T(4,128)S(1)}, bf16[2,4,3072]{2,1,0:T(4,128)(2,1)S(1)}, bf16[2,4,3072]{2,1,0:T(4,128)(2,1)S(1)}, bf16[2,4,3072]{2,1,0:T(4,128)(2,1)S(1)}) custom-call(bf16[8,4,384]{2,1,0:T(4,128)(2,1)S(1)} %all_to_all.5.refs_0_, bf16[192,3072]{1,0:T(8,128)(2,1)S(1)} %get-tuple-element.24.refs_1_, ...), custom_call_target="tpu_custom_call" | custom-call | tf_op jit(solution)/shard_map/project/pallas_call | solution.py:385
  16.3 0.5 collective-permute-start.1
  16.8 0.7 %collective-permute-start.2 = (bf16[2,4,3072]{2,1,0:T(4,128)(2,1)S(1)}, bf16[2,4,3072]{2,1,0:T(4,128)(2,1)S(1)}, u32[]{:S(2)}, u32[]{:S(2)}) collective-permute-start(bf16[2,4,3072]{2,1,0:T(4,128)(2,1)S(1)} %get-tuple-element.27), channel_id=1, source_target_pairs={{0,8},{1,9},{2,10},{3,11},{4,12},{5,13},{6,14},{7,15},{8,0},{9,1},... | collective-permute-start | bytes 147464 | tf_op jit(solution)/shard_map/ppermute | solution.py:293
  17.4 3.3 %collective-permute-start.3 = (bf16[2,4,3072]{2,1,0:T(4,128)(2,1)S(1)}, bf16[2,4,3072]{2,1,0:T(4,128)(2,1)S(1)}, u32[]{:S(2)}, u32[]{:S(2)}) collective-permute-start(bf16[2,4,3072]{2,1,0:T(4,128)(2,1)S(1)} %get-tuple-element.28), channel_id=1, source_target_pairs={{0,12},{1,13},{2,14},{3,15},{4,8},{5,9},{6,10},{7,11},{8,4},{9,5},... | collective-permute-start | bytes 147464 | tf_op jit(solution)/shard_map/ppermute | solution.py:293
  20.7 0.0 collective-permute-done.1.refs_3_
  20.7 1.2 %collective-permute-done.2.refs_4_ = bf16[2,4,3072]{2,1,0:T(4,128)(2,1)S(1)} collective-permute-done((bf16[2,4,3072]{2,1,0:T(4,128)(2,1)S(1)}, bf16[2,4,3072]{2,1,0:T(4,128)(2,1)S(1)}, u32[]{:S(2)}, u32[]{:S(2)}) %collective-permute-start.2) | collective-permute-done | bytes 49184 | tf_op jit(solution)/shard_map/ppermute | solution.py:293
  22.0 1.4 %collective-permute-done.3.refs_5_ = bf16[2,4,3072]{2,1,0:T(4,128)(2,1)S(1)} collective-permute-done((bf16[2,4,3072]{2,1,0:T(4,128)(2,1)S(1)}, bf16[2,4,3072]{2,1,0:T(4,128)(2,1)S(1)}, u32[]{:S(2)}, u32[]{:S(2)}) %collective-permute-start.3) | collective-permute-done | bytes 49184 | tf_op jit(solution)/shard_map/ppermute | solution.py:293
  23.4 0.0 copy-done.3
  23.4 0.6 %share.1 = (f32[2,4,3072]{2,1,0:T(4,128)S(1)}, bf16[2,4,3200]{2,1,0:T(4,128)(2,1)S(1)}) custom-call(s32[2,2,2]{2,1,0:T(2,128)S(1)} %copy-done.3, bf16[2,2,3072]{2,1,0:T(2,128)(2,1)S(1)} %copy-done, f32[2,4,3072]{2,1,0:T(4,128)S(1)} %get-tuple-element.25.refs_2_, bf16[2,4,3072]{2,1,0:T(4,128)(2,1)S(1)} %collective-permute-done.1.refs_3_, ...), custom_call_target="tpu_custom_call" | custom-call | tf_op jit(solution)/shard_map/share/pallas_call | solution.py:396
  24.1 0.7 %collective-permute-start.4 = (bf16[2,4,3200]{2,1,0:T(4,128)(2,1)S(1)}, bf16[2,4,3200]{2,1,0:T(4,128)(2,1)S(1)}, u32[]{:S(2)}, u32[]{:S(2)}) collective-permute-start(bf16[2,4,3200]{2,1,0:T(4,128)(2,1)S(1)} %get-tuple-element.30.sent_ref), channel_id=1, source_target_pairs={{0,2},{1,3},{2,0},{3,1},{4,6},{5,7},{6,4},{7,5},{8,10},{9,11},{10,... | collective-permute-start | bytes 153608 | tf_op jit(solution)/shard_map/ppermute | solution.py:293
  24.8 3.5 %collective-permute-done.4.got_ref = bf16[2,4,3200]{2,1,0:T(4,128)(2,1)S(1)} collective-permute-done((bf16[2,4,3200]{2,1,0:T(4,128)(2,1)S(1)}, bf16[2,4,3200]{2,1,0:T(4,128)(2,1)S(1)}, u32[]{:S(2)}, u32[]{:S(2)}) %collective-permute-start.4) | collective-permute-done | bytes 51232 | tf_op jit(solution)/shard_map/ppermute | solution.py:293
  28.2 0.0 copy-done.2
  28.2 0.0 slice-start.5
  28.3 0.0 slice-start.8
  28.3 0.5 norm.1
  28.8 3.2 %collective-permute-start.7 = (bf16[2,4,3200]{2,1,0:T(4,128)(2,1)S(1)}, bf16[2,4,3200]{2,1,0:T(4,128)(2,1)S(1)}, u32[]{:S(2)}, u32[]{:S(2)}) collective-permute-start(bf16[2,4,3200]{2,1,0:T(4,128)(2,1)S(1)} %get-tuple-element.32.refs_0_), channel_id=1, source_target_pairs={{0,12},{1,13},{2,14},{3,15},{4,8},{5,9},{6,10},{7,11},{8,4},{9,5},... | collective-permute-start | bytes 153608 | tf_op jit(solution)/shard_map/ppermute | solution.py:293
  32.0 0.0 collective-permute-start.6
  32.0 1.2 %collective-permute-start.5 = (bf16[2,4,3200]{2,1,0:T(4,128)(2,1)S(1)}, bf16[2,4,3200]{2,1,0:T(4,128)(2,1)S(1)}, u32[]{:S(2)}, u32[]{:S(2)}) collective-permute-start(bf16[2,4,3200]{2,1,0:T(4,128)(2,1)S(1)} %get-tuple-element.32.refs_0_), channel_id=1, source_target_pairs={{0,4},{1,5},{2,6},{3,7},{4,0},{5,1},{6,2},{7,3},{8,12},{9,13},{10,... | collective-permute-start | bytes 153608 | tf_op jit(solution)/shard_map/ppermute | solution.py:293
  33.2 1.5 %collective-permute-done.7.refs_3_ = bf16[2,4,3200]{2,1,0:T(4,128)(2,1)S(1)} collective-permute-done((bf16[2,4,3200]{2,1,0:T(4,128)(2,1)S(1)}, bf16[2,4,3200]{2,1,0:T(4,128)(2,1)S(1)}, u32[]{:S(2)}, u32[]{:S(2)}) %collective-permute-start.7) | collective-permute-done | bytes 51232 | tf_op jit(solution)/shard_map/ppermute | solution.py:293
  34.7 2.3 %collective-permute-done.6.refs_2_ = bf16[2,4,3200]{2,1,0:T(4,128)(2,1)S(1)} collective-permute-done((bf16[2,4,3200]{2,1,0:T(4,128)(2,1)S(1)}, bf16[2,4,3200]{2,1,0:T(4,128)(2,1)S(1)}, u32[]{:S(2)}, u32[]{:S(2)}) %collective-permute-start.6) | collective-permute-done | bytes 51232 | tf_op jit(solution)/shard_map/ppermute | solution.py:293
  37.0 0.0 collective-permute-done.5.refs_1_
  37.0 0.1 collective-permute-start.8
  37.1 1.4 %collective-permute-done.8.refs_1_ = bf16[8,4,3200]{2,1,0:T(4,128)(2,1)S(1)} collective-permute-done((bf16[8,4,3200]{2,1,0:T(4,128)(2,1)S(1)}, bf16[8,4,3200]{2,1,0:T(4,128)(2,1)S(1)}, u32[]{:S(2)}, u32[]{:S(2)}) %collective-permute-start.8) | collective-permute-done | bytes 204832 | tf_op jit(solution)/shard_map/ppermute | solution.py:293
  38.5 0.0 slice-done.4
  38.6 0.0 slice-done.7
  38.6 0.0 slice-done
  38.6 0.0 slice-done.1
  38.6 0.0 slice-done.5
  38.6 0.0 slice-done.8
  38.6 0.0 slice-done.2
  38.6 6.7 %experts.1 = (f32[8,4,3072]{2,1,0:T(4,128)S(1)}, bf16[8,4,3072]{2,1,0:T(4,128)(2,1)S(1)}) custom-call(bf16[8,4,3200]{2,1,0:T(4,128)(2,1)S(1)} %join.1.refs_0_, bf16[8,4,3200]{2,1,0:T(4,128)(2,1)S(1)} %collective-permute-done.8.refs_1_, bf16[3072,2048]{1,0:T(8,128)(2,1)S(1)} %bitcast.2, bf16[3072,2048]{1,0:T(8,128)(2,1)S(1)} %bitcast.4, ...), custom_call_target="tpu_custom_call" | custom-call | tf_op jit(solution)/shard_map/experts/pallas_call | solution.py:413
  45.3 0.2 collective-permute-start.9
  45.5 1.3 %collective-permute-done.9.refs_1_ = bf16[8,4,3072]{2,1,0:T(4,128)(2,1)S(1)} collective-permute-done((bf16[8,4,3072]{2,1,0:T(4,128)(2,1)S(1)}, bf16[8,4,3072]{2,1,0:T(4,128)(2,1)S(1)}, u32[]{:S(2)}, u32[]{:S(2)}) %collective-permute-start.9) | collective-permute-done | bytes 196640 | tf_op jit(solution)/shard_map/ppermute | solution.py:293
  46.8 0.1 fold.2
  46.9 0.4 collective-permute-start.10
  47.3 2.0 %collective-permute-start.11 = (bf16[2,4,3072]{2,1,0:T(4,128)(2,1)S(1)}, bf16[2,4,3072]{2,1,0:T(4,128)(2,1)S(1)}, u32[]{:S(2)}, u32[]{:S(2)}) collective-permute-start(bf16[2,4,3072]{2,1,0:T(4,128)(2,1)S(1)} %get-tuple-element.37), channel_id=1, source_target_pairs={{0,8},{1,9},{2,10},{3,11},{4,12},{5,13},{6,14},{7,15},{8,0},{9,1},... | collective-permute-start | bytes 147464 | tf_op jit(solution)/shard_map/ppermute | solution.py:293
  49.3 2.1 %collective-permute-start.12 = (bf16[2,4,3072]{2,1,0:T(4,128)(2,1)S(1)}, bf16[2,4,3072]{2,1,0:T(4,128)(2,1)S(1)}, u32[]{:S(2)}, u32[]{:S(2)}) collective-permute-start(bf16[2,4,3072]{2,1,0:T(4,128)(2,1)S(1)} %get-tuple-element.38), channel_id=1, source_target_pairs={{0,12},{1,13},{2,14},{3,15},{4,8},{5,9},{6,10},{7,11},{8,4},{9,5},... | collective-permute-start | bytes 147464 | tf_op jit(solution)/shard_map/ppermute | solution.py:293
  51.4 0.2 collective-permute-done.10.refs_1_
  51.6 2.4 %collective-permute-done.11.refs_2_ = bf16[2,4,3072]{2,1,0:T(4,128)(2,1)S(1)} collective-permute-done((bf16[2,4,3072]{2,1,0:T(4,128)(2,1)S(1)}, bf16[2,4,3072]{2,1,0:T(4,128)(2,1)S(1)}, u32[]{:S(2)}, u32[]{:S(2)}) %collective-permute-start.11) | collective-permute-done | bytes 49184 | tf_op jit(solution)/shard_map/ppermute | solution.py:293
  54.0 1.3 %collective-permute-done.12.refs_3_ = bf16[2,4,3072]{2,1,0:T(4,128)(2,1)S(1)} collective-permute-done((bf16[2,4,3072]{2,1,0:T(4,128)(2,1)S(1)}, bf16[2,4,3072]{2,1,0:T(4,128)(2,1)S(1)}, u32[]{:S(2)}, u32[]{:S(2)}) %collective-permute-start.12) | collective-permute-done | bytes 49184 | tf_op jit(solution)/shard_map/ppermute | solution.py:293
  55.3 0.7 %collective-permute-start.13 = (bf16[1,4,3072]{2,1,0:T(4,128)(2,1)S(1)}, bf16[1,4,3072]{2,1,0:T(4,128)(2,1)S(1)}, u32[]{:S(2)}, u32[]{:S(2)}) collective-permute-start(bf16[1,4,3072]{2,1,0:T(4,128)(2,1)S(1)} %get-tuple-element.40), channel_id=1, source_target_pairs={{0,2},{1,3},{2,0},{3,1},{4,6},{5,7},{6,4},{7,5},{8,10},{9,11},{10,... | collective-permute-start | bytes 73736 | tf_op jit(solution)/shard_map/ppermute | solution.py:293
  56.0 3.2 %collective-permute-done.13.refs_2_ = bf16[1,4,3072]{2,1,0:T(4,128)(2,1)S(1)} collective-permute-done((bf16[1,4,3072]{2,1,0:T(4,128)(2,1)S(1)}, bf16[1,4,3072]{2,1,0:T(4,128)(2,1)S(1)}, u32[]{:S(2)}, u32[]{:S(2)}) %collective-permute-start.13) | collective-permute-done | bytes 24608 | tf_op jit(solution)/shard_map/ppermute | solution.py:293
  59.2 0.6 %final.1 = bf16[2,2,3072]{2,1,0:T(2,128)(2,1)} custom-call(f32[4,3072]{1,0:T(4,128)S(1)} %get-tuple-element.31.refs_0_, f32[1,4,3072]{2,1,0:T(4,128)S(1)} %get-tuple-element.39.refs_1_, bf16[1,4,3072]{2,1,0:T(4,128)(2,1)S(1)} %collective-permute-done.13.refs_2_), custom_call_target="tpu_custom_call" | custom-call | tf_op jit(solution)/shard_map/final/pallas_call | solution.py:425
  (19 shorter events, 0.1 us)
Async XLA Ops:
  0.0 23.4 %copy-start.3 = (s32[2,2,2]{2,1,0:T(2,128)S(1)}, s32[2,2,2]{2,1,0:T(2,128)}, u32[]{:S(2)}) copy-start(s32[2,2,2]{2,1,0:T(2,128)} %refs_0_.4) | copy-start | bytes 100
  0.0 23.4 %copy-start = (bf16[2,2,3072]{2,1,0:T(2,128)(2,1)S(1)}, bf16[2,2,3072]{2,1,0:T(2,128)(2,1)}, u32[]{:S(2)}) copy-start(bf16[2,2,3072]{2,1,0:T(2,128)(2,1)} %refs_1_.3) | copy-start | bytes 73732
  0.0 15.6 %collective-permute-start = (bf16[192,3072]{1,0:T(8,128)(2,1)}, bf16[192,3072]{1,0:T(8,128)(2,1)S(1)}, u32[]{:S(2)}, u32[]{:S(2)}) collective-permute-start(bf16[192,3072]{1,0:T(8,128)(2,1)} %refs_6_.2), channel_id=1, source_target_pairs={{0,1},{1,0},{2,3},{3,2},{4,5},{5,4},{6,7},{7,6},{8,9},{9,8},{10,11... | collective-permute-start | bytes 3538952 | tf_op jit(solution)/shard_map/ppermute | solution.py:293
  15.6 12.7 %copy-start.1 = (bf16[3072,4]{0,1:T(4,128)(2,1)S(1)}, bf16[3072,4]{0,1:T(4,128)(2,1)}, u32[]{:S(2)}) copy-start(bf16[3072,4]{0,1:T(4,128)(2,1)} %param.23) | copy-start | bytes 73732
  15.6 12.7 %copy-start.2 = (bf16[3072]{0:T(1024)(128)(2,1)S(1)}, bf16[3072]{0:T(1024)(128)(2,1)}, u32[]{:S(2)}) copy-start(bf16[3072]{0:T(1024)(128)(2,1)} %gain_ref.1) | copy-start | bytes 18436
  15.6 23.0 %slice-start.3 = ((s8[12582912]{0:T(1024)(128)(4,1)}), s8[4194304]{0:T(1024)(128)(4,1)S(1)}, s32[]{:S(2)}) async-start(s8[12582912]{0:T(1024)(128)(4,1)} %bitcast.3), calls=%async_computation.4 | async-start | bytes 8388608
  15.6 23.0 %slice-start.6 = ((s8[12582912]{0:T(1024)(128)(4,1)}), s8[4194304]{0:T(1024)(128)(4,1)S(1)}, s32[]{:S(2)}) async-start(s8[12582912]{0:T(1024)(128)(4,1)} %bitcast.5), calls=%async_computation.7 | async-start | bytes 8388608
  16.3 4.5 %collective-permute-start.1 = (bf16[2,4,3072]{2,1,0:T(4,128)(2,1)S(1)}, bf16[2,4,3072]{2,1,0:T(4,128)(2,1)S(1)}, u32[]{:S(2)}, u32[]{:S(2)}) collective-permute-start(bf16[2,4,3072]{2,1,0:T(4,128)(2,1)S(1)} %get-tuple-element.26), channel_id=1, source_target_pairs={{0,4},{1,5},{2,6},{3,7},{4,0},{5,1},{6,2},{7,3},{8,12},{9,13},{10,... | collective-permute-start | bytes 147464 | tf_op jit(solution)/shard_map/ppermute | solution.py:293
  16.8 5.2 %collective-permute-start.2 = (bf16[2,4,3072]{2,1,0:T(4,128)(2,1)S(1)}, bf16[2,4,3072]{2,1,0:T(4,128)(2,1)S(1)}, u32[]{:S(2)}, u32[]{:S(2)}) collective-permute-start(bf16[2,4,3072]{2,1,0:T(4,128)(2,1)S(1)} %get-tuple-element.27), channel_id=1, source_target_pairs={{0,8},{1,9},{2,10},{3,11},{4,12},{5,13},{6,14},{7,15},{8,0},{9,1},... | collective-permute-start | bytes 147464 | tf_op jit(solution)/shard_map/ppermute | solution.py:293
  17.4 6.0 %collective-permute-start.3 = (bf16[2,4,3072]{2,1,0:T(4,128)(2,1)S(1)}, bf16[2,4,3072]{2,1,0:T(4,128)(2,1)S(1)}, u32[]{:S(2)}, u32[]{:S(2)}) collective-permute-start(bf16[2,4,3072]{2,1,0:T(4,128)(2,1)S(1)} %get-tuple-element.28), channel_id=1, source_target_pairs={{0,12},{1,13},{2,14},{3,15},{4,8},{5,9},{6,10},{7,11},{8,4},{9,5},... | collective-permute-start | bytes 147464 | tf_op jit(solution)/shard_map/ppermute | solution.py:293
  23.4 15.1 %slice-start.4 = ((s8[12582912]{0:T(1024)(128)(4,1)}), s8[4194304]{0:T(1024)(128)(4,1)S(1)}, s32[]{:S(2)}) async-start(s8[12582912]{0:T(1024)(128)(4,1)} %bitcast.3), calls=%async_computation.5 | async-start | bytes 8388608
  23.4 15.1 %slice-start.7 = ((s8[12582912]{0:T(1024)(128)(4,1)}), s8[4194304]{0:T(1024)(128)(4,1)S(1)}, s32[]{:S(2)}) async-start(s8[12582912]{0:T(1024)(128)(4,1)} %bitcast.5), calls=%async_computation.8 | async-start | bytes 8388608
  24.1 4.2 %collective-permute-start.4 = (bf16[2,4,3200]{2,1,0:T(4,128)(2,1)S(1)}, bf16[2,4,3200]{2,1,0:T(4,128)(2,1)S(1)}, u32[]{:S(2)}, u32[]{:S(2)}) collective-permute-start(bf16[2,4,3200]{2,1,0:T(4,128)(2,1)S(1)} %get-tuple-element.30.sent_ref), channel_id=1, source_target_pairs={{0,2},{1,3},{2,0},{3,1},{4,6},{5,7},{6,4},{7,5},{8,10},{9,11},{10,... | collective-permute-start | bytes 153608 | tf_op jit(solution)/shard_map/ppermute | solution.py:293
  28.2 10.3 %slice-start = ((s8[12582912]{0:T(1024)(128)(4,1)}), s8[4194304]{0:T(1024)(128)(4,1)S(1)}, s32[]{:S(2)}) async-start(s8[12582912]{0:T(1024)(128)(4,1)} %bitcast.1), calls=%async_computation.1 | async-start | bytes 8388608
  28.2 10.3 %slice-start.1 = ((s8[12582912]{0:T(1024)(128)(4,1)}), s8[4194304]{0:T(1024)(128)(4,1)S(1)}, s32[]{:S(2)}) async-start(s8[12582912]{0:T(1024)(128)(4,1)} %bitcast.1), calls=%async_computation.2 | async-start | bytes 8388608
  28.2 10.3 %slice-start.5 = ((s8[12582912]{0:T(1024)(128)(4,1)}), s8[4194304]{0:T(1024)(128)(4,1)S(1)}, s32[]{:S(2)}) async-start(s8[12582912]{0:T(1024)(128)(4,1)} %bitcast.3), calls=%async_computation.6 | async-start | bytes 8388608
  28.3 10.3 %slice-start.8 = ((s8[12582912]{0:T(1024)(128)(4,1)}), s8[4194304]{0:T(1024)(128)(4,1)S(1)}, s32[]{:S(2)}) async-start(s8[12582912]{0:T(1024)(128)(4,1)} %bitcast.5), calls=%async_computation.9 | async-start | bytes 8388608
  28.8 9.8 %slice-start.2 = ((s8[12582912]{0:T(1024)(128)(4,1)}), s8[4194304]{0:T(1024)(128)(4,1)S(1)}, s32[]{:S(2)}) async-start(s8[12582912]{0:T(1024)(128)(4,1)} %bitcast.1), calls=%async_computation.3 | async-start | bytes 8388608
  28.8 5.9 %collective-permute-start.7 = (bf16[2,4,3200]{2,1,0:T(4,128)(2,1)S(1)}, bf16[2,4,3200]{2,1,0:T(4,128)(2,1)S(1)}, u32[]{:S(2)}, u32[]{:S(2)}) collective-permute-start(bf16[2,4,3200]{2,1,0:T(4,128)(2,1)S(1)} %get-tuple-element.32.refs_0_), channel_id=1, source_target_pairs={{0,12},{1,13},{2,14},{3,15},{4,8},{5,9},{6,10},{7,11},{8,4},{9,5},... | collective-permute-start | bytes 153608 | tf_op jit(solution)/shard_map/ppermute | solution.py:293
  32.0 5.0 %collective-permute-start.6 = (bf16[2,4,3200]{2,1,0:T(4,128)(2,1)S(1)}, bf16[2,4,3200]{2,1,0:T(4,128)(2,1)S(1)}, u32[]{:S(2)}, u32[]{:S(2)}) collective-permute-start(bf16[2,4,3200]{2,1,0:T(4,128)(2,1)S(1)} %get-tuple-element.32.refs_0_), channel_id=1, source_target_pairs={{0,8},{1,9},{2,10},{3,11},{4,12},{5,13},{6,14},{7,15},{8,0},{9,1},... | collective-permute-start | bytes 153608 | tf_op jit(solution)/shard_map/ppermute | solution.py:293
  32.0 5.0 %collective-permute-start.5 = (bf16[2,4,3200]{2,1,0:T(4,128)(2,1)S(1)}, bf16[2,4,3200]{2,1,0:T(4,128)(2,1)S(1)}, u32[]{:S(2)}, u32[]{:S(2)}) collective-permute-start(bf16[2,4,3200]{2,1,0:T(4,128)(2,1)S(1)} %get-tuple-element.32.refs_0_), channel_id=1, source_target_pairs={{0,4},{1,5},{2,6},{3,7},{4,0},{5,1},{6,2},{7,3},{8,12},{9,13},{10,... | collective-permute-start | bytes 153608 | tf_op jit(solution)/shard_map/ppermute | solution.py:293
  37.0 1.5 %collective-permute-start.8 = (bf16[8,4,3200]{2,1,0:T(4,128)(2,1)S(1)}, bf16[8,4,3200]{2,1,0:T(4,128)(2,1)S(1)}, u32[]{:S(2)}, u32[]{:S(2)}) collective-permute-start(bf16[8,4,3200]{2,1,0:T(4,128)(2,1)S(1)} %join.1.refs_0_), channel_id=1, source_target_pairs={{0,1},{1,0},{2,3},{3,2},{4,5},{5,4},{6,7},{7,6},{8,9},{9,8},{10,11... | collective-permute-start | bytes 614408 | tf_op jit(solution)/shard_map/ppermute | solution.py:293
  45.3 1.5 %collective-permute-start.9 = (bf16[8,4,3072]{2,1,0:T(4,128)(2,1)S(1)}, bf16[8,4,3072]{2,1,0:T(4,128)(2,1)S(1)}, u32[]{:S(2)}, u32[]{:S(2)}) collective-permute-start(bf16[8,4,3072]{2,1,0:T(4,128)(2,1)S(1)} %get-tuple-element.34), channel_id=1, source_target_pairs={{0,1},{1,0},{2,3},{3,2},{4,5},{5,4},{6,7},{7,6},{8,9},{9,8},{10,11... | collective-permute-start | bytes 589832 | tf_op jit(solution)/shard_map/ppermute | solution.py:293
  46.9 4.7 %collective-permute-start.10 = (bf16[2,4,3072]{2,1,0:T(4,128)(2,1)S(1)}, bf16[2,4,3072]{2,1,0:T(4,128)(2,1)S(1)}, u32[]{:S(2)}, u32[]{:S(2)}) collective-permute-start(bf16[2,4,3072]{2,1,0:T(4,128)(2,1)S(1)} %get-tuple-element.36), channel_id=1, source_target_pairs={{0,4},{1,5},{2,6},{3,7},{4,0},{5,1},{6,2},{7,3},{8,12},{9,13},{10,... | collective-permute-start | bytes 147464 | tf_op jit(solution)/shard_map/ppermute | solution.py:293
  47.3 6.7 %collective-permute-start.11 = (bf16[2,4,3072]{2,1,0:T(4,128)(2,1)S(1)}, bf16[2,4,3072]{2,1,0:T(4,128)(2,1)S(1)}, u32[]{:S(2)}, u32[]{:S(2)}) collective-permute-start(bf16[2,4,3072]{2,1,0:T(4,128)(2,1)S(1)} %get-tuple-element.37), channel_id=1, source_target_pairs={{0,8},{1,9},{2,10},{3,11},{4,12},{5,13},{6,14},{7,15},{8,0},{9,1},... | collective-permute-start | bytes 147464 | tf_op jit(solution)/shard_map/ppermute | solution.py:293
  49.3 6.0 %collective-permute-start.12 = (bf16[2,4,3072]{2,1,0:T(4,128)(2,1)S(1)}, bf16[2,4,3072]{2,1,0:T(4,128)(2,1)S(1)}, u32[]{:S(2)}, u32[]{:S(2)}) collective-permute-start(bf16[2,4,3072]{2,1,0:T(4,128)(2,1)S(1)} %get-tuple-element.38), channel_id=1, source_target_pairs={{0,12},{1,13},{2,14},{3,15},{4,8},{5,9},{6,10},{7,11},{8,4},{9,5},... | collective-permute-start | bytes 147464 | tf_op jit(solution)/shard_map/ppermute | solution.py:293
  55.3 3.9 %collective-permute-start.13 = (bf16[1,4,3072]{2,1,0:T(4,128)(2,1)S(1)}, bf16[1,4,3072]{2,1,0:T(4,128)(2,1)S(1)}, u32[]{:S(2)}, u32[]{:S(2)}) collective-permute-start(bf16[1,4,3072]{2,1,0:T(4,128)(2,1)S(1)} %get-tuple-element.40), channel_id=1, source_target_pairs={{0,2},{1,3},{2,0},{3,1},{4,6},{5,7},{6,4},{7,5},{8,10},{9,11},{10,... | collective-permute-start | bytes 73736 | tf_op jit(solution)/shard_map/ppermute | solution.py:293

commit v8 on v7

--- a/solution.py
+++ b/solution.py
@@ -15,9 +15,7 @@
 MIB = 1 << 20
 
 VMEM = pl.BlockSpec(memory_space=pltpu.VMEM)
-SMEM = pl.BlockSpec(memory_space=pltpu.SMEM)
 HBM = pl.BlockSpec(memory_space=pltpu.HBM)
-ANY = pl.BlockSpec(memory_space=pl.ANY)
 
 
 def params(mib):
@@ -181,14 +179,11 @@
     total = total_of(refs[:count])
     x_rows = jnp.concatenate([x_ref[m].astype(jnp.float32) for m in range(batches)], axis=0)
     own = total[0] + x_rows
-    row = lax.broadcasted_iota(jnp.int32, (rows, LANES), 0)
     column = lax.broadcasted_iota(jnp.int32, (rows, LANES), 1)
+    routes = jnp.concatenate([idx_ref[m] for m in range(batches)], axis=0)
     member = jnp.zeros((rows, LANES), jnp.float32)
-    for m in range(batches):
-        for s in range(sessions):
-            for k in range(idx_ref.shape[2]):
-                hit = (row == m * sessions + s) & (column == idx_ref[m, s, k])
-                member = jnp.where(hit, 1.0, member)
+    for k in range(routes.shape[1]):
+        member = jnp.where(column == routes[:, k : k + 1], 1.0, member)
     keep_ref[0] = own
     keep_ref[1] = total[1]
     out_ref[0, :, :features] = own.astype(jnp.bfloat16)
@@ -395,12 +390,12 @@
     wide = jax.ShapeDtypeStruct((2, rows, features + LANES), jnp.bfloat16)
     keep, send = pl.pallas_call(
         lambda *refs: share_kernel(len(attn_parts), *refs),
-        in_specs=[SMEM] + [VMEM] * (1 + len(attn_parts)) + [HBM],
+        in_specs=[VMEM] * (2 + len(attn_parts)) + [HBM],
         out_specs=(VMEM, VMEM),
         out_shape=(jax.ShapeDtypeStruct((2, rows, features), jnp.float32), wide),
         compiler_params=params(8),
         name="share",
-    )(experts_idx, here(x_in), *attn_parts, far(w_gate))
+    )(here(experts_idx), here(x_in), *attn_parts, far(w_gate))
     resid, message = pl.pallas_call(
         norm_kernel,
         in_specs=[VMEM] * 5 + [HBM],

time: 60 us -> 59.4 us (0.990)
  no operation moved by 1% of the time
where the time goes in v8:
time: 59.4 us; the launch traced here: 59.3 us
  waiting for transfers between devices  19.8 us (33%)
  starting transfers between devices  15.4 us (26%)
  blocking collectives  13.3 us (22%)
  Pallas kernels  10.5 us (18%)
    ppermute x14, waiting for transfers between devices, hop(): return lax.ppermute(blocks, 'dev', [(i, i ^ mask) for i in range(devices)])  19.8 us
    ppermute x14, starting transfers between devices, hop(): return lax.ppermute(blocks, 'dev', [(i, i ^ mask) for i in range(devices)])  15.4 us
    all_to_all x1, blocking collectives, exchange(): lax.all_to_all(blocks, 'dev', split_axis=0, concat_axis=0, axis_index_gro...  13.3 us
    pallas_call x1, Pallas kernels, local(): pl.pallas_call(lambda *refs: expert_kernel(expert_count, *refs), in_specs...  6.68 us
    pallas_call x1, Pallas kernels, local(): pl.pallas_call(attend_kernel, in_specs=[HBM] * len(operands), out_specs=(...  1.81 us
  transfers between devices with their start and end apart: 14, of which 11 were waited for; matrix products, arithmetic and copies ran while one was open for 0% of the time, Pallas kernels for 3%

profile of v8, /device:TPU:0, one launch (start us, length us, event | category | flops | bytes accessed | tf_op | source)
XLA Modules:
  0.0 59.3 jit_solution(7156744811244489796)
XLA Ops:
  0.0 0.5 collective-permute-start
  0.5 1.8 %attend.1 = (bf16[8,4,384]{2,1,0:T(4,128)(2,1)S(1)}, bf16[192,3072]{1,0:T(8,128)(2,1)S(1)}) custom-call(bf16[2,2,3072]{2,1,0:T(2,128)(2,1)} %refs_0_.3, bf16[2,2,128,512]{3,2,1,0:T(8,128)(2,1)} %refs_1_.2, bf16[2,2,512]{2,1,0:T(2,128)(2,1)} %refs_2_.2, s32[2,2]{1,0:T(2,128)} %refs_3_.3, bf16[2,2,128,512]{3,2,1,0:T(8,128)(2,1)} %refs_4_.3, ...), custom_call_target="tpu_custom_call" | custom-call | tf_op jit(solution)/shard_map/attend/pallas_call | solution.py:362
  2.3 13.3 %all_to_all.5.refs_0_ = bf16[8,4,384]{2,1,0:T(4,128)(2,1)S(1)} all-to-all(bf16[8,4,384]{2,1,0:T(4,128)(2,1)S(1)} %get-tuple-element.23), channel_id=1, replica_groups={{0,2,4,6,8,10,12,14},{1,3,5,7,9,11,13,15},{16,18,20,22,24,26,28,30},{17..., dimensions={0} | all-to-all | bytes 49152 | tf_op jit(solution)/shard_map/all_to_all | solution.py:334
  15.6 0.0 collective-permute-done.refs_2_
  15.6 0.0 slice-start.6
  15.6 0.7 %project.1 = (f32[2,4,3072]{2,1,0:T(4,128)S(1)}, bf16[2,4,3072]{2,1,0:T(4,128)(2,1)S(1)}, bf16[2,4,3072]{2,1,0:T(4,128)(2,1)S(1)}, bf16[2,4,3072]{2,1,0:T(4,128)(2,1)S(1)}) custom-call(bf16[8,4,384]{2,1,0:T(4,128)(2,1)S(1)} %all_to_all.5.refs_0_, bf16[192,3072]{1,0:T(8,128)(2,1)S(1)} %get-tuple-element.24.refs_1_, ...), custom_call_target="tpu_custom_call" | custom-call | tf_op jit(solution)/shard_map/project/pallas_call | solution.py:380
  16.3 0.5 collective-permute-start.1
  16.8 0.7 %collective-permute-start.2 = (bf16[2,4,3072]{2,1,0:T(4,128)(2,1)S(1)}, bf16[2,4,3072]{2,1,0:T(4,128)(2,1)S(1)}, u32[]{:S(2)}, u32[]{:S(2)}) collective-permute-start(bf16[2,4,3072]{2,1,0:T(4,128)(2,1)S(1)} %get-tuple-element.27), channel_id=1, source_target_pairs={{0,8},{1,9},{2,10},{3,11},{4,12},{5,13},{6,14},{7,15},{8,0},{9,1},... | collective-permute-start | bytes 147464 | tf_op jit(solution)/shard_map/ppermute | solution.py:288
  17.4 3.3 %collective-permute-start.3 = (bf16[2,4,3072]{2,1,0:T(4,128)(2,1)S(1)}, bf16[2,4,3072]{2,1,0:T(4,128)(2,1)S(1)}, u32[]{:S(2)}, u32[]{:S(2)}) collective-permute-start(bf16[2,4,3072]{2,1,0:T(4,128)(2,1)S(1)} %get-tuple-element.28), channel_id=1, source_target_pairs={{0,12},{1,13},{2,14},{3,15},{4,8},{5,9},{6,10},{7,11},{8,4},{9,5},... | collective-permute-start | bytes 147464 | tf_op jit(solution)/shard_map/ppermute | solution.py:288
  20.7 0.0 collective-permute-done.1.refs_3_
  20.7 1.2 %collective-permute-done.2.refs_4_ = bf16[2,4,3072]{2,1,0:T(4,128)(2,1)S(1)} collective-permute-done((bf16[2,4,3072]{2,1,0:T(4,128)(2,1)S(1)}, bf16[2,4,3072]{2,1,0:T(4,128)(2,1)S(1)}, u32[]{:S(2)}, u32[]{:S(2)}) %collective-permute-start.2) | collective-permute-done | bytes 49184 | tf_op jit(solution)/shard_map/ppermute | solution.py:288
  22.0 1.4 %collective-permute-done.3.refs_5_ = bf16[2,4,3072]{2,1,0:T(4,128)(2,1)S(1)} collective-permute-done((bf16[2,4,3072]{2,1,0:T(4,128)(2,1)S(1)}, bf16[2,4,3072]{2,1,0:T(4,128)(2,1)S(1)}, u32[]{:S(2)}, u32[]{:S(2)}) %collective-permute-start.3) | collective-permute-done | bytes 49184 | tf_op jit(solution)/shard_map/ppermute | solution.py:288
  23.4 0.0 copy-done.3
  23.4 0.0 copy-done
  23.4 0.1 share.1
  23.5 0.7 %collective-permute-start.4 = (bf16[2,4,3200]{2,1,0:T(4,128)(2,1)S(1)}, bf16[2,4,3200]{2,1,0:T(4,128)(2,1)S(1)}, u32[]{:S(2)}, u32[]{:S(2)}) collective-permute-start(bf16[2,4,3200]{2,1,0:T(4,128)(2,1)S(1)} %get-tuple-element.30.sent_ref), channel_id=1, source_target_pairs={{0,2},{1,3},{2,0},{3,1},{4,6},{5,7},{6,4},{7,5},{8,10},{9,11},{10,... | collective-permute-start | bytes 153608 | tf_op jit(solution)/shard_map/ppermute | solution.py:288
  24.2 3.5 %collective-permute-done.4.got_ref = bf16[2,4,3200]{2,1,0:T(4,128)(2,1)S(1)} collective-permute-done((bf16[2,4,3200]{2,1,0:T(4,128)(2,1)S(1)}, bf16[2,4,3200]{2,1,0:T(4,128)(2,1)S(1)}, u32[]{:S(2)}, u32[]{:S(2)}) %collective-permute-start.4) | collective-permute-done | bytes 51232 | tf_op jit(solution)/shard_map/ppermute | solution.py:288
  27.7 0.0 copy-done.1
  27.7 0.0 copy-done.2
  27.7 0.0 slice-start.5
  27.7 0.0 slice-start.8
  27.7 0.5 norm.1
  28.2 3.2 %collective-permute-start.7 = (bf16[2,4,3200]{2,1,0:T(4,128)(2,1)S(1)}, bf16[2,4,3200]{2,1,0:T(4,128)(2,1)S(1)}, u32[]{:S(2)}, u32[]{:S(2)}) collective-permute-start(bf16[2,4,3200]{2,1,0:T(4,128)(2,1)S(1)} %get-tuple-element.32.refs_0_), channel_id=1, source_target_pairs={{0,12},{1,13},{2,14},{3,15},{4,8},{5,9},{6,10},{7,11},{8,4},{9,5},... | collective-permute-start | bytes 153608 | tf_op jit(solution)/shard_map/ppermute | solution.py:288
  31.4 0.0 collective-permute-start.6
  31.4 1.2 %collective-permute-start.5 = (bf16[2,4,3200]{2,1,0:T(4,128)(2,1)S(1)}, bf16[2,4,3200]{2,1,0:T(4,128)(2,1)S(1)}, u32[]{:S(2)}, u32[]{:S(2)}) collective-permute-start(bf16[2,4,3200]{2,1,0:T(4,128)(2,1)S(1)} %get-tuple-element.32.refs_0_), channel_id=1, source_target_pairs={{0,4},{1,5},{2,6},{3,7},{4,0},{5,1},{6,2},{7,3},{8,12},{9,13},{10,... | collective-permute-start | bytes 153608 | tf_op jit(solution)/shard_map/ppermute | solution.py:288
  32.6 1.5 %collective-permute-done.7.refs_3_ = bf16[2,4,3200]{2,1,0:T(4,128)(2,1)S(1)} collective-permute-done((bf16[2,4,3200]{2,1,0:T(4,128)(2,1)S(1)}, bf16[2,4,3200]{2,1,0:T(4,128)(2,1)S(1)}, u32[]{:S(2)}, u32[]{:S(2)}) %collective-permute-start.7) | collective-permute-done | bytes 51232 | tf_op jit(solution)/shard_map/ppermute | solution.py:288
  34.1 2.3 %collective-permute-done.6.refs_2_ = bf16[2,4,3200]{2,1,0:T(4,128)(2,1)S(1)} collective-permute-done((bf16[2,4,3200]{2,1,0:T(4,128)(2,1)S(1)}, bf16[2,4,3200]{2,1,0:T(4,128)(2,1)S(1)}, u32[]{:S(2)}, u32[]{:S(2)}) %collective-permute-start.6) | collective-permute-done | bytes 51232 | tf_op jit(solution)/shard_map/ppermute | solution.py:288
  36.4 0.0 collective-permute-done.5.refs_1_
  36.5 0.1 collective-permute-start.8
  36.5 1.4 %collective-permute-done.8.refs_1_ = bf16[8,4,3200]{2,1,0:T(4,128)(2,1)S(1)} collective-permute-done((bf16[8,4,3200]{2,1,0:T(4,128)(2,1)S(1)}, bf16[8,4,3200]{2,1,0:T(4,128)(2,1)S(1)}, u32[]{:S(2)}, u32[]{:S(2)}) %collective-permute-start.8) | collective-permute-done | bytes 204832 | tf_op jit(solution)/shard_map/ppermute | solution.py:288
  38.0 0.0 slice-done.3
  38.0 0.0 slice-done.6
  38.0 0.0 slice-done.4
  38.0 0.0 slice-done.7
  38.0 0.0 slice-done
  38.1 6.7 %experts.1 = (f32[8,4,3072]{2,1,0:T(4,128)S(1)}, bf16[8,4,3072]{2,1,0:T(4,128)(2,1)S(1)}) custom-call(bf16[8,4,3200]{2,1,0:T(4,128)(2,1)S(1)} %join.1.refs_0_, bf16[8,4,3200]{2,1,0:T(4,128)(2,1)S(1)} %collective-permute-done.8.refs_1_, bf16[3072,2048]{1,0:T(8,128)(2,1)S(1)} %bitcast.2, bf16[3072,2048]{1,0:T(8,128)(2,1)S(1)} %bitcast.4, ...), custom_call_target="tpu_custom_call" | custom-call | tf_op jit(solution)/shard_map/experts/pallas_call | solution.py:408
  44.8 0.2 collective-permute-start.9
  45.0 1.3 %collective-permute-done.9.refs_1_ = bf16[8,4,3072]{2,1,0:T(4,128)(2,1)S(1)} collective-permute-done((bf16[8,4,3072]{2,1,0:T(4,128)(2,1)S(1)}, bf16[8,4,3072]{2,1,0:T(4,128)(2,1)S(1)}, u32[]{:S(2)}, u32[]{:S(2)}) %collective-permute-start.9) | collective-permute-done | bytes 196640 | tf_op jit(solution)/shard_map/ppermute | solution.py:288
  46.3 0.1 fold.2
  46.3 0.4 collective-permute-start.10
  46.7 2.0 %collective-permute-start.11 = (bf16[2,4,3072]{2,1,0:T(4,128)(2,1)S(1)}, bf16[2,4,3072]{2,1,0:T(4,128)(2,1)S(1)}, u32[]{:S(2)}, u32[]{:S(2)}) collective-permute-start(bf16[2,4,3072]{2,1,0:T(4,128)(2,1)S(1)} %get-tuple-element.37), channel_id=1, source_target_pairs={{0,8},{1,9},{2,10},{3,11},{4,12},{5,13},{6,14},{7,15},{8,0},{9,1},... | collective-permute-start | bytes 147464 | tf_op jit(solution)/shard_map/ppermute | solution.py:288
  48.7 2.1 %collective-permute-start.12 = (bf16[2,4,3072]{2,1,0:T(4,128)(2,1)S(1)}, bf16[2,4,3072]{2,1,0:T(4,128)(2,1)S(1)}, u32[]{:S(2)}, u32[]{:S(2)}) collective-permute-start(bf16[2,4,3072]{2,1,0:T(4,128)(2,1)S(1)} %get-tuple-element.38), channel_id=1, source_target_pairs={{0,12},{1,13},{2,14},{3,15},{4,8},{5,9},{6,10},{7,11},{8,4},{9,5},... | collective-permute-start | bytes 147464 | tf_op jit(solution)/shard_map/ppermute | solution.py:288
  50.8 0.2 collective-permute-done.10.refs_1_
  51.0 2.4 %collective-permute-done.11.refs_2_ = bf16[2,4,3072]{2,1,0:T(4,128)(2,1)S(1)} collective-permute-done((bf16[2,4,3072]{2,1,0:T(4,128)(2,1)S(1)}, bf16[2,4,3072]{2,1,0:T(4,128)(2,1)S(1)}, u32[]{:S(2)}, u32[]{:S(2)}) %collective-permute-start.11) | collective-permute-done | bytes 49184 | tf_op jit(solution)/shard_map/ppermute | solution.py:288
  53.4 1.3 %collective-permute-done.12.refs_3_ = bf16[2,4,3072]{2,1,0:T(4,128)(2,1)S(1)} collective-permute-done((bf16[2,4,3072]{2,1,0:T(4,128)(2,1)S(1)}, bf16[2,4,3072]{2,1,0:T(4,128)(2,1)S(1)}, u32[]{:S(2)}, u32[]{:S(2)}) %collective-permute-start.12) | collective-permute-done | bytes 49184 | tf_op jit(solution)/shard_map/ppermute | solution.py:288
  54.7 0.7 %collective-permute-start.13 = (bf16[1,4,3072]{2,1,0:T(4,128)(2,1)S(1)}, bf16[1,4,3072]{2,1,0:T(4,128)(2,1)S(1)}, u32[]{:S(2)}, u32[]{:S(2)}) collective-permute-start(bf16[1,4,3072]{2,1,0:T(4,128)(2,1)S(1)} %get-tuple-element.40), channel_id=1, source_target_pairs={{0,2},{1,3},{2,0},{3,1},{4,6},{5,7},{6,4},{7,5},{8,10},{9,11},{10,... | collective-permute-start | bytes 73736 | tf_op jit(solution)/shard_map/ppermute | solution.py:288
  55.4 3.2 %collective-permute-done.13.refs_2_ = bf16[1,4,3072]{2,1,0:T(4,128)(2,1)S(1)} collective-permute-done((bf16[1,4,3072]{2,1,0:T(4,128)(2,1)S(1)}, bf16[1,4,3072]{2,1,0:T(4,128)(2,1)S(1)}, u32[]{:S(2)}, u32[]{:S(2)}) %collective-permute-start.13) | collective-permute-done | bytes 24608 | tf_op jit(solution)/shard_map/ppermute | solution.py:288
  58.6 0.6 %final.1 = bf16[2,2,3072]{2,1,0:T(2,128)(2,1)} custom-call(f32[4,3072]{1,0:T(4,128)S(1)} %get-tuple-element.31.refs_0_, f32[1,4,3072]{2,1,0:T(4,128)S(1)} %get-tuple-element.39.refs_1_, bf16[1,4,3072]{2,1,0:T(4,128)(2,1)S(1)} %collective-permute-done.13.refs_2_), custom_call_target="tpu_custom_call" | custom-call | tf_op jit(solution)/shard_map/final/pallas_call | solution.py:420
  (19 shorter events, 0.1 us)
Async XLA Ops:
  0.0 23.4 %copy-start.3 = (s32[2,2,2]{2,1,0:T(2,128)S(1)}, s32[2,2,2]{2,1,0:T(2,128)}, u32[]{:S(2)}) copy-start(s32[2,2,2]{2,1,0:T(2,128)} %refs_0_.4) | copy-start | bytes 100
  0.0 23.4 %copy-start = (bf16[2,2,3072]{2,1,0:T(2,128)(2,1)S(1)}, bf16[2,2,3072]{2,1,0:T(2,128)(2,1)}, u32[]{:S(2)}) copy-start(bf16[2,2,3072]{2,1,0:T(2,128)(2,1)} %refs_1_.3) | copy-start | bytes 73732
  0.0 15.6 %collective-permute-start = (bf16[192,3072]{1,0:T(8,128)(2,1)}, bf16[192,3072]{1,0:T(8,128)(2,1)S(1)}, u32[]{:S(2)}, u32[]{:S(2)}) collective-permute-start(bf16[192,3072]{1,0:T(8,128)(2,1)} %refs_6_.2), channel_id=1, source_target_pairs={{0,1},{1,0},{2,3},{3,2},{4,5},{5,4},{6,7},{7,6},{8,9},{9,8},{10,11... | collective-permute-start | bytes 3538952 | tf_op jit(solution)/shard_map/ppermute | solution.py:288
  15.6 12.1 %copy-start.1 = (bf16[3072,4]{0,1:T(4,128)(2,1)S(1)}, bf16[3072,4]{0,1:T(4,128)(2,1)}, u32[]{:S(2)}) copy-start(bf16[3072,4]{0,1:T(4,128)(2,1)} %param.23) | copy-start | bytes 73732
  15.6 12.1 %copy-start.2 = (bf16[3072]{0:T(1024)(128)(2,1)S(1)}, bf16[3072]{0:T(1024)(128)(2,1)}, u32[]{:S(2)}) copy-start(bf16[3072]{0:T(1024)(128)(2,1)} %gain_ref.1) | copy-start | bytes 18436
  15.6 22.4 %slice-start.3 = ((s8[12582912]{0:T(1024)(128)(4,1)}), s8[4194304]{0:T(1024)(128)(4,1)S(1)}, s32[]{:S(2)}) async-start(s8[12582912]{0:T(1024)(128)(4,1)} %bitcast.3), calls=%async_computation.4 | async-start | bytes 8388608
  15.6 22.4 %slice-start.6 = ((s8[12582912]{0:T(1024)(128)(4,1)}), s8[4194304]{0:T(1024)(128)(4,1)S(1)}, s32[]{:S(2)}) async-start(s8[12582912]{0:T(1024)(128)(4,1)} %bitcast.5), calls=%async_computation.7 | async-start | bytes 8388608
  16.3 4.5 %collective-permute-start.1 = (bf16[2,4,3072]{2,1,0:T(4,128)(2,1)S(1)}, bf16[2,4,3072]{2,1,0:T(4,128)(2,1)S(1)}, u32[]{:S(2)}, u32[]{:S(2)}) collective-permute-start(bf16[2,4,3072]{2,1,0:T(4,128)(2,1)S(1)} %get-tuple-element.26), channel_id=1, source_target_pairs={{0,4},{1,5},{2,6},{3,7},{4,0},{5,1},{6,2},{7,3},{8,12},{9,13},{10,... | collective-permute-start | bytes 147464 | tf_op jit(solution)/shard_map/ppermute | solution.py:288
  16.8 5.2 %collective-permute-start.2 = (bf16[2,4,3072]{2,1,0:T(4,128)(2,1)S(1)}, bf16[2,4,3072]{2,1,0:T(4,128)(2,1)S(1)}, u32[]{:S(2)}, u32[]{:S(2)}) collective-permute-start(bf16[2,4,3072]{2,1,0:T(4,128)(2,1)S(1)} %get-tuple-element.27), channel_id=1, source_target_pairs={{0,8},{1,9},{2,10},{3,11},{4,12},{5,13},{6,14},{7,15},{8,0},{9,1},... | collective-permute-start | bytes 147464 | tf_op jit(solution)/shard_map/ppermute | solution.py:288
  17.4 6.0 %collective-permute-start.3 = (bf16[2,4,3072]{2,1,0:T(4,128)(2,1)S(1)}, bf16[2,4,3072]{2,1,0:T(4,128)(2,1)S(1)}, u32[]{:S(2)}, u32[]{:S(2)}) collective-permute-start(bf16[2,4,3072]{2,1,0:T(4,128)(2,1)S(1)} %get-tuple-element.28), channel_id=1, source_target_pairs={{0,12},{1,13},{2,14},{3,15},{4,8},{5,9},{6,10},{7,11},{8,4},{9,5},... | collective-permute-start | bytes 147464 | tf_op jit(solution)/shard_map/ppermute | solution.py:288
  23.4 14.6 %slice-start.4 = ((s8[12582912]{0:T(1024)(128)(4,1)}), s8[4194304]{0:T(1024)(128)(4,1)S(1)}, s32[]{:S(2)}) async-start(s8[12582912]{0:T(1024)(128)(4,1)} %bitcast.3), calls=%async_computation.5 | async-start | bytes 8388608
  23.4 14.6 %slice-start.7 = ((s8[12582912]{0:T(1024)(128)(4,1)}), s8[4194304]{0:T(1024)(128)(4,1)S(1)}, s32[]{:S(2)}) async-start(s8[12582912]{0:T(1024)(128)(4,1)} %bitcast.5), calls=%async_computation.8 | async-start | bytes 8388608
  23.5 4.2 %collective-permute-start.4 = (bf16[2,4,3200]{2,1,0:T(4,128)(2,1)S(1)}, bf16[2,4,3200]{2,1,0:T(4,128)(2,1)S(1)}, u32[]{:S(2)}, u32[]{:S(2)}) collective-permute-start(bf16[2,4,3200]{2,1,0:T(4,128)(2,1)S(1)} %get-tuple-element.30.sent_ref), channel_id=1, source_target_pairs={{0,2},{1,3},{2,0},{3,1},{4,6},{5,7},{6,4},{7,5},{8,10},{9,11},{10,... | collective-permute-start | bytes 153608 | tf_op jit(solution)/shard_map/ppermute | solution.py:288
  27.7 10.3 %slice-start = ((s8[12582912]{0:T(1024)(128)(4,1)}), s8[4194304]{0:T(1024)(128)(4,1)S(1)}, s32[]{:S(2)}) async-start(s8[12582912]{0:T(1024)(128)(4,1)} %bitcast.1), calls=%async_computation.1 | async-start | bytes 8388608
  27.7 10.3 %slice-start.1 = ((s8[12582912]{0:T(1024)(128)(4,1)}), s8[4194304]{0:T(1024)(128)(4,1)S(1)}, s32[]{:S(2)}) async-start(s8[12582912]{0:T(1024)(128)(4,1)} %bitcast.1), calls=%async_computation.2 | async-start | bytes 8388608
  27.7 10.3 %slice-start.5 = ((s8[12582912]{0:T(1024)(128)(4,1)}), s8[4194304]{0:T(1024)(128)(4,1)S(1)}, s32[]{:S(2)}) async-start(s8[12582912]{0:T(1024)(128)(4,1)} %bitcast.3), calls=%async_computation.6 | async-start | bytes 8388608
  27.7 10.3 %slice-start.8 = ((s8[12582912]{0:T(1024)(128)(4,1)}), s8[4194304]{0:T(1024)(128)(4,1)S(1)}, s32[]{:S(2)}) async-start(s8[12582912]{0:T(1024)(128)(4,1)} %bitcast.5), calls=%async_computation.9 | async-start | bytes 8388608
  28.2 9.8 %slice-start.2 = ((s8[12582912]{0:T(1024)(128)(4,1)}), s8[4194304]{0:T(1024)(128)(4,1)S(1)}, s32[]{:S(2)}) async-start(s8[12582912]{0:T(1024)(128)(4,1)} %bitcast.1), calls=%async_computation.3 | async-start | bytes 8388608
  28.2 5.9 %collective-permute-start.7 = (bf16[2,4,3200]{2,1,0:T(4,128)(2,1)S(1)}, bf16[2,4,3200]{2,1,0:T(4,128)(2,1)S(1)}, u32[]{:S(2)}, u32[]{:S(2)}) collective-permute-start(bf16[2,4,3200]{2,1,0:T(4,128)(2,1)S(1)} %get-tuple-element.32.refs_0_), channel_id=1, source_target_pairs={{0,12},{1,13},{2,14},{3,15},{4,8},{5,9},{6,10},{7,11},{8,4},{9,5},... | collective-permute-start | bytes 153608 | tf_op jit(solution)/shard_map/ppermute | solution.py:288
  31.4 5.0 %collective-permute-start.6 = (bf16[2,4,3200]{2,1,0:T(4,128)(2,1)S(1)}, bf16[2,4,3200]{2,1,0:T(4,128)(2,1)S(1)}, u32[]{:S(2)}, u32[]{:S(2)}) collective-permute-start(bf16[2,4,3200]{2,1,0:T(4,128)(2,1)S(1)} %get-tuple-element.32.refs_0_), channel_id=1, source_target_pairs={{0,8},{1,9},{2,10},{3,11},{4,12},{5,13},{6,14},{7,15},{8,0},{9,1},... | collective-permute-start | bytes 153608 | tf_op jit(solution)/shard_map/ppermute | solution.py:288
  31.4 5.0 %collective-permute-start.5 = (bf16[2,4,3200]{2,1,0:T(4,128)(2,1)S(1)}, bf16[2,4,3200]{2,1,0:T(4,128)(2,1)S(1)}, u32[]{:S(2)}, u32[]{:S(2)}) collective-permute-start(bf16[2,4,3200]{2,1,0:T(4,128)(2,1)S(1)} %get-tuple-element.32.refs_0_), channel_id=1, source_target_pairs={{0,4},{1,5},{2,6},{3,7},{4,0},{5,1},{6,2},{7,3},{8,12},{9,13},{10,... | collective-permute-start | bytes 153608 | tf_op jit(solution)/shard_map/ppermute | solution.py:288
  36.5 1.5 %collective-permute-start.8 = (bf16[8,4,3200]{2,1,0:T(4,128)(2,1)S(1)}, bf16[8,4,3200]{2,1,0:T(4,128)(2,1)S(1)}, u32[]{:S(2)}, u32[]{:S(2)}) collective-permute-start(bf16[8,4,3200]{2,1,0:T(4,128)(2,1)S(1)} %join.1.refs_0_), channel_id=1, source_target_pairs={{0,1},{1,0},{2,3},{3,2},{4,5},{5,4},{6,7},{7,6},{8,9},{9,8},{10,11... | collective-permute-start | bytes 614408 | tf_op jit(solution)/shard_map/ppermute | solution.py:288
  44.8 1.5 %collective-permute-start.9 = (bf16[8,4,3072]{2,1,0:T(4,128)(2,1)S(1)}, bf16[8,4,3072]{2,1,0:T(4,128)(2,1)S(1)}, u32[]{:S(2)}, u32[]{:S(2)}) collective-permute-start(bf16[8,4,3072]{2,1,0:T(4,128)(2,1)S(1)} %get-tuple-element.34), channel_id=1, source_target_pairs={{0,1},{1,0},{2,3},{3,2},{4,5},{5,4},{6,7},{7,6},{8,9},{9,8},{10,11... | collective-permute-start | bytes 589832 | tf_op jit(solution)/shard_map/ppermute | solution.py:288
  46.3 4.7 %collective-permute-start.10 = (bf16[2,4,3072]{2,1,0:T(4,128)(2,1)S(1)}, bf16[2,4,3072]{2,1,0:T(4,128)(2,1)S(1)}, u32[]{:S(2)}, u32[]{:S(2)}) collective-permute-start(bf16[2,4,3072]{2,1,0:T(4,128)(2,1)S(1)} %get-tuple-element.36), channel_id=1, source_target_pairs={{0,4},{1,5},{2,6},{3,7},{4,0},{5,1},{6,2},{7,3},{8,12},{9,13},{10,... | collective-permute-start | bytes 147464 | tf_op jit(solution)/shard_map/ppermute | solution.py:288
  46.7 6.7 %collective-permute-start.11 = (bf16[2,4,3072]{2,1,0:T(4,128)(2,1)S(1)}, bf16[2,4,3072]{2,1,0:T(4,128)(2,1)S(1)}, u32[]{:S(2)}, u32[]{:S(2)}) collective-permute-start(bf16[2,4,3072]{2,1,0:T(4,128)(2,1)S(1)} %get-tuple-element.37), channel_id=1, source_target_pairs={{0,8},{1,9},{2,10},{3,11},{4,12},{5,13},{6,14},{7,15},{8,0},{9,1},... | collective-permute-start | bytes 147464 | tf_op jit(solution)/shard_map/ppermute | solution.py:288
  48.7 6.0 %collective-permute-start.12 = (bf16[2,4,3072]{2,1,0:T(4,128)(2,1)S(1)}, bf16[2,4,3072]{2,1,0:T(4,128)(2,1)S(1)}, u32[]{:S(2)}, u32[]{:S(2)}) collective-permute-start(bf16[2,4,3072]{2,1,0:T(4,128)(2,1)S(1)} %get-tuple-element.38), channel_id=1, source_target_pairs={{0,12},{1,13},{2,14},{3,15},{4,8},{5,9},{6,10},{7,11},{8,4},{9,5},... | collective-permute-start | bytes 147464 | tf_op jit(solution)/shard_map/ppermute | solution.py:288
  54.7 3.9 %collective-permute-start.13 = (bf16[1,4,3072]{2,1,0:T(4,128)(2,1)S(1)}, bf16[1,4,3072]{2,1,0:T(4,128)(2,1)S(1)}, u32[]{:S(2)}, u32[]{:S(2)}) collective-permute-start(bf16[1,4,3072]{2,1,0:T(4,128)(2,1)S(1)} %get-tuple-element.40), channel_id=1, source_target_pairs={{0,2},{1,3},{2,0},{3,1},{4,6},{5,7},{6,4},{7,5},{8,10},{9,11},{10,... | collective-permute-start | bytes 73736 | tf_op jit(solution)/shard_map/ppermute | solution.py:288

commit v9 on v8

--- a/solution.py
+++ b/solution.py
@@ -252,7 +252,7 @@
     stages, bit = [], 2
     while bit < devices:
         if bit > 2 and 2 * bit < devices:
-            stages.append((bit, 2 * bit, 3 * bit))
+            stages.append((3 * bit, 2 * bit, bit))
             bit *= 4
         else:
             stages.append((bit,))

time: 59.4 us -> 58.8 us (0.990)
  waiting for transfers between devices: 19.8 us -> 19.2 us
    ppermute x14, waiting for transfers between devices: 19.8 us -> 19.2 us  [hop(): return lax.ppermute(blocks, 'dev', [(i, i ^ mask) for i in range(devices)])]
where the time goes in v9:
time: 58.8 us; the launch traced here: 58.7 us
  waiting for transfers between devices  19.2 us (33%)
  starting transfers between devices  15.5 us (26%)
  blocking collectives  13.3 us (23%)
  Pallas kernels  10.5 us (18%)
    ppermute x14, waiting for transfers between devices, hop(): return lax.ppermute(blocks, 'dev', [(i, i ^ mask) for i in range(devices)])  19.2 us
    ppermute x14, starting transfers between devices, hop(): return lax.ppermute(blocks, 'dev', [(i, i ^ mask) for i in range(devices)])  15.5 us
    all_to_all x1, blocking collectives, exchange(): lax.all_to_all(blocks, 'dev', split_axis=0, concat_axis=0, axis_index_gro...  13.3 us
    pallas_call x1, Pallas kernels, local(): pl.pallas_call(lambda *refs: expert_kernel(expert_count, *refs), in_specs...  6.68 us
    pallas_call x1, Pallas kernels, local(): pl.pallas_call(attend_kernel, in_specs=[HBM] * len(operands), out_specs=(...  1.81 us
  transfers between devices with their start and end apart: 14, of which 11 were waited for; matrix products, arithmetic and copies ran while one was open for 0% of the time, Pallas kernels for 3%

profile of v9, /device:TPU:0, one launch (start us, length us, event | category | flops | bytes accessed | tf_op | source)
XLA Modules:
  0.0 58.7 jit_solution(6820409922991222344)
XLA Ops:
  0.0 0.5 collective-permute-start
  0.5 1.8 %attend.1 = (bf16[8,4,384]{2,1,0:T(4,128)(2,1)S(1)}, bf16[192,3072]{1,0:T(8,128)(2,1)S(1)}) custom-call(bf16[2,2,3072]{2,1,0:T(2,128)(2,1)} %refs_0_.3, bf16[2,2,128,512]{3,2,1,0:T(8,128)(2,1)} %refs_1_.2, bf16[2,2,512]{2,1,0:T(2,128)(2,1)} %refs_2_.2, s32[2,2]{1,0:T(2,128)} %refs_3_.3, bf16[2,2,128,512]{3,2,1,0:T(8,128)(2,1)} %refs_4_.3, ...), custom_call_target="tpu_custom_call" | custom-call | tf_op jit(solution)/shard_map/attend/pallas_call | solution.py:362
  2.3 13.3 %all_to_all.5.refs_0_ = bf16[8,4,384]{2,1,0:T(4,128)(2,1)S(1)} all-to-all(bf16[8,4,384]{2,1,0:T(4,128)(2,1)S(1)} %get-tuple-element.23), channel_id=1, replica_groups={{0,2,4,6,8,10,12,14},{1,3,5,7,9,11,13,15},{16,18,20,22,24,26,28,30},{17..., dimensions={0} | all-to-all | bytes 49152 | tf_op jit(solution)/shard_map/all_to_all | solution.py:334
  15.6 0.0 collective-permute-done.refs_2_
  15.6 0.0 slice-start.6
  15.6 0.7 %project.1 = (f32[2,4,3072]{2,1,0:T(4,128)S(1)}, bf16[2,4,3072]{2,1,0:T(4,128)(2,1)S(1)}, bf16[2,4,3072]{2,1,0:T(4,128)(2,1)S(1)}, bf16[2,4,3072]{2,1,0:T(4,128)(2,1)S(1)}) custom-call(bf16[8,4,384]{2,1,0:T(4,128)(2,1)S(1)} %all_to_all.5.refs_0_, bf16[192,3072]{1,0:T(8,128)(2,1)S(1)} %get-tuple-element.24.refs_1_, ...), custom_call_target="tpu_custom_call" | custom-call | tf_op jit(solution)/shard_map/project/pallas_call | solution.py:380
  16.3 0.6 %collective-permute-start.1 = (bf16[2,4,3072]{2,1,0:T(4,128)(2,1)S(1)}, bf16[2,4,3072]{2,1,0:T(4,128)(2,1)S(1)}, u32[]{:S(2)}, u32[]{:S(2)}) collective-permute-start(bf16[2,4,3072]{2,1,0:T(4,128)(2,1)S(1)} %get-tuple-element.26), channel_id=1, source_target_pairs={{0,12},{1,13},{2,14},{3,15},{4,8},{5,9},{6,10},{7,11},{8,4},{9,5},... | collective-permute-start | bytes 147464 | tf_op jit(solution)/shard_map/ppermute | solution.py:288
  16.9 1.3 %collective-permute-start.2 = (bf16[2,4,3072]{2,1,0:T(4,128)(2,1)S(1)}, bf16[2,4,3072]{2,1,0:T(4,128)(2,1)S(1)}, u32[]{:S(2)}, u32[]{:S(2)}) collective-permute-start(bf16[2,4,3072]{2,1,0:T(4,128)(2,1)S(1)} %get-tuple-element.27), channel_id=1, source_target_pairs={{0,8},{1,9},{2,10},{3,11},{4,12},{5,13},{6,14},{7,15},{8,0},{9,1},... | collective-permute-start | bytes 147464 | tf_op jit(solution)/shard_map/ppermute | solution.py:288
  18.2 2.5 %collective-permute-start.3 = (bf16[2,4,3072]{2,1,0:T(4,128)(2,1)S(1)}, bf16[2,4,3072]{2,1,0:T(4,128)(2,1)S(1)}, u32[]{:S(2)}, u32[]{:S(2)}) collective-permute-start(bf16[2,4,3072]{2,1,0:T(4,128)(2,1)S(1)} %get-tuple-element.28), channel_id=1, source_target_pairs={{0,4},{1,5},{2,6},{3,7},{4,0},{5,1},{6,2},{7,3},{8,12},{9,13},{10,... | collective-permute-start | bytes 147464 | tf_op jit(solution)/shard_map/ppermute | solution.py:288
  20.7 1.6 %collective-permute-done.1.refs_3_ = bf16[2,4,3072]{2,1,0:T(4,128)(2,1)S(1)} collective-permute-done((bf16[2,4,3072]{2,1,0:T(4,128)(2,1)S(1)}, bf16[2,4,3072]{2,1,0:T(4,128)(2,1)S(1)}, u32[]{:S(2)}, u32[]{:S(2)}) %collective-permute-start.1) | collective-permute-done | bytes 49184 | tf_op jit(solution)/shard_map/ppermute | solution.py:288
  22.3 0.7 %collective-permute-done.2.refs_4_ = bf16[2,4,3072]{2,1,0:T(4,128)(2,1)S(1)} collective-permute-done((bf16[2,4,3072]{2,1,0:T(4,128)(2,1)S(1)}, bf16[2,4,3072]{2,1,0:T(4,128)(2,1)S(1)}, u32[]{:S(2)}, u32[]{:S(2)}) %collective-permute-start.2) | collective-permute-done | bytes 49184 | tf_op jit(solution)/shard_map/ppermute | solution.py:288
  23.0 0.0 collective-permute-done.3.refs_5_
  23.0 0.0 copy-done
  23.1 0.0 slice-start.4
  23.1 0.0 slice-start.7
  23.1 0.1 share.1
  23.2 0.8 %collective-permute-start.4 = (bf16[2,4,3200]{2,1,0:T(4,128)(2,1)S(1)}, bf16[2,4,3200]{2,1,0:T(4,128)(2,1)S(1)}, u32[]{:S(2)}, u32[]{:S(2)}) collective-permute-start(bf16[2,4,3200]{2,1,0:T(4,128)(2,1)S(1)} %get-tuple-element.30.sent_ref), channel_id=1, source_target_pairs={{0,2},{1,3},{2,0},{3,1},{4,6},{5,7},{6,4},{7,5},{8,10},{9,11},{10,... | collective-permute-start | bytes 153608 | tf_op jit(solution)/shard_map/ppermute | solution.py:288
  23.9 3.4 %collective-permute-done.4.got_ref = bf16[2,4,3200]{2,1,0:T(4,128)(2,1)S(1)} collective-permute-done((bf16[2,4,3200]{2,1,0:T(4,128)(2,1)S(1)}, bf16[2,4,3200]{2,1,0:T(4,128)(2,1)S(1)}, u32[]{:S(2)}, u32[]{:S(2)}) %collective-permute-start.4) | collective-permute-done | bytes 51232 | tf_op jit(solution)/shard_map/ppermute | solution.py:288
  27.3 0.0 slice-start.5
  27.4 0.0 slice-start.8
  27.4 0.5 norm.1
  27.9 1.8 %collective-permute-start.7 = (bf16[2,4,3200]{2,1,0:T(4,128)(2,1)S(1)}, bf16[2,4,3200]{2,1,0:T(4,128)(2,1)S(1)}, u32[]{:S(2)}, u32[]{:S(2)}) collective-permute-start(bf16[2,4,3200]{2,1,0:T(4,128)(2,1)S(1)} %get-tuple-element.32.refs_0_), channel_id=1, source_target_pairs={{0,4},{1,5},{2,6},{3,7},{4,0},{5,1},{6,2},{7,3},{8,12},{9,13},{10,... | collective-permute-start | bytes 153608 | tf_op jit(solution)/shard_map/ppermute | solution.py:288
  29.6 0.9 %collective-permute-start.6 = (bf16[2,4,3200]{2,1,0:T(4,128)(2,1)S(1)}, bf16[2,4,3200]{2,1,0:T(4,128)(2,1)S(1)}, u32[]{:S(2)}, u32[]{:S(2)}) collective-permute-start(bf16[2,4,3200]{2,1,0:T(4,128)(2,1)S(1)} %get-tuple-element.32.refs_0_), channel_id=1, source_target_pairs={{0,8},{1,9},{2,10},{3,11},{4,12},{5,13},{6,14},{7,15},{8,0},{9,1},... | collective-permute-start | bytes 153608 | tf_op jit(solution)/shard_map/ppermute | solution.py:288
  30.5 1.7 %collective-permute-start.5 = (bf16[2,4,3200]{2,1,0:T(4,128)(2,1)S(1)}, bf16[2,4,3200]{2,1,0:T(4,128)(2,1)S(1)}, u32[]{:S(2)}, u32[]{:S(2)}) collective-permute-start(bf16[2,4,3200]{2,1,0:T(4,128)(2,1)S(1)} %get-tuple-element.32.refs_0_), channel_id=1, source_target_pairs={{0,12},{1,13},{2,14},{3,15},{4,8},{5,9},{6,10},{7,11},{8,4},{9,5},... | collective-permute-start | bytes 153608 | tf_op jit(solution)/shard_map/ppermute | solution.py:288
  32.3 0.2 collective-permute-done.7.refs_3_
  32.4 2.5 %collective-permute-done.6.refs_2_ = bf16[2,4,3200]{2,1,0:T(4,128)(2,1)S(1)} collective-permute-done((bf16[2,4,3200]{2,1,0:T(4,128)(2,1)S(1)}, bf16[2,4,3200]{2,1,0:T(4,128)(2,1)S(1)}, u32[]{:S(2)}, u32[]{:S(2)}) %collective-permute-start.6) | collective-permute-done | bytes 51232 | tf_op jit(solution)/shard_map/ppermute | solution.py:288
  34.9 1.5 %collective-permute-done.5.refs_1_ = bf16[2,4,3200]{2,1,0:T(4,128)(2,1)S(1)} collective-permute-done((bf16[2,4,3200]{2,1,0:T(4,128)(2,1)S(1)}, bf16[2,4,3200]{2,1,0:T(4,128)(2,1)S(1)}, u32[]{:S(2)}, u32[]{:S(2)}) %collective-permute-start.5) | collective-permute-done | bytes 51232 | tf_op jit(solution)/shard_map/ppermute | solution.py:288
  36.5 0.1 collective-permute-start.8
  36.6 1.4 %collective-permute-done.8.refs_1_ = bf16[8,4,3200]{2,1,0:T(4,128)(2,1)S(1)} collective-permute-done((bf16[8,4,3200]{2,1,0:T(4,128)(2,1)S(1)}, bf16[8,4,3200]{2,1,0:T(4,128)(2,1)S(1)}, u32[]{:S(2)}, u32[]{:S(2)}) %collective-permute-start.8) | collective-permute-done | bytes 204832 | tf_op jit(solution)/shard_map/ppermute | solution.py:288
  38.0 0.0 slice-done.4
  38.0 0.0 slice-done.7
  38.0 0.0 slice-done
  38.0 0.0 slice-done.1
  38.0 0.0 slice-done.5
  38.0 0.0 slice-done.8
  38.1 6.7 %experts.1 = (f32[8,4,3072]{2,1,0:T(4,128)S(1)}, bf16[8,4,3072]{2,1,0:T(4,128)(2,1)S(1)}) custom-call(bf16[8,4,3200]{2,1,0:T(4,128)(2,1)S(1)} %join.1.refs_0_, bf16[8,4,3200]{2,1,0:T(4,128)(2,1)S(1)} %collective-permute-done.8.refs_1_, bf16[3072,2048]{1,0:T(8,128)(2,1)S(1)} %bitcast.2, bf16[3072,2048]{1,0:T(8,128)(2,1)S(1)} %bitcast.4, ...), custom_call_target="tpu_custom_call" | custom-call | tf_op jit(solution)/shard_map/experts/pallas_call | solution.py:408
  44.8 0.2 collective-permute-start.9
  45.0 1.3 %collective-permute-done.9.refs_1_ = bf16[8,4,3072]{2,1,0:T(4,128)(2,1)S(1)} collective-permute-done((bf16[8,4,3072]{2,1,0:T(4,128)(2,1)S(1)}, bf16[8,4,3072]{2,1,0:T(4,128)(2,1)S(1)}, u32[]{:S(2)}, u32[]{:S(2)}) %collective-permute-start.9) | collective-permute-done | bytes 196640 | tf_op jit(solution)/shard_map/ppermute | solution.py:288
  46.3 0.1 fold.2
  46.4 1.8 %collective-permute-start.10 = (bf16[2,4,3072]{2,1,0:T(4,128)(2,1)S(1)}, bf16[2,4,3072]{2,1,0:T(4,128)(2,1)S(1)}, u32[]{:S(2)}, u32[]{:S(2)}) collective-permute-start(bf16[2,4,3072]{2,1,0:T(4,128)(2,1)S(1)} %get-tuple-element.36), channel_id=1, source_target_pairs={{0,12},{1,13},{2,14},{3,15},{4,8},{5,9},{6,10},{7,11},{8,4},{9,5},... | collective-permute-start | bytes 147464 | tf_op jit(solution)/shard_map/ppermute | solution.py:288
  48.2 0.0 collective-permute-start.11
  48.2 2.7 %collective-permute-start.12 = (bf16[2,4,3072]{2,1,0:T(4,128)(2,1)S(1)}, bf16[2,4,3072]{2,1,0:T(4,128)(2,1)S(1)}, u32[]{:S(2)}, u32[]{:S(2)}) collective-permute-start(bf16[2,4,3072]{2,1,0:T(4,128)(2,1)S(1)} %get-tuple-element.38), channel_id=1, source_target_pairs={{0,4},{1,5},{2,6},{3,7},{4,0},{5,1},{6,2},{7,3},{8,12},{9,13},{10,... | collective-permute-start | bytes 147464 | tf_op jit(solution)/shard_map/ppermute | solution.py:288
  50.8 1.8 %collective-permute-done.10.refs_1_ = bf16[2,4,3072]{2,1,0:T(4,128)(2,1)S(1)} collective-permute-done((bf16[2,4,3072]{2,1,0:T(4,128)(2,1)S(1)}, bf16[2,4,3072]{2,1,0:T(4,128)(2,1)S(1)}, u32[]{:S(2)}, u32[]{:S(2)}) %collective-permute-start.10) | collective-permute-done | bytes 49184 | tf_op jit(solution)/shard_map/ppermute | solution.py:288
  52.7 1.5 %collective-permute-done.11.refs_2_ = bf16[2,4,3072]{2,1,0:T(4,128)(2,1)S(1)} collective-permute-done((bf16[2,4,3072]{2,1,0:T(4,128)(2,1)S(1)}, bf16[2,4,3072]{2,1,0:T(4,128)(2,1)S(1)}, u32[]{:S(2)}, u32[]{:S(2)}) %collective-permute-start.11) | collective-permute-done | bytes 49184 | tf_op jit(solution)/shard_map/ppermute | solution.py:288
  54.1 0.0 collective-permute-done.12.refs_3_
  54.2 0.7 %collective-permute-start.13 = (bf16[1,4,3072]{2,1,0:T(4,128)(2,1)S(1)}, bf16[1,4,3072]{2,1,0:T(4,128)(2,1)S(1)}, u32[]{:S(2)}, u32[]{:S(2)}) collective-permute-start(bf16[1,4,3072]{2,1,0:T(4,128)(2,1)S(1)} %get-tuple-element.40), channel_id=1, source_target_pairs={{0,2},{1,3},{2,0},{3,1},{4,6},{5,7},{6,4},{7,5},{8,10},{9,11},{10,... | collective-permute-start | bytes 73736 | tf_op jit(solution)/shard_map/ppermute | solution.py:288
  54.8 3.2 %collective-permute-done.13.refs_2_ = bf16[1,4,3072]{2,1,0:T(4,128)(2,1)S(1)} collective-permute-done((bf16[1,4,3072]{2,1,0:T(4,128)(2,1)S(1)}, bf16[1,4,3072]{2,1,0:T(4,128)(2,1)S(1)}, u32[]{:S(2)}, u32[]{:S(2)}) %collective-permute-start.13) | collective-permute-done | bytes 24608 | tf_op jit(solution)/shard_map/ppermute | solution.py:288
  58.0 0.6 %final.1 = bf16[2,2,3072]{2,1,0:T(2,128)(2,1)} custom-call(f32[4,3072]{1,0:T(4,128)S(1)} %get-tuple-element.31.refs_0_, f32[1,4,3072]{2,1,0:T(4,128)S(1)} %get-tuple-element.39.refs_1_, bf16[1,4,3072]{2,1,0:T(4,128)(2,1)S(1)} %collective-permute-done.13.refs_2_), custom_call_target="tpu_custom_call" | custom-call | tf_op jit(solution)/shard_map/final/pallas_call | solution.py:420
  (19 shorter events, 0.1 us)
Async XLA Ops:
  0.0 23.0 %copy-start.3 = (s32[2,2,2]{2,1,0:T(2,128)S(1)}, s32[2,2,2]{2,1,0:T(2,128)}, u32[]{:S(2)}) copy-start(s32[2,2,2]{2,1,0:T(2,128)} %refs_0_.4) | copy-start | bytes 100
  0.0 23.0 %copy-start = (bf16[2,2,3072]{2,1,0:T(2,128)(2,1)S(1)}, bf16[2,2,3072]{2,1,0:T(2,128)(2,1)}, u32[]{:S(2)}) copy-start(bf16[2,2,3072]{2,1,0:T(2,128)(2,1)} %refs_1_.3) | copy-start | bytes 73732
  0.0 15.6 %collective-permute-start = (bf16[192,3072]{1,0:T(8,128)(2,1)}, bf16[192,3072]{1,0:T(8,128)(2,1)S(1)}, u32[]{:S(2)}, u32[]{:S(2)}) collective-permute-start(bf16[192,3072]{1,0:T(8,128)(2,1)} %refs_6_.2), channel_id=1, source_target_pairs={{0,1},{1,0},{2,3},{3,2},{4,5},{5,4},{6,7},{7,6},{8,9},{9,8},{10,11... | collective-permute-start | bytes 3538952 | tf_op jit(solution)/shard_map/ppermute | solution.py:288
  15.6 11.8 %copy-start.1 = (bf16[3072,4]{0,1:T(4,128)(2,1)S(1)}, bf16[3072,4]{0,1:T(4,128)(2,1)}, u32[]{:S(2)}) copy-start(bf16[3072,4]{0,1:T(4,128)(2,1)} %param.23) | copy-start | bytes 73732
  15.6 11.8 %copy-start.2 = (bf16[3072]{0:T(1024)(128)(2,1)S(1)}, bf16[3072]{0:T(1024)(128)(2,1)}, u32[]{:S(2)}) copy-start(bf16[3072]{0:T(1024)(128)(2,1)} %gain_ref.1) | copy-start | bytes 18436
  15.6 22.4 %slice-start.3 = ((s8[12582912]{0:T(1024)(128)(4,1)}), s8[4194304]{0:T(1024)(128)(4,1)S(1)}, s32[]{:S(2)}) async-start(s8[12582912]{0:T(1024)(128)(4,1)} %bitcast.3), calls=%async_computation.4 | async-start | bytes 8388608
  15.6 22.4 %slice-start.6 = ((s8[12582912]{0:T(1024)(128)(4,1)}), s8[4194304]{0:T(1024)(128)(4,1)S(1)}, s32[]{:S(2)}) async-start(s8[12582912]{0:T(1024)(128)(4,1)} %bitcast.5), calls=%async_computation.7 | async-start | bytes 8388608
  16.3 6.1 %collective-permute-start.1 = (bf16[2,4,3072]{2,1,0:T(4,128)(2,1)S(1)}, bf16[2,4,3072]{2,1,0:T(4,128)(2,1)S(1)}, u32[]{:S(2)}, u32[]{:S(2)}) collective-permute-start(bf16[2,4,3072]{2,1,0:T(4,128)(2,1)S(1)} %get-tuple-element.26), channel_id=1, source_target_pairs={{0,12},{1,13},{2,14},{3,15},{4,8},{5,9},{6,10},{7,11},{8,4},{9,5},... | collective-permute-start | bytes 147464 | tf_op jit(solution)/shard_map/ppermute | solution.py:288
  16.9 6.2 %collective-permute-start.2 = (bf16[2,4,3072]{2,1,0:T(4,128)(2,1)S(1)}, bf16[2,4,3072]{2,1,0:T(4,128)(2,1)S(1)}, u32[]{:S(2)}, u32[]{:S(2)}) collective-permute-start(bf16[2,4,3072]{2,1,0:T(4,128)(2,1)S(1)} %get-tuple-element.27), channel_id=1, source_target_pairs={{0,8},{1,9},{2,10},{3,11},{4,12},{5,13},{6,14},{7,15},{8,0},{9,1},... | collective-permute-start | bytes 147464 | tf_op jit(solution)/shard_map/ppermute | solution.py:288
  18.2 4.8 %collective-permute-start.3 = (bf16[2,4,3072]{2,1,0:T(4,128)(2,1)S(1)}, bf16[2,4,3072]{2,1,0:T(4,128)(2,1)S(1)}, u32[]{:S(2)}, u32[]{:S(2)}) collective-permute-start(bf16[2,4,3072]{2,1,0:T(4,128)(2,1)S(1)} %get-tuple-element.28), channel_id=1, source_target_pairs={{0,4},{1,5},{2,6},{3,7},{4,0},{5,1},{6,2},{7,3},{8,12},{9,13},{10,... | collective-permute-start | bytes 147464 | tf_op jit(solution)/shard_map/ppermute | solution.py:288
  23.1 14.9 %slice-start.4 = ((s8[12582912]{0:T(1024)(128)(4,1)}), s8[4194304]{0:T(1024)(128)(4,1)S(1)}, s32[]{:S(2)}) async-start(s8[12582912]{0:T(1024)(128)(4,1)} %bitcast.3), calls=%async_computation.5 | async-start | bytes 8388608
  23.1 14.9 %slice-start.7 = ((s8[12582912]{0:T(1024)(128)(4,1)}), s8[4194304]{0:T(1024)(128)(4,1)S(1)}, s32[]{:S(2)}) async-start(s8[12582912]{0:T(1024)(128)(4,1)} %bitcast.5), calls=%async_computation.8 | async-start | bytes 8388608
  23.2 4.2 %collective-permute-start.4 = (bf16[2,4,3200]{2,1,0:T(4,128)(2,1)S(1)}, bf16[2,4,3200]{2,1,0:T(4,128)(2,1)S(1)}, u32[]{:S(2)}, u32[]{:S(2)}) collective-permute-start(bf16[2,4,3200]{2,1,0:T(4,128)(2,1)S(1)} %get-tuple-element.30.sent_ref), channel_id=1, source_target_pairs={{0,2},{1,3},{2,0},{3,1},{4,6},{5,7},{6,4},{7,5},{8,10},{9,11},{10,... | collective-permute-start | bytes 153608 | tf_op jit(solution)/shard_map/ppermute | solution.py:288
  27.3 10.7 %slice-start = ((s8[12582912]{0:T(1024)(128)(4,1)}), s8[4194304]{0:T(1024)(128)(4,1)S(1)}, s32[]{:S(2)}) async-start(s8[12582912]{0:T(1024)(128)(4,1)} %bitcast.1), calls=%async_computation.1 | async-start | bytes 8388608
  27.3 10.7 %slice-start.1 = ((s8[12582912]{0:T(1024)(128)(4,1)}), s8[4194304]{0:T(1024)(128)(4,1)S(1)}, s32[]{:S(2)}) async-start(s8[12582912]{0:T(1024)(128)(4,1)} %bitcast.1), calls=%async_computation.2 | async-start | bytes 8388608
  27.3 10.7 %slice-start.5 = ((s8[12582912]{0:T(1024)(128)(4,1)}), s8[4194304]{0:T(1024)(128)(4,1)S(1)}, s32[]{:S(2)}) async-start(s8[12582912]{0:T(1024)(128)(4,1)} %bitcast.3), calls=%async_computation.6 | async-start | bytes 8388608
  27.4 10.7 %slice-start.8 = ((s8[12582912]{0:T(1024)(128)(4,1)}), s8[4194304]{0:T(1024)(128)(4,1)S(1)}, s32[]{:S(2)}) async-start(s8[12582912]{0:T(1024)(128)(4,1)} %bitcast.5), calls=%async_computation.9 | async-start | bytes 8388608
  27.9 10.2 %slice-start.2 = ((s8[12582912]{0:T(1024)(128)(4,1)}), s8[4194304]{0:T(1024)(128)(4,1)S(1)}, s32[]{:S(2)}) async-start(s8[12582912]{0:T(1024)(128)(4,1)} %bitcast.1), calls=%async_computation.3 | async-start | bytes 8388608
  27.9 4.6 %collective-permute-start.7 = (bf16[2,4,3200]{2,1,0:T(4,128)(2,1)S(1)}, bf16[2,4,3200]{2,1,0:T(4,128)(2,1)S(1)}, u32[]{:S(2)}, u32[]{:S(2)}) collective-permute-start(bf16[2,4,3200]{2,1,0:T(4,128)(2,1)S(1)} %get-tuple-element.32.refs_0_), channel_id=1, source_target_pairs={{0,4},{1,5},{2,6},{3,7},{4,0},{5,1},{6,2},{7,3},{8,12},{9,13},{10,... | collective-permute-start | bytes 153608 | tf_op jit(solution)/shard_map/ppermute | solution.py:288
  29.6 5.3 %collective-permute-start.6 = (bf16[2,4,3200]{2,1,0:T(4,128)(2,1)S(1)}, bf16[2,4,3200]{2,1,0:T(4,128)(2,1)S(1)}, u32[]{:S(2)}, u32[]{:S(2)}) collective-permute-start(bf16[2,4,3200]{2,1,0:T(4,128)(2,1)S(1)} %get-tuple-element.32.refs_0_), channel_id=1, source_target_pairs={{0,8},{1,9},{2,10},{3,11},{4,12},{5,13},{6,14},{7,15},{8,0},{9,1},... | collective-permute-start | bytes 153608 | tf_op jit(solution)/shard_map/ppermute | solution.py:288
  30.5 5.9 %collective-permute-start.5 = (bf16[2,4,3200]{2,1,0:T(4,128)(2,1)S(1)}, bf16[2,4,3200]{2,1,0:T(4,128)(2,1)S(1)}, u32[]{:S(2)}, u32[]{:S(2)}) collective-permute-start(bf16[2,4,3200]{2,1,0:T(4,128)(2,1)S(1)} %get-tuple-element.32.refs_0_), channel_id=1, source_target_pairs={{0,12},{1,13},{2,14},{3,15},{4,8},{5,9},{6,10},{7,11},{8,4},{9,5},... | collective-permute-start | bytes 153608 | tf_op jit(solution)/shard_map/ppermute | solution.py:288
  36.5 1.5 %collective-permute-start.8 = (bf16[8,4,3200]{2,1,0:T(4,128)(2,1)S(1)}, bf16[8,4,3200]{2,1,0:T(4,128)(2,1)S(1)}, u32[]{:S(2)}, u32[]{:S(2)}) collective-permute-start(bf16[8,4,3200]{2,1,0:T(4,128)(2,1)S(1)} %join.1.refs_0_), channel_id=1, source_target_pairs={{0,1},{1,0},{2,3},{3,2},{4,5},{5,4},{6,7},{7,6},{8,9},{9,8},{10,11... | collective-permute-start | bytes 614408 | tf_op jit(solution)/shard_map/ppermute | solution.py:288
  44.8 1.5 %collective-permute-start.9 = (bf16[8,4,3072]{2,1,0:T(4,128)(2,1)S(1)}, bf16[8,4,3072]{2,1,0:T(4,128)(2,1)S(1)}, u32[]{:S(2)}, u32[]{:S(2)}) collective-permute-start(bf16[8,4,3072]{2,1,0:T(4,128)(2,1)S(1)} %get-tuple-element.34), channel_id=1, source_target_pairs={{0,1},{1,0},{2,3},{3,2},{4,5},{5,4},{6,7},{7,6},{8,9},{9,8},{10,11... | collective-permute-start | bytes 589832 | tf_op jit(solution)/shard_map/ppermute | solution.py:288
  46.4 6.3 %collective-permute-start.10 = (bf16[2,4,3072]{2,1,0:T(4,128)(2,1)S(1)}, bf16[2,4,3072]{2,1,0:T(4,128)(2,1)S(1)}, u32[]{:S(2)}, u32[]{:S(2)}) collective-permute-start(bf16[2,4,3072]{2,1,0:T(4,128)(2,1)S(1)} %get-tuple-element.36), channel_id=1, source_target_pairs={{0,12},{1,13},{2,14},{3,15},{4,8},{5,9},{6,10},{7,11},{8,4},{9,5},... | collective-permute-start | bytes 147464 | tf_op jit(solution)/shard_map/ppermute | solution.py:288
  48.2 6.0 %collective-permute-start.11 = (bf16[2,4,3072]{2,1,0:T(4,128)(2,1)S(1)}, bf16[2,4,3072]{2,1,0:T(4,128)(2,1)S(1)}, u32[]{:S(2)}, u32[]{:S(2)}) collective-permute-start(bf16[2,4,3072]{2,1,0:T(4,128)(2,1)S(1)} %get-tuple-element.37), channel_id=1, source_target_pairs={{0,8},{1,9},{2,10},{3,11},{4,12},{5,13},{6,14},{7,15},{8,0},{9,1},... | collective-permute-start | bytes 147464 | tf_op jit(solution)/shard_map/ppermute | solution.py:288
  48.2 6.0 %collective-permute-start.12 = (bf16[2,4,3072]{2,1,0:T(4,128)(2,1)S(1)}, bf16[2,4,3072]{2,1,0:T(4,128)(2,1)S(1)}, u32[]{:S(2)}, u32[]{:S(2)}) collective-permute-start(bf16[2,4,3072]{2,1,0:T(4,128)(2,1)S(1)} %get-tuple-element.38), channel_id=1, source_target_pairs={{0,4},{1,5},{2,6},{3,7},{4,0},{5,1},{6,2},{7,3},{8,12},{9,13},{10,... | collective-permute-start | bytes 147464 | tf_op jit(solution)/shard_map/ppermute | solution.py:288
  54.2 3.9 %collective-permute-start.13 = (bf16[1,4,3072]{2,1,0:T(4,128)(2,1)S(1)}, bf16[1,4,3072]{2,1,0:T(4,128)(2,1)S(1)}, u32[]{:S(2)}, u32[]{:S(2)}) collective-permute-start(bf16[1,4,3072]{2,1,0:T(4,128)(2,1)S(1)} %get-tuple-element.40), channel_id=1, source_target_pairs={{0,2},{1,3},{2,0},{3,1},{4,6},{5,7},{6,4},{7,5},{8,10},{9,11},{10,... | collective-permute-start | bytes 73736 | tf_op jit(solution)/shard_map/ppermute | solution.py:288
